TPU v7x, 256 devices: a whole 4x4x8 slice. The times are simulated.
256 devices in a mesh: seq: 8 (over z_lo, x), dp: 32 (over z_hi, y, core).
Axes of the slice: x: 4, y: 4, z: 8 (z_hi: 4, z_lo: 2; z = z_hi * 2 + z_lo), core: 2. Of those that a mesh axis runs over, the one named last changes fastest.
Arguments:
- queries: bfloat16 [32, 1024, 2048], P('dp', None, 'seq'), may hold values from -8 to 8
- key_heads: bfloat16 [32, 1024, 1024], P('dp', None, 'seq'), may hold values from -8 to 8
- value_heads: bfloat16 [32, 1024, 1024], P('dp', None, 'seq'), may hold values from -6 to 6
- grad_out: bfloat16 [32, 1024, 2048], P('dp', 'seq'), may hold values from -6 to 6
- features: bfloat16 [32, 1024, 4096], P('dp', 'seq'), may hold values from -6 to 6
Outputs:
- query_grad: bfloat16 [32, 1024, 2048], P('dp', 'seq')
- key_grad: bfloat16 [32, 1024, 1024], P('dp', 'seq')
- weight_grad: float32 [4096, 1024], P('dp', 'seq')
All inputs are finite; a program needn't handle non-finite values.
Results may differ from a plain program's by a relative error of at most 0.0058.
Values may be sent and summed in bfloat16 or wider, within the bound.
No kernel may reach another device: no remote copies, remote signals or barrier semaphores. Data moves between devices by JAX's collectives and lax.ppermute only.
A program may use at most 128 MiB of HBM per device.

v0:
```python
import math

import jax
import jax.numpy as jnp
from jax import lax
from jax.sharding import PartitionSpec as P

HEADS = 16
KV = 8
HD = 128


def for_sending(shard):

    def short(part):
        return part.astype(jnp.bfloat16) if part.dtype == jnp.float32 else part

    return jax.tree.map(short, shard)


def group_grads(query_group, key_rows, value_rows, cot_group):
    group_size = query_group.shape[0]
    length = query_group.shape[1]
    head_size = query_group.shape[2]
    inv_root = 1.0 / math.sqrt(head_size)
    nblocks = max(1, length // 512)
    block_rows = length // nblocks
    key_acc = jnp.zeros((length, head_size), jnp.float32)
    value_acc = jnp.zeros((length, head_size), jnp.float32)
    query_out = []
    contract_rows = (((0,), (0,)), ((), ()))
    contract_cols = (((1,), (1,)), ((), ()))
    for head_idx in range(group_size):
        pieces = []
        for block_idx in range(nblocks):
            row_start = block_idx * block_rows
            row_stop = row_start + block_rows
            query_block = query_group[head_idx, row_start:row_stop]
            cot_block = cot_group[head_idx, row_start:row_stop]
            key_part = key_rows[:row_stop]
            value_part = value_rows[:row_stop]
            scores = (
                lax.dot_general(
                    query_block, key_part, contract_cols, preferred_element_type=jnp.float32
                )
                * inv_root
            )
            row_pos = lax.broadcasted_iota(jnp.int32, scores.shape, 0) + row_start
            col_pos = lax.broadcasted_iota(jnp.int32, scores.shape, 1)
            scores = jnp.where(col_pos <= row_pos, scores, -jnp.inf)
            row_max = jnp.max(scores, axis=1, keepdims=True)
            weights = jnp.exp(scores - row_max)
            probs = weights / jnp.sum(weights, axis=1, keepdims=True)
            probs_b = probs.astype(jnp.bfloat16)
            value_acc = value_acc.at[:row_stop].add(
                lax.dot_general(
                    probs_b, cot_block, contract_rows, preferred_element_type=jnp.float32
                )
            )
            dprobs = lax.dot_general(
                cot_block, value_part, contract_cols, preferred_element_type=jnp.float32
            )
            row_dot = jnp.sum(probs * dprobs, axis=1, keepdims=True)
            score_grad = (probs * (dprobs - row_dot)).astype(jnp.bfloat16)
            pieces.append(
                (
                    jnp.dot(score_grad, key_part, preferred_element_type=jnp.float32) * inv_root
                ).astype(jnp.bfloat16)
            )
            key_acc = key_acc.at[:row_stop].add(
                lax.dot_general(
                    score_grad, query_block, contract_rows, preferred_element_type=jnp.float32
                )
            )
        query_out.append(jnp.concatenate(pieces, axis=0))
    return (
        jnp.stack(query_out),
        (key_acc * inv_root).astype(jnp.bfloat16),
        value_acc.astype(jnp.bfloat16),
    )


def on_device(queries, key_heads, value_heads, grad_out, features):
    group_size = HEADS // KV
    local_query = queries[0]
    length = local_query.shape[0]
    kv_local = key_heads.shape[2] // HD
    cot_heads = lax.all_to_all(grad_out[0], "seq", split_axis=1, concat_axis=0, tiled=True)
    query_split = local_query.reshape(length, kv_local, group_size, HD).transpose(1, 2, 0, 3)
    cot_split = cot_heads.reshape(length, kv_local, group_size, HD).transpose(1, 2, 0, 3)
    key_split = key_heads[0].reshape(length, kv_local, HD).transpose(1, 0, 2)
    value_split = value_heads[0].reshape(length, kv_local, HD).transpose(1, 0, 2)

    def per_group(carry, items):
        return (carry, group_grads(*items))

    unused, (query_part, key_part, value_part) = lax.scan(
        per_group, jnp.zeros((), jnp.float32), (query_split, key_split, value_split, cot_split)
    )
    query_rows = query_part.transpose(2, 0, 1, 3).reshape(length, kv_local * group_size * HD)
    query_tok = lax.all_to_all(
        for_sending(query_rows), "seq", split_axis=0, concat_axis=1, tiled=True
    ).astype(query_rows.dtype)
    key_rows = key_part.transpose(1, 0, 2).reshape(length, kv_local * HD)
    value_rows = value_part.transpose(1, 0, 2).reshape(length, kv_local * HD)
    input_rows = features[0]
    contract_rows = (((0,), (0,)), ((), ()))
    key_tok, value_tok = (
        lax.all_to_all(key_rows, "seq", split_axis=0, concat_axis=1, tiled=True),
        lax.all_to_all(value_rows, "seq", split_axis=0, concat_axis=1, tiled=True),
    )
    owned_rows = lax.psum_scatter(
        lax.dot_general(input_rows, value_tok, contract_rows, preferred_element_type=jnp.float32),
        "dp",
        scatter_dimension=0,
        tiled=True,
    )
    weight_grad = lax.psum_scatter(owned_rows, "seq", scatter_dimension=1, tiled=True)
    return (query_tok[None], key_tok[None], weight_grad)


def solution(mesh):
    placed = (
        P("dp", None, "seq"),
        P("dp", None, "seq"),
        P("dp", None, "seq"),
        P("dp", "seq", None),
        P("dp", "seq", None),
    )
    return jax.shard_map(
        on_device,
        mesh=mesh,
        in_specs=placed,
        out_specs=(P("dp", "seq", None), P("dp", "seq", None), P("dp", "seq")),
        check_vma=False,
    )
```

profile of v0, /device:TPU:8, one launch (start us, length us, event | category | flops | bytes accessed | tf_op | source)
XLA Modules:
  0.0 270.7 jit_solution(18297406666145339471)
XLA Ops:
  7.2 2.2 copy.37
  9.4 5.7 %all-to-all-start = ((bf16[128,8,256]{0,2,1:T(8,128)(2,1)}), bf16[128,8,256]{0,2,1:T(8,128)(2,1)}, u32[]{:S(2)}, u32[]{:S(2)}) async-start(bf16[128,8,256]{0,2,1:T(8,128)(2,1)} %bitcast.5), calls=%async_computation | async-start | bytes 1048576 | tf_op jit(solution)/shard_map/all_to_all | solution.py:88
  16.4 1.6 fusion.52
  18.4 1.7 fusion.54
  20.1 1.3 copy-done.3
  21.9 2.8 %all-to-all-done = bf16[128,8,256]{0,2,1:T(8,128)(2,1)} async-done(((bf16[128,8,256]{0,2,1:T(8,128)(2,1)}), bf16[128,8,256]{0,2,1:T(8,128)(2,1)}, u32[]{:S(2)}, u32[]{:S(2)}) %all-to-all-start) | async-done | bytes 524320 | tf_op jit(solution)/shard_map/all_to_all | solution.py:88
  24.7 2.2 copy.38
  26.9 2.1 reshape.279
  29.0 1.7 fusion.23
  31.0 0.7 convolution_add_fusion.1
  32.6 1.5 fusion.8
  34.1 1.1 copy.49
  35.2 10.4 %all_to_all.67 = bf16[8,128,128]{1,2,0:T(8,128)(2,1)S(1)} all-to-all(bf16[8,128,128]{1,2,0:T(8,128)(2,1)S(1)} %copy.49), channel_id=1, replica_groups=mesh['seq'=8,'dp'=32] {'seq'}, dimensions={0} | all-to-all | bytes 524288 | tf_op jit(solution)/shard_map/all_to_all | solution.py:110
  45.6 8.0 %convolution_bitcast_fusion = f32[4096,1024]{0,1:T(8,128)} fusion(bf16[128,1024]{0,1:T(8,128)(2,1)S(1)} %bitcast.168, bf16[1,128,4096]{2,1,0:T(8,128)(2,1)S(1)} %copy-done), kind=kOutput, calls=%fused_computation | convolution fusion | flops 1073741824 | bytes 18087936 | tf_op jit(solution)/shard_map/dot_general | solution.py:113
  53.7 1.2 copy-done.13
  55.7 0.7 copy-done.16
  57.2 0.8 multiply_reduce_fusion.1
  58.0 0.5 multiply_convert_fusion.1
  60.2 1.2 copy-done.2
  61.3 0.8 multiply_reduce_fusion
  62.7 1.2 fusion.7
  63.9 4.0 %all-to-all-start.2 = ((bf16[8,128,128]{2,1,0:T(8,128)(2,1)}), bf16[8,128,128]{2,1,0:T(8,128)(2,1)}, u32[]{:S(2)}, u32[]{:S(2)}) async-start(bf16[8,128,128]{2,1,0:T(8,128)(2,1)} %bitcast.169), calls=%async_computation.2 | async-start | bytes 524288 | tf_op jit(solution)/shard_map/all_to_all | solution.py:109
  68.0 1.5 fusion.11
  70.9 150.0 %reduce-scatter.3.cloned.1.call-done = f32[128,1024]{0,1:T(8,128)} async-done(((f32[4096,1024]{0,1:T(8,128)}), f32[128,1024]{0,1:T(8,128)}) %reduce-scatter.3.cloned.1.call-update) | async-done | bytes 524304 | tf_op jit(solution)/shard_map/reduce_scatter | solution.py:112
  221.3 0.9 copy.47
  222.2 4.6 %all-to-all-start.1 = ((bf16[8,128,256]{1,2,0:T(8,128)(2,1)}), bf16[8,128,256]{1,2,0:T(8,128)(2,1)S(1)}, u32[]{:S(2)}, u32[]{:S(2)}) async-start(bf16[8,128,256]{1,2,0:T(8,128)(2,1)} %copy.47), calls=%async_computation.1 | async-start | bytes 1048576 | tf_op jit(solution)/shard_map/all_to_all | solution.py:101
  226.8 1.1 copy.48
  227.9 0.8 broadcast_in_dim.57
  228.7 7.2 %all-to-all-done.1 = bf16[8,128,256]{1,2,0:T(8,128)(2,1)S(1)} async-done(((bf16[8,128,256]{1,2,0:T(8,128)(2,1)}), bf16[8,128,256]{1,2,0:T(8,128)(2,1)S(1)}, u32[]{:S(2)}, u32[]{:S(2)}) %all-to-all-start.1) | async-done | bytes 524320 | tf_op jit(solution)/shard_map/all_to_all | solution.py:101
  235.9 1.0 copy.50
  236.9 25.4 %reduce-scatter.5.cloned.1.call-done = f32[128,128]{0,1:T(8,128)} async-done(((f32[128,1024]{0,1:T(8,128)}), f32[128,128]{0,1:T(8,128)}) %reduce-scatter.5.cloned.1.call-update) | async-done | bytes 65552 | tf_op jit(solution)/shard_map/reduce_scatter | solution.py:118
  262.3 1.6 copy.51
  (68 shorter events, 8.8 us)
Async XLA Ops:
  7.2 38.5 %copy-start = (bf16[1,128,4096]{2,1,0:T(8,128)(2,1)S(1)}, bf16[1,128,4096]{2,1,0:T(8,128)(2,1)}, u32[]{:S(2)}) copy-start(bf16[1,128,4096]{2,1,0:T(8,128)(2,1)} %param.33) | copy-start | bytes 3145732
  7.2 7.9 %copy-start.17 = (bf16[1,1024,256]{2,1,0:T(8,128)(2,1)S(1)}, bf16[1,1024,256]{2,1,0:T(8,128)(2,1)}, u32[]{:S(2)}) copy-start(bf16[1,1024,256]{2,1,0:T(8,128)(2,1)} %param.29) | copy-start | bytes 1572868
  7.2 8.1 %copy-start.14 = (bf16[1,1024,128]{2,1,0:T(8,128)(2,1)S(1)}, bf16[1,1024,128]{2,1,0:T(8,128)(2,1)}, u32[]{:S(2)}) copy-start(bf16[1,1024,128]{2,1,0:T(8,128)(2,1)} %param.30) | copy-start | bytes 786436
  9.4 15.3 %all-to-all-start = ((bf16[128,8,256]{0,2,1:T(8,128)(2,1)}), bf16[128,8,256]{0,2,1:T(8,128)(2,1)}, u32[]{:S(2)}, u32[]{:S(2)}) async-start(bf16[128,8,256]{0,2,1:T(8,128)(2,1)} %bitcast.5), calls=%async_computation | async-start | bytes 1048576 | tf_op jit(solution)/shard_map/all_to_all | solution.py:88
  15.0 205.8 %reduce-scatter.3.cloned.1.call-start = ((), (), s32[]{:S(2)}) async-start(), calls=%async_computation.6 | async-start | bytes 17301504 | tf_op jit(solution)/shard_map/reduce_scatter | solution.py:112
  15.3 0.8 copy-start.15
  15.6 2.3 copy-start.9
  16.0 2.0 copy-start.12
  17.9 14.7 %copy-start.1 = (f32[512,1024]{1,0:T(8,128)}, f32[512,1024]{1,0:T(8,128)S(1)}, u32[]{:S(2)}) copy-start(f32[512,1024]{1,0:T(8,128)S(1)} %get-tuple-element.208) | copy-start | bytes 6291460
  20.1 1.3 copy-start.3
  29.0 1.9 copy-start.4
  29.0 2.0 copy-start.18
  31.0 1.2 copy-start.10
  53.7 1.2 copy-start.13
  53.7 1.4 copy-start.19
  53.7 1.4 copy-start.20
  55.4 1.0 copy-start.16
  55.4 1.8 copy-start.5
  56.4 1.6 copy-start.6
  58.0 1.2 copy-start.11
  59.5 1.8 copy-start.2
  59.8 2.3 copy-start.7
  63.9 158.3 %all-to-all-start.2 = ((bf16[8,128,128]{2,1,0:T(8,128)(2,1)}), bf16[8,128,128]{2,1,0:T(8,128)(2,1)}, u32[]{:S(2)}, u32[]{:S(2)}) async-start(bf16[8,128,128]{2,1,0:T(8,128)(2,1)} %bitcast.169), calls=%async_computation.2 | async-start | bytes 524288 | tf_op jit(solution)/shard_map/all_to_all | solution.py:109
  68.0 194.3 %reduce-scatter.5.cloned.1.call-start = ((), (), s32[]{:S(2)}) async-start(), calls=%async_computation.7 | async-start | bytes 589824 | tf_op jit(solution)/shard_map/reduce_scatter | solution.py:118
  68.0 2.5 copy-start.8
  222.2 13.7 %all-to-all-start.1 = ((bf16[8,128,256]{1,2,0:T(8,128)(2,1)}), bf16[8,128,256]{1,2,0:T(8,128)(2,1)S(1)}, u32[]{:S(2)}, u32[]{:S(2)}) async-start(bf16[8,128,256]{1,2,0:T(8,128)(2,1)} %copy.47), calls=%async_computation.1 | async-start | bytes 1048576 | tf_op jit(solution)/shard_map/all_to_all | solution.py:101
Sparse Core Ops, SparseCore 0:
  53.8 167.0 reduce-scatter.2
  223.4 38.8 reduce-scatter.4
where the time goes:
time: 272 us; the launch traced here: 271 us
  waiting for transfers between devices  185 us (68%)
  matrix products  23.4 us (9%)
  local copies, waits for them, and re-layouts  19.6 us (7%)
  between operations  14.4 us (5%)
  starting transfers between devices  14.3 us (5%)
  blocking collectives  10.4 us (4%)
  other arithmetic  3.13 us (1%)
    reduce_scatter x1, waiting for transfers between devices, on_device(): lax.psum_scatter(lax.dot_general(input_rows, value_tok, contract_rows, pr...  150 us
    reduce_scatter x1, waiting for transfers between devices, on_device(): lax.psum_scatter(owned_rows, 'seq', scatter_dimension=1, tiled=True)  25.4 us
    unnamed x47, local copies, waits for them, and re-layouts  11.2 us
    all_to_all x1, blocking collectives, on_device(): lax.all_to_all(value_rows, 'seq', split_axis=0, concat_axis=1, tiled=True)  10.4 us
    dot_general x1, matrix products, on_device(): lax.dot_general(input_rows, value_tok, contract_rows, preferred_element_t...  8.04 us
    all_to_all x1, waiting for transfers between devices, on_device(): lax.all_to_all(for_sending(query_rows), 'seq', split_axis=0, concat_axis=...  7.2 us
    all_to_all x1, starting transfers between devices, on_device(): lax.all_to_all(grad_out[0], 'seq', split_axis=1, concat_axis=0, tiled=True)  5.65 us
  transfers between devices with their start and end apart: 5, of which 4 were waited for; matrix products, arithmetic and copies ran while one was open for 7% of the time, Pallas kernels for 0%

commit v1 on v0

v1 whole, which is shorter than its diff:
```python
import functools
import math

import jax
import jax.numpy as jnp
from jax import lax
from jax.experimental import pallas as pl
from jax.experimental.pallas import tpu as pltpu
from jax.sharding import Mesh
from jax.sharding import PartitionSpec as P

HD = 128
BLK = 256
NN = (((1,), (0,)), ((), ()))
NT = (((1,), (1,)), ((), ()))
F32 = jnp.float32
BF16 = jnp.bfloat16
VMEM_LIMIT = 48 * 1024 * 1024


def dot(a, b, dims):
    return lax.dot_general(a, b, dims, preferred_element_type=F32)


def probs_kernel(q_ref, k_ref, p_ref):
    length = k_ref.shape[0]
    inv_root = 1.0 / math.sqrt(HD)
    for start in range(0, length, BLK):
        stop = start + BLK
        scores = dot(k_ref[:stop], q_ref[start:stop], NT) * inv_root
        shape = (BLK, BLK)
        keep = lax.broadcasted_iota(jnp.int32, shape, 0) <= lax.broadcasted_iota(
            jnp.int32, shape, 1
        )
        last = jnp.where(keep, scores[start:], -jnp.inf)
        if start:
            scores = jnp.concatenate([scores[:start], last], axis=0)
        else:
            scores = last
        weights = jnp.exp(scores - jnp.max(scores, axis=0, keepdims=True))
        scale = 1.0 / jnp.sum(weights, axis=0, keepdims=True)
        p_ref[0, :stop, start:stop] = (weights * scale).astype(BF16)


def value_kernel(p_ref, cot_ref, out_ref):
    length = cot_ref.shape[0]
    for jstart in range(0, length, BLK):
        jstop = jstart + BLK
        total = jnp.zeros((BLK, HD), F32)
        for head in range(2):
            total += dot(
                p_ref[head, jstart:jstop, jstart:],
                cot_ref[jstart:, head * HD : (head + 1) * HD],
                NN,
            )
        out_ref[:, jstart:jstop] = total.T.astype(BF16)


def grads_kernel(p_ref, q_ref, k_ref, v_ref, cot_ref, out_ref, kt_ref, dk_ref):
    length = k_ref.shape[0]
    inv_root = 1.0 / math.sqrt(HD)
    kt_ref[...] = k_ref[...].T
    dk_ref[...] = jnp.zeros_like(dk_ref)
    for head in range(2):
        cols = slice(head * HD, (head + 1) * HD)
        for start in range(0, length, BLK):
            stop = start + BLK
            dprobs = dot(v_ref[:stop], cot_ref[start:stop, cols], NT)
            probs = p_ref[head, :stop, start:stop].astype(F32)
            row_dot = jnp.sum(probs * dprobs, axis=0, keepdims=True) / jnp.sum(
                probs, axis=0, keepdims=True
            )
            score_grad = (probs * (dprobs - row_dot)).astype(BF16)
            dk_ref[:stop] += dot(score_grad, q_ref[start:stop, cols], NN)
            dq_t = dot(kt_ref[:, :stop], score_grad, NN) * inv_root
            out_ref[start:stop, cols] = dq_t.T.astype(BF16)
    out_ref[:, 2 * HD :] = (dk_ref[...] * inv_root).astype(BF16)


def params():
    return pltpu.CompilerParams(vmem_limit_bytes=VMEM_LIMIT)


def probs_of(q, k):
    length = k.shape[0]
    return pl.pallas_call(
        probs_kernel,
        grid=(2,),
        in_specs=[
            pl.BlockSpec((length, HD), lambda h: (0, h)),
            pl.BlockSpec((length, HD), lambda h: (0, 0)),
        ],
        out_specs=pl.BlockSpec((1, length, length), lambda h: (h, 0, 0)),
        out_shape=jax.ShapeDtypeStruct((2, length, length), BF16),
        compiler_params=params(),
        cost_estimate=pl.CostEstimate(
            flops=4 * length * length * HD, bytes_accessed=5 << 20, transcendentals=length * length
        ),
    )(q, k)


def value_grad_of(probs, cot):
    length = cot.shape[0]
    return pl.pallas_call(
        value_kernel,
        out_shape=jax.ShapeDtypeStruct((HD, length), BF16),
        compiler_params=params(),
        cost_estimate=pl.CostEstimate(
            flops=4 * length * length * HD, bytes_accessed=5 << 20, transcendentals=0
        ),
    )(probs, cot)


def grads_of(probs, q, k, v, cot):
    length = cot.shape[0]
    return pl.pallas_call(
        grads_kernel,
        out_shape=jax.ShapeDtypeStruct((length, 3 * HD), BF16),
        scratch_shapes=[pltpu.VMEM((HD, length), BF16), pltpu.VMEM((length, HD), F32)],
        compiler_params=params(),
        cost_estimate=pl.CostEstimate(
            flops=16 * length * length * HD, bytes_accessed=6 << 20, transcendentals=0
        ),
    )(probs, q, k, v, cot)


def shift(array, axis, size, by):
    return lax.ppermute(array, axis, [(i, (i + by) % size) for i in range(size)])


def on_device(queries, key_heads, value_heads, grad_out, features):
    q, k, v = queries[0], key_heads[0], value_heads[0]
    length = q.shape[0]
    seq = ("z_lo", "x")
    x, z_lo, z_hi = lax.axis_index("x"), lax.axis_index("z_lo"), lax.axis_index("z_hi")
    core = lax.axis_index("core")
    tok = grad_out.shape[1]

    cot_parts = grad_out[0].reshape(tok, 8, 2 * HD).transpose(1, 0, 2)
    cot = lax.all_to_all(cot_parts, seq, 0, 0).reshape(length, 2 * HD)

    width = features.shape[2] // 4
    feat_parts = features[0].reshape(tok, 4, width).transpose(1, 0, 2)
    feat_own = lax.all_to_all(feat_parts, "x", 0, 0).reshape(4 * tok, width)
    feat_other = shift(feat_own, "z_lo", 2, 1)

    probs = probs_of(q, k)
    dv = value_grad_of(probs, cot)

    left = shift(dv, "x", 4, 1)
    right = shift(dv, "x", 4, -1)
    half = length // 2
    far_a = shift(left[:, :half], "x", 4, 1)
    far_b = shift(right[:, half:], "x", 4, -1)

    moved = grads_of(probs, q, k, v, cot)
    moved = lax.all_to_all(moved.reshape(8, tok, 3 * HD), seq, 0, 0)
    query_grad = moved[:, :, : 2 * HD].transpose(1, 0, 2).reshape(1, tok, 16 * HD)
    key_grad = moved[:, :, 2 * HD :].transpose(1, 0, 2).reshape(1, tok, 8 * HD)

    far = jnp.concatenate([far_a, far_b], axis=1)
    values = jnp.concatenate([dv, right, far, left], axis=0)
    own = lax.dynamic_slice_in_dim(values, z_lo * half, half, 1)
    other = lax.dynamic_slice_in_dim(values, (1 - z_lo) * half, half, 1)
    partial = dot(own, feat_own, NN) + dot(other, feat_other, NN)
    partial = partial.reshape(4 * HD, 4, 2, HD)
    keep = lax.dynamic_index_in_dim(partial, core, 2, keepdims=False)
    send = lax.dynamic_index_in_dim(partial, 1 - core, 2, keepdims=False).astype(BF16)
    keep = keep + shift(send.transpose(1, 0, 2), "core", 2, 1).astype(F32).transpose(1, 0, 2)
    keep = keep.transpose(1, 0, 2).astype(BF16)
    over_y = lax.all_to_all(keep, "y", 0, 0)
    summed = jnp.sum(over_y.astype(F32), axis=0).astype(BF16).reshape(4, HD, HD)
    total = jnp.zeros((HD, HD), F32)
    for step in range(4):
        block = lax.dynamic_index_in_dim(summed, (z_hi + step - x) % 4, 0, keepdims=False)
        pairs = [
            (sx * 4 + sz, ((sz + step) % 4) * 4 + sx) for sx in range(4) for sz in range(4)
        ]
        total += lax.ppermute(block, ("x", "z_hi"), pairs).astype(F32)
    return query_grad, key_grad, total.T


def solution(mesh):
    fine = Mesh(mesh.devices.reshape(2, 4, 4, 4, 2), ("z_lo", "x", "z_hi", "y", "core"))
    seq, dp = ("z_lo", "x"), ("z_hi", "y", "core")
    return jax.shard_map(
        on_device,
        mesh=fine,
        in_specs=(P(dp, None, seq), P(dp, None, seq), P(dp, None, seq), P(dp, seq, None), P(dp, seq, None)),
        out_specs=(P(dp, seq, None), P(dp, seq, None), P(dp, seq)),
        check_vma=False,
    )
```

time: 272 us -> 112 us (0.41)
  the two profiles are of different devices: /device:TPU:8 before, /device:TPU:160 now
where the time goes in v1:
time: 112 us; the launch traced here: 111 us
  waiting for transfers between devices  38.8 us (35%)
  starting transfers between devices  36.1 us (32%)
  local copies, waits for them, and re-layouts  19.4 us (17%)
  Pallas kernels  10.2 us (9%)
  matrix products  4.02 us (4%)
  other arithmetic  1.99 us (2%)
    all_to_all x1, waiting for transfers between devices, on_device(): feat_own = lax.all_to_all(feat_parts, 'x', 0, 0).reshape(4 * tok, width)  14.1 us
    ppermute x4, starting transfers between devices, on_device(): total += lax.ppermute(block, ('x', 'z_hi'), pairs).astype(F32)  10.9 us
    all_to_all x1, waiting for transfers between devices, on_device(): over_y = lax.all_to_all(keep, 'y', 0, 0)  8.7 us
    unnamed x16, local copies, waits for them, and re-layouts  7.4 us
    ppermute x4, waiting for transfers between devices, on_device(): total += lax.ppermute(block, ('x', 'z_hi'), pairs).astype(F32)  6.85 us
    pallas_call x1, Pallas kernels, grads_of(): pl.pallas_call(grads_kernel, out_shape=jax.ShapeDtypeStruct((length, 3 *...  6.85 us
    all_to_all x1, starting transfers between devices, on_device(): moved = lax.all_to_all(moved.reshape(8, tok, 3 * HD), seq, 0, 0)  6.75 us
    ppermute x6, waiting for transfers between devices, shift(): lax.ppermute(array, axis, [(i, (i + by) % size) for i in range(size)])  5.62 us
  transfers between devices with their start and end apart: 14, of which 6 were waited for; matrix products, arithmetic and copies ran while one was open for 16% of the time, Pallas kernels for 9%

profile of v1, /device:TPU:160, one launch (start us, length us, event | category | flops | bytes accessed | tf_op | source)
XLA Modules:
  0.0 111.3 jit_solution(8886745953985428689)
XLA Ops:
  0.6 2.3 %copy.19 = bf16[1,128,4096]{1,2,0:T(8,128)(2,1)} copy(bf16[1,128,4096]{2,1,0:T(8,128)(2,1)} %param.9) | data formatting | bytes 2097152 | tf_op args[4]
  3.0 4.3 %all-to-all-start.2 = ((bf16[4,128,1024]{1,2,0:T(8,128)(2,1)}), bf16[4,128,1024]{1,2,0:T(8,128)(2,1)S(1)}, u32[]{:S(2)}, u32[]{:S(2)}) async-start(bf16[4,128,1024]{1,2,0:T(8,128)(2,1)} %bitcast.9), calls=%async_computation.2 | async-start | bytes 2097152 | tf_op jit(solution)/shard_map/all_to_all | solution.py:144
  7.4 0.9 copy.34
  8.3 14.1 %all-to-all-done.2 = bf16[4,128,1024]{1,2,0:T(8,128)(2,1)S(1)} async-done(((bf16[4,128,1024]{1,2,0:T(8,128)(2,1)}), bf16[4,128,1024]{1,2,0:T(8,128)(2,1)S(1)}, u32[]{:S(2)}, u32[]{:S(2)}) %all-to-all-start.2) | async-done | bytes 1048608 | tf_op jit(solution)/shard_map/all_to_all | solution.py:144
  22.4 4.4 %all-to-all-start = ((bf16[8,128,256]{2,1,0:T(8,128)(2,1)}), bf16[8,128,256]{2,1,0:T(8,128)(2,1)S(1)}, u32[]{:S(2)}, u32[]{:S(2)}) async-start(bf16[8,128,256]{2,1,0:T(8,128)(2,1)} %bitcast.48), calls=%async_computation | async-start | bytes 1048576 | tf_op jit(solution)/shard_map/all_to_all | solution.py:140
  27.5 2.4 %shard_map.76.p_ref = bf16[2,1024,1024]{2,1,0:T(8,128)(2,1)S(1)} custom-call(bf16[1024,256]{1,0:T(8,128)(2,1)S(1)} %bitcast.51, bf16[1024,128]{1,0:T(8,128)(2,1)S(1)} %bitcast.53), custom_call_target="tpu_custom_call" | custom-call | flops 536870912 | bytes 5242880 | tf_op jit(solution)/shard_map/pallas_call | solution.py:86
  29.9 1.9 %copy-done = bf16[2,1024,1024]{2,1,0:T(8,128)(2,1)} copy-done((bf16[2,1024,1024]{2,1,0:T(8,128)(2,1)}, bf16[2,1024,1024]{2,1,0:T(8,128)(2,1)S(1)}, u32[]{:S(2)}) %copy-start) | copy-done | bytes 4194328
  31.9 3.6 %all-to-all-done = bf16[8,128,256]{2,1,0:T(8,128)(2,1)S(1)} async-done(((bf16[8,128,256]{2,1,0:T(8,128)(2,1)}), bf16[8,128,256]{2,1,0:T(8,128)(2,1)S(1)}, u32[]{:S(2)}, u32[]{:S(2)}) %all-to-all-start) | async-done | bytes 524320 | tf_op jit(solution)/shard_map/all_to_all | solution.py:140
  35.5 2.2 %copy-done.1 = bf16[2,1024,1024]{2,1,0:T(8,128)(2,1)S(1)} copy-done((bf16[2,1024,1024]{2,1,0:T(8,128)(2,1)S(1)}, bf16[2,1024,1024]{2,1,0:T(8,128)(2,1)}, u32[]{:S(2)}) %copy-start.1) | copy-done | bytes 4194328
  37.7 0.9 shard_map.78
  38.6 2.0 %collective-permute-start = (bf16[128,1024]{1,0:T(8,128)(2,1)S(1)}, bf16[128,1024]{1,0:T(8,128)(2,1)S(1)}, u32[]{:S(2)}, u32[]{:S(2)}) collective-permute-start(bf16[128,1024]{1,0:T(8,128)(2,1)S(1)} %shard_map.78), channel_id=1, source_target_pairs={{0,96},{32,0},{64,32},{96,64},{1,97},{33,1},{65,33},{97,65},{2,98}... | collective-permute-start | bytes 786440 | tf_op jit(solution)/shard_map/ppermute | solution.py:128
  40.7 4.6 %collective-permute-done = bf16[128,1024]{1,0:T(8,128)(2,1)S(1)} collective-permute-done((bf16[128,1024]{1,0:T(8,128)(2,1)S(1)}, bf16[128,1024]{1,0:T(8,128)(2,1)S(1)}, u32[]{:S(2)}, u32[]{:S(2)}) %collective-permute-start) | collective-permute-done | bytes 262176 | tf_op jit(solution)/shard_map/ppermute | solution.py:128
  46.0 2.9 %collective-permute-start.3 = (bf16[128,512]{1,0:T(8,128)(2,1)}, bf16[128,512]{1,0:T(8,128)(2,1)S(1)}, u32[]{:S(2)}, u32[]{:S(2)}) collective-permute-start(bf16[128,512]{1,0:T(8,128)(2,1)} %slice.19), channel_id=1, source_target_pairs={{0,96},{32,0},{64,32},{96,64},{1,97},{33,1},{65,33},{97,65},{2,98}... | collective-permute-start | bytes 393224 | tf_op jit(solution)/shard_map/ppermute | solution.py:128
  49.5 6.8 %shard_map.77 = bf16[1024,384]{1,0:T(8,128)(2,1)} custom-call(bf16[2,1024,1024]{2,1,0:T(8,128)(2,1)} %copy-done, bf16[1024,256]{1,0:T(8,128)(2,1)S(1)} %bitcast.52, bf16[1024,128]{1,0:T(8,128)(2,1)S(1)} %bitcast.54, bf16[1024,128]{1,0:T(8,128)(2,1)S(1)} %bitcast.55, bf16[1024,256]{1,0:T(8,128)(2,1)S(1)} %bitcast.50), custom_call_target="tpu_custom_call" | custom-call | flops 2147483648 | bytes 6291456 | tf_op jit(solution)/shard_map/pallas_call | solution.py:116
  56.4 6.7 %all-to-all-start.1 = ((bf16[8,128,384]{2,1,0:T(8,128)(2,1)}), bf16[8,128,384]{2,1,0:T(8,128)(2,1)}, u32[]{:S(2)}, u32[]{:S(2)}) async-start(bf16[8,128,384]{2,1,0:T(8,128)(2,1)} %bitcast.5), calls=%async_computation.1 | async-start | bytes 1572864 | tf_op jit(solution)/shard_map/all_to_all | solution.py:157
  63.1 1.0 pad_maximum_fusion
  64.1 2.0 %fusion.3 = f32[512,1024]{1,0:T(8,128)S(1)} fusion(bf16[512,1024]{1,0:T(8,128)(2,1)} %collective-permute-done.4, bf16[512,1024]{1,0:T(8,128)(2,1)S(1)} %pad_maximum_fusion, s32[]{:T(128)S(6)} %select_n.46), kind=kOutput, calls=%fused_computation.9 | convolution fusion | flops 536870912 | bytes 3670020 | tf_op jit(solution)/shard_map/dot_general | solution.py:22
  66.1 2.1 %convolution_add_fusion = f32[512,1024]{1,0:T(8,128)} fusion(f32[512,1024]{1,0:T(8,128)S(1)} %fusion.3, bf16[512,1024]{1,0:T(8,128)(2,1)S(1)} %bitcast.57, bf16[512,1024]{1,0:T(8,128)(2,1)S(1)} %pad_maximum_fusion, s32[]{:T(128)S(6)} %select_n.45), kind=kOutput, calls=%fused_computation | convolution fusion | flops 537395200 | bytes 5767172 | tf_op jit(solution)/shard_map/dot_general | solution.py:22
  68.2 3.0 %reshape.33 = f32[512,4,2,128]{3,2,1,0:T(2,128)S(1)} reshape(f32[512,1024]{1,0:T(8,128)} %convolution_add_fusion) | data formatting | bytes 4194304 | tf_op jit(solution)/shard_map/reshape | solution.py:166
  71.2 1.0 constant_dynamic-slice_fusion
  72.4 0.9 constant_dynamic-slice_fusion.1
  73.3 1.0 collective-permute-done.5
  74.3 0.9 fusion.1
  75.2 4.5 %all-to-all-start.3 = ((bf16[4,512,128]{2,1,0:T(8,128)(2,1)}), bf16[4,512,128]{2,1,0:T(8,128)(2,1)S(1)}, u32[]{:S(2)}, u32[]{:S(2)}) async-start(bf16[4,512,128]{2,1,0:T(8,128)(2,1)} %fusion.1), calls=%async_computation.3 | async-start | bytes 1048576 | tf_op jit(solution)/shard_map/all_to_all | solution.py:171
  79.6 1.1 slice_bitcast_fusion
  80.7 8.7 %all-to-all-done.3 = bf16[4,512,128]{2,1,0:T(8,128)(2,1)S(1)} async-done(((bf16[4,512,128]{2,1,0:T(8,128)(2,1)}), bf16[4,512,128]{2,1,0:T(8,128)(2,1)S(1)}, u32[]{:S(2)}, u32[]{:S(2)}) %all-to-all-start.3) | async-done | bytes 524320 | tf_op jit(solution)/shard_map/all_to_all | solution.py:171
  89.9 1.8 %collective-permute-start.8 = (bf16[128,128]{1,0:T(8,128)(2,1)S(1)}, bf16[128,128]{1,0:T(8,128)(2,1)S(1)}, u32[]{:S(2)}, u32[]{:S(2)}) collective-permute-start(bf16[128,128]{1,0:T(8,128)(2,1)S(1)} %get-tuple-element.8), channel_id=1, source_target_pairs={{0,64},{8,96},{16,0},{24,32},{32,72},{40,104},{48,8},{56,40},{64,8... | collective-permute-start | bytes 98312 | tf_op jit(solution)/shard_map/ppermute | solution.py:179
  91.7 6.8 %collective-permute-start.7 = (bf16[128,128]{1,0:T(8,128)(2,1)S(1)}, bf16[128,128]{1,0:T(8,128)(2,1)S(1)}, u32[]{:S(2)}, u32[]{:S(2)}) collective-permute-start(bf16[128,128]{1,0:T(8,128)(2,1)S(1)} %get-tuple-element.9), channel_id=1, source_target_pairs={{0,32},{8,64},{16,96},{24,0},{32,40},{40,72},{48,104},{56,8},{64,4... | collective-permute-start | bytes 98312 | tf_op jit(solution)/shard_map/ppermute | solution.py:179
  98.5 1.9 %collective-permute-start.6 = (bf16[128,128]{1,0:T(8,128)(2,1)S(1)}, bf16[128,128]{1,0:T(8,128)(2,1)S(1)}, u32[]{:S(2)}, u32[]{:S(2)}) collective-permute-start(bf16[128,128]{1,0:T(8,128)(2,1)S(1)} %get-tuple-element.6), channel_id=1, source_target_pairs={{0,0},{8,32},{16,64},{24,96},{32,8},{40,40},{48,72},{56,104},{64,1... | collective-permute-start | bytes 98312 | tf_op jit(solution)/shard_map/ppermute | solution.py:179
  100.4 1.0 slice_bitcast_fusion.1
  101.7 1.0 reshape.30
  103.8 6.8 %collective-permute-done.6 = bf16[128,128]{1,0:T(8,128)(2,1)S(1)} collective-permute-done((bf16[128,128]{1,0:T(8,128)(2,1)S(1)}, bf16[128,128]{1,0:T(8,128)(2,1)S(1)}, u32[]{:S(2)}, u32[]{:S(2)}) %collective-permute-start.6) | collective-permute-done | bytes 32800 | tf_op jit(solution)/shard_map/ppermute | solution.py:179
  (35 shorter events, 4.9 us)
Async XLA Ops:
  0.6 6.6 %copy-start.5 = (bf16[1,128,2048]{2,1,0:T(8,128)(2,1)S(1)}, bf16[1,128,2048]{2,1,0:T(8,128)(2,1)}, u32[]{:S(2)}) copy-start(bf16[1,128,2048]{2,1,0:T(8,128)(2,1)} %param.8) | copy-start | bytes 1572868
  3.0 19.4 %all-to-all-start.2 = ((bf16[4,128,1024]{1,2,0:T(8,128)(2,1)}), bf16[4,128,1024]{1,2,0:T(8,128)(2,1)S(1)}, u32[]{:S(2)}, u32[]{:S(2)}) async-start(bf16[4,128,1024]{1,2,0:T(8,128)(2,1)} %bitcast.9), calls=%async_computation.2 | async-start | bytes 2097152 | tf_op jit(solution)/shard_map/all_to_all | solution.py:144
  7.4 20.1 %copy-start.2 = (bf16[1,1024,256]{2,1,0:T(8,128)(2,1)S(1)}, bf16[1,1024,256]{2,1,0:T(8,128)(2,1)}, u32[]{:S(2)}) copy-start(bf16[1,1024,256]{2,1,0:T(8,128)(2,1)} %param.5) | copy-start | bytes 1572868
  7.4 20.1 %copy-start.3 = (bf16[1,1024,128]{2,1,0:T(8,128)(2,1)S(1)}, bf16[1,1024,128]{2,1,0:T(8,128)(2,1)}, u32[]{:S(2)}) copy-start(bf16[1,1024,128]{2,1,0:T(8,128)(2,1)} %param.6) | copy-start | bytes 786436
  22.4 13.1 %all-to-all-start = ((bf16[8,128,256]{2,1,0:T(8,128)(2,1)}), bf16[8,128,256]{2,1,0:T(8,128)(2,1)S(1)}, u32[]{:S(2)}, u32[]{:S(2)}) async-start(bf16[8,128,256]{2,1,0:T(8,128)(2,1)} %bitcast.48), calls=%async_computation | async-start | bytes 1048576 | tf_op jit(solution)/shard_map/all_to_all | solution.py:140
  27.3 36.8 %collective-permute-start.4 = (bf16[512,1024]{1,0:T(8,128)(2,1)S(1)}, bf16[512,1024]{1,0:T(8,128)(2,1)}, u32[]{:S(2)}, u32[]{:S(2)}) collective-permute-start(bf16[512,1024]{1,0:T(8,128)(2,1)S(1)} %bitcast.56), channel_id=1, source_target_pairs={{0,128},{128,0},{1,129},{129,1},{2,130},{130,2},{3,131},{131,3},{4... | collective-permute-start | bytes 3145736 | tf_op jit(solution)/shard_map/ppermute | solution.py:128
  29.9 1.9 %copy-start = (bf16[2,1024,1024]{2,1,0:T(8,128)(2,1)}, bf16[2,1024,1024]{2,1,0:T(8,128)(2,1)S(1)}, u32[]{:S(2)}) copy-start(bf16[2,1024,1024]{2,1,0:T(8,128)(2,1)S(1)} %shard_map.76.p_ref) | copy-start | bytes 12582916
  35.5 2.2 %copy-start.1 = (bf16[2,1024,1024]{2,1,0:T(8,128)(2,1)S(1)}, bf16[2,1024,1024]{2,1,0:T(8,128)(2,1)}, u32[]{:S(2)}) copy-start(bf16[2,1024,1024]{2,1,0:T(8,128)(2,1)} %copy-done) | copy-start | bytes 12582916
  37.7 11.9 %copy-start.4 = (bf16[1,1024,128]{2,1,0:T(8,128)(2,1)S(1)}, bf16[1,1024,128]{2,1,0:T(8,128)(2,1)}, u32[]{:S(2)}) copy-start(bf16[1,1024,128]{2,1,0:T(8,128)(2,1)} %param.7) | copy-start | bytes 786436
  38.6 6.7 %collective-permute-start = (bf16[128,1024]{1,0:T(8,128)(2,1)S(1)}, bf16[128,1024]{1,0:T(8,128)(2,1)S(1)}, u32[]{:S(2)}, u32[]{:S(2)}) collective-permute-start(bf16[128,1024]{1,0:T(8,128)(2,1)S(1)} %shard_map.78), channel_id=1, source_target_pairs={{0,96},{32,0},{64,32},{96,64},{1,97},{33,1},{65,33},{97,65},{2,98}... | collective-permute-start | bytes 786440 | tf_op jit(solution)/shard_map/ppermute | solution.py:128
  40.6 8.3 %collective-permute-start.1 = (bf16[128,1024]{1,0:T(8,128)(2,1)S(1)}, bf16[128,1024]{1,0:T(8,128)(2,1)S(1)}, u32[]{:S(2)}, u32[]{:S(2)}) collective-permute-start(bf16[128,1024]{1,0:T(8,128)(2,1)S(1)} %shard_map.78), channel_id=1, source_target_pairs={{0,32},{32,64},{64,96},{96,0},{1,33},{33,65},{65,97},{97,1},{2,34}... | collective-permute-start | bytes 786440 | tf_op jit(solution)/shard_map/ppermute | solution.py:128
  46.0 17.2 %collective-permute-start.3 = (bf16[128,512]{1,0:T(8,128)(2,1)}, bf16[128,512]{1,0:T(8,128)(2,1)S(1)}, u32[]{:S(2)}, u32[]{:S(2)}) collective-permute-start(bf16[128,512]{1,0:T(8,128)(2,1)} %slice.19), channel_id=1, source_target_pairs={{0,96},{32,0},{64,32},{96,64},{1,97},{33,1},{65,33},{97,65},{2,98}... | collective-permute-start | bytes 393224 | tf_op jit(solution)/shard_map/ppermute | solution.py:128
  49.5 13.6 %collective-permute-start.2 = (bf16[128,512]{1,0:T(8,128)(2,1)}, bf16[128,512]{1,0:T(8,128)(2,1)}, u32[]{:S(2)}, u32[]{:S(2)}) collective-permute-start(bf16[128,512]{1,0:T(8,128)(2,1)} %slice.18), channel_id=1, source_target_pairs={{0,32},{32,64},{64,96},{96,0},{1,33},{33,65},{65,97},{97,1},{2,34}... | collective-permute-start | bytes 393224 | tf_op jit(solution)/shard_map/ppermute | solution.py:128
  56.4 18.8 %all-to-all-start.1 = ((bf16[8,128,384]{2,1,0:T(8,128)(2,1)}), bf16[8,128,384]{2,1,0:T(8,128)(2,1)}, u32[]{:S(2)}, u32[]{:S(2)}) async-start(bf16[8,128,384]{2,1,0:T(8,128)(2,1)} %bitcast.5), calls=%async_computation.1 | async-start | bytes 1572864 | tf_op jit(solution)/shard_map/all_to_all | solution.py:157
  72.3 2.0 %collective-permute-start.5 = (bf16[4,512,128]{2,1,0:T(8,128)(2,1)S(1)}, bf16[4,512,128]{2,1,0:T(8,128)(2,1)S(1)}, u32[]{:S(2)}, u32[]{:S(2)}) collective-permute-start(bf16[4,512,128]{2,1,0:T(8,128)(2,1)S(1)} %bitcast.59), channel_id=1, source_target_pairs={{0,1},{1,0},{2,3},{3,2},{4,5},{5,4},{6,7},{7,6},{8,9},{9,8},{10,11... | collective-permute-start | bytes 1572872 | tf_op jit(solution)/shard_map/ppermute | solution.py:128
  75.2 14.2 %all-to-all-start.3 = ((bf16[4,512,128]{2,1,0:T(8,128)(2,1)}), bf16[4,512,128]{2,1,0:T(8,128)(2,1)S(1)}, u32[]{:S(2)}, u32[]{:S(2)}) async-start(bf16[4,512,128]{2,1,0:T(8,128)(2,1)} %fusion.1), calls=%async_computation.3 | async-start | bytes 1048576 | tf_op jit(solution)/shard_map/all_to_all | solution.py:171
  89.5 14.2 %collective-permute-start.9 = (bf16[128,128]{1,0:T(8,128)(2,1)S(1)}, bf16[128,128]{1,0:T(8,128)(2,1)S(1)}, u32[]{:S(2)}, u32[]{:S(2)}) collective-permute-start(bf16[128,128]{1,0:T(8,128)(2,1)S(1)} %get-tuple-element.7), channel_id=1, source_target_pairs={{0,96},{8,0},{16,32},{24,64},{32,104},{40,8},{48,40},{56,72},{64,1... | collective-permute-start | bytes 98312 | tf_op jit(solution)/shard_map/ppermute | solution.py:179
  89.9 13.9 %collective-permute-start.8 = (bf16[128,128]{1,0:T(8,128)(2,1)S(1)}, bf16[128,128]{1,0:T(8,128)(2,1)S(1)}, u32[]{:S(2)}, u32[]{:S(2)}) collective-permute-start(bf16[128,128]{1,0:T(8,128)(2,1)S(1)} %get-tuple-element.8), channel_id=1, source_target_pairs={{0,64},{8,96},{16,0},{24,32},{32,72},{40,104},{48,8},{56,40},{64,8... | collective-permute-start | bytes 98312 | tf_op jit(solution)/shard_map/ppermute | solution.py:179
  91.7 12.1 %collective-permute-start.7 = (bf16[128,128]{1,0:T(8,128)(2,1)S(1)}, bf16[128,128]{1,0:T(8,128)(2,1)S(1)}, u32[]{:S(2)}, u32[]{:S(2)}) collective-permute-start(bf16[128,128]{1,0:T(8,128)(2,1)S(1)} %get-tuple-element.9), channel_id=1, source_target_pairs={{0,32},{8,64},{16,96},{24,0},{32,40},{40,72},{48,104},{56,8},{64,4... | collective-permute-start | bytes 98312 | tf_op jit(solution)/shard_map/ppermute | solution.py:179
  98.5 12.1 %collective-permute-start.6 = (bf16[128,128]{1,0:T(8,128)(2,1)S(1)}, bf16[128,128]{1,0:T(8,128)(2,1)S(1)}, u32[]{:S(2)}, u32[]{:S(2)}) collective-permute-start(bf16[128,128]{1,0:T(8,128)(2,1)S(1)} %get-tuple-element.6), channel_id=1, source_target_pairs={{0,0},{8,32},{16,64},{24,96},{32,8},{40,40},{48,72},{56,104},{64,1... | collective-permute-start | bytes 98312 | tf_op jit(solution)/shard_map/ppermute | solution.py:179

commit v2 on v1

v2 whole, which is shorter than its diff:
```python
import math

import jax
import jax.numpy as jnp
from jax import lax
from jax.experimental import pallas as pl
from jax.experimental.pallas import tpu as pltpu
from jax.sharding import Mesh
from jax.sharding import PartitionSpec as P

HD = 128
BLK = 256
NN = (((1,), (0,)), ((), ()))
NT = (((1,), (1,)), ((), ()))
F32 = jnp.float32
BF16 = jnp.bfloat16
VMEM_LIMIT = 24 * 1024 * 1024
LONG = 1 << 35


def dot(a, b, dims):
    return lax.dot_general(a, b, dims, preferred_element_type=F32)


def probs_kernel(q_ref, k_ref, p_ref, buf_ref, sems):
    length = k_ref.shape[0]
    inv_root = 1.0 / math.sqrt(HD)
    shape = (BLK, BLK)
    keep = lax.broadcasted_iota(jnp.int32, shape, 0) <= lax.broadcasted_iota(jnp.int32, shape, 1)
    copies = []
    for head in range(2):
        for start in range(0, length, BLK):
            stop = start + BLK
            q_block = q_ref[start:stop, head * HD : (head + 1) * HD]
            scores = dot(k_ref[:stop], q_block, NT) * inv_root
            last = jnp.where(keep, scores[start:], -jnp.inf)
            if start:
                scores = jnp.concatenate([scores[:start], last], axis=0)
            else:
                scores = last
            weights = jnp.exp(scores - jnp.max(scores, axis=0, keepdims=True))
            scale = 1.0 / jnp.sum(weights, axis=0, keepdims=True)
            buf_ref[head, :stop, start:stop] = (weights * scale).astype(BF16)
            part = (head, pl.ds(0, stop), pl.ds(start, BLK))
            copies.append(
                pltpu.make_async_copy(buf_ref.at[part], p_ref.at[part], sems.at[len(copies)])
            )
            copies[-1].start()
    for copy in copies:
        copy.wait()


def value_kernel(p_ref, cot_ref, out_ref):
    length = cot_ref.shape[0]
    for jstart in range(0, length, BLK):
        jstop = jstart + BLK
        total = jnp.zeros((BLK, HD), F32)
        for head in range(2):
            total += dot(
                p_ref[head, jstart:jstop, jstart:],
                cot_ref[jstart:, head * HD : (head + 1) * HD],
                NN,
            )
        out_ref[:, jstart:jstop] = total.T.astype(BF16)


def grads_kernel(p_ref, q_ref, k_ref, v_ref, cot_ref, out_ref, kt_ref, dk_ref):
    length = k_ref.shape[0]
    inv_root = 1.0 / math.sqrt(HD)
    kt_ref[...] = k_ref[...].T
    dk_ref[...] = jnp.zeros_like(dk_ref)

    for head in range(2):
        cols = slice(head * HD, (head + 1) * HD)
        for start in range(0, length, BLK):
            stop = start + BLK
            dprobs = dot(v_ref[:stop], cot_ref[start:stop, cols], NT)
            probs = p_ref[head, :stop, start:stop].astype(F32)
            row_dot = jnp.sum(probs * dprobs, axis=0, keepdims=True) / jnp.sum(
                probs, axis=0, keepdims=True
            )
            score_grad = (probs * (dprobs - row_dot)).astype(BF16)
            dk_ref[:stop] += dot(score_grad, q_ref[start:stop, cols], NN)
            dq_t = dot(kt_ref[:, :stop], score_grad, NN) * inv_root
            out_ref[start:stop, cols] = dq_t.T.astype(BF16)
    out_ref[:, 2 * HD :] = (dk_ref[...] * inv_root).astype(BF16)


def params():
    return pltpu.CompilerParams(vmem_limit_bytes=VMEM_LIMIT)


def in_hbm(array):
    return pltpu.with_memory_space_constraint(array, pltpu.HBM)


def probs_of(q, k):
    length = k.shape[0]
    vmem = pl.BlockSpec(memory_space=pltpu.VMEM)
    return pl.pallas_call(
        probs_kernel,
        in_specs=[vmem, vmem],
        out_specs=pl.BlockSpec(memory_space=pl.ANY),
        out_shape=pltpu.HBM((2, length, length), BF16),
        scratch_shapes=[pltpu.VMEM((2, length, length), BF16), pltpu.SemaphoreType.DMA((8,))],
        compiler_params=params(),
        cost_estimate=pl.CostEstimate(
            flops=LONG, bytes_accessed=5 << 20, transcendentals=length * length
        ),
    )(in_hbm(q), in_hbm(k))


def grads_of(place, probs, q, k, v, cot, after):
    length = cot.shape[0]
    return call(
        grads_kernel,
        shape_of(length, 3 * HD),
        probs, q, k, v, cot,
        after=[after],
        flops=LONG,
        nbytes=6 << 20,
        scratch=[pltpu.VMEM((HD, length), BF16), pltpu.VMEM((length, HD), F32)],
    )


def pack_cot_kernel(cot_ref, out_ref):
    for dest in range(8):
        out_ref[dest] = cot_ref[:, dest * 2 * HD : (dest + 1) * 2 * HD]


def pack_features_kernel(place_ref, f_ref, *out_refs):
    width = out_refs[0].shape[1]
    for step, ref in enumerate(out_refs):
        start = pl.multiple_of(lax.rem(place_ref[0] + step, 4) * width, width)
        ref[...] = f_ref[:, pl.ds(start, width)]


def gate_kernel():
    pass


def product_kernel(place_ref, *refs):
    v_refs, f_refs, (keep_ref, send_ref, v_ref, f_ref, sems) = refs[:4], refs[4:12], refs[12:]
    x, core, z_lo = place_ref[0], place_ref[1], place_ref[2]
    tok = f_refs[0].shape[0]
    copies = []
    for step, ref in enumerate(v_refs):
        rows = pl.ds(pl.multiple_of(lax.rem(x + step, 4) * HD, HD), HD)
        copies.append(pltpu.make_async_copy(ref, v_ref.at[rows], sems.at[step]))
    for index, ref in enumerate(f_refs):
        block = lax.rem(z_lo + index // 4, 2) * 4 + lax.rem(x + 4 - index % 4, 4)
        rows = pl.ds(pl.multiple_of(block * tok, tok), tok)
        copies.append(pltpu.make_async_copy(ref, f_ref.at[rows], sems.at[4 + index]))
    for copy in copies:
        copy.start()
    for copy in copies:
        copy.wait()
    for y in range(4):
        total = dot(v_ref[...], f_ref[:, y * 2 * HD : (y + 1) * 2 * HD], NN)
        mine = jnp.where(core == 0, total[:, :HD], total[:, HD:])
        other = jnp.where(core == 0, total[:, HD:], total[:, :HD]).astype(BF16)
        for e in range(4):
            keep_ref[e, y] = mine[e * HD : (e + 1) * HD]
            send_ref[e, y] = other[e * HD : (e + 1) * HD]


def add_kernel(keep_ref, got_ref, out_ref):
    out_ref[...] = (keep_ref[...] + got_ref[...].astype(F32)).astype(BF16)


def sum_kernel(got_ref, out_ref):
    for x in range(4):
        total = got_ref[x, 0].astype(F32)
        for y in range(1, 4):
            total += got_ref[x, y].astype(F32)
        out_ref[x] = total.astype(BF16)


def last_kernel(got_ref, out_ref):
    total = got_ref[0].astype(F32)
    for z in range(1, 4):
        total += got_ref[z].astype(F32)
    out_ref[...] = total.T


def assemble_kernel(got_ref, q_ref, k_ref):
    for src in range(8):
        q_ref[:, src * 2 * HD : (src + 1) * 2 * HD] = got_ref[src, :, : 2 * HD]
        k_ref[:, src * HD : (src + 1) * HD] = got_ref[src, :, 2 * HD :]


def call(
    kernel, shapes, *args, place=None, after=(), behind=(), anywhere=False, flops=0,
    nbytes=1 << 20, scratch=(),
):
    space = pltpu.MemorySpace.HBM if anywhere else pltpu.VMEM
    specs = [pl.BlockSpec(memory_space=space)] * len(args)
    shapes = list(shapes) if isinstance(shapes, (list, tuple)) else [shapes]
    out_specs = [pl.BlockSpec(memory_space=pltpu.VMEM)] * len(shapes)
    if place is not None:
        args = (place,) + args
        specs = [pl.BlockSpec(memory_space=pltpu.SMEM)] + specs
    n_in, n_out, n_after, n_behind = len(args), len(shapes), len(after), len(behind)
    args += tuple(after) + tuple(behind)
    specs += [pl.BlockSpec(memory_space=pl.ANY)] * (n_after + n_behind)
    shapes += [jax.ShapeDtypeStruct(x.shape, x.dtype) for x in behind]
    out_specs += [pl.BlockSpec(memory_space=pl.ANY)] * n_behind
    first_out = n_in + n_after + n_behind

    def body(*refs):
        outs = refs[first_out : first_out + n_out]
        kernel(*refs[:n_in], *outs, *refs[first_out + n_out + n_behind :])

    outs = pl.pallas_call(
        body,
        out_shape=shapes,
        in_specs=specs,
        out_specs=out_specs,
        scratch_shapes=list(scratch),
        input_output_aliases={n_in + n_after + i: n_out + i for i in range(n_behind)},
        compiler_params=params(),
        cost_estimate=pl.CostEstimate(flops=flops, bytes_accessed=nbytes, transcendentals=0),
    )(*args)
    return outs if len(outs) > 1 else outs[0]


def shape_of(*dims, dtype=BF16):
    return jax.ShapeDtypeStruct(dims, dtype)


def shift(array, axis, size, by):
    return lax.ppermute(array, axis, [(i, (i + by) % size) for i in range(size)])


def on_device(queries, key_heads, value_heads, grad_out, features):
    q, k, v = queries[0], key_heads[0], value_heads[0]
    length = q.shape[0]
    seq = ("z_lo", "x")
    place = jnp.stack([lax.axis_index(a) for a in ("x", "core", "z_lo")]).astype(jnp.int32)
    tok = grad_out.shape[1]
    width = features.shape[2] // 4

    cot_parts = call(pack_cot_kernel, shape_of(8, tok, 2 * HD), grad_out[0])
    cot = lax.all_to_all(cot_parts, seq, 0, 0).reshape(length, 2 * HD)

    parts = call(
        pack_features_kernel, [shape_of(tok, width)] * 4, features[0], place=place, nbytes=2 << 20
    )
    near = [shift(parts[step], "x", 4, step) for step in range(1, 4)]
    far = shift(parts[0], "z_lo", 2, 1)

    probs = probs_of(q, k)
    dv = call(value_kernel, shape_of(HD, length), probs, cot, flops=1 << 29, nbytes=5 << 20)
    near = [call(gate_kernel, [], after=[dv], behind=[part]) for part in near]
    feats = [parts[0], *near, far] + [shift(part, "z_lo", 2, 1) for part in near]

    values = [dv] + [shift(dv, "x", 4, -step) for step in range(1, 4)]

    moved = grads_of(place, probs, q, k, v, cot, dv)
    keep, send = call(
        product_kernel,
        (shape_of(4, 4, HD, HD, dtype=F32), shape_of(4, 4, HD, HD)),
        *[in_hbm(block) for block in values + feats],
        place=place,
        after=[moved],
        anywhere=True,
        flops=LONG,
        nbytes=5 << 20,
        scratch=[
            pltpu.VMEM((4 * HD, length), BF16),
            pltpu.VMEM((length, width), BF16),
            pltpu.SemaphoreType.DMA((12,)),
        ],
    )
    got = lax.all_to_all(moved.reshape(8, tok, 3 * HD), seq, 0, 0)
    send = call(gate_kernel, [], after=[got], behind=[send])
    both = call(add_kernel, shape_of(4, 4, HD, HD), keep, shift(send, "core", 2, 1))
    over_y = lax.all_to_all(both.reshape(16, HD, HD), ("x", "y"), 0, 0).reshape(4, 4, HD, HD)
    summed = call(sum_kernel, shape_of(4, HD, HD), over_y, flops=LONG)
    over_z = lax.all_to_all(summed, "z_hi", 0, 0)
    query_grad, key_grad = call(
        assemble_kernel,
        (shape_of(tok, 16 * HD), shape_of(tok, 8 * HD)),
        got,
        after=[both],
    )
    weight_grad = call(last_kernel, shape_of(HD, HD, dtype=F32), over_z)
    return query_grad[None], key_grad[None], weight_grad


def solution(mesh):
    fine = Mesh(mesh.devices.reshape(2, 4, 4, 4, 2), ("z_lo", "x", "z_hi", "y", "core"))
    seq, dp = ("z_lo", "x"), ("z_hi", "y", "core")
    return jax.shard_map(
        on_device,
        mesh=fine,
        in_specs=(P(dp, None, seq), P(dp, None, seq), P(dp, None, seq), P(dp, seq, None), P(dp, seq, None)),
        out_specs=(P(dp, seq, None), P(dp, seq, None), P(dp, seq)),
        check_vma=False,
    )
```

time: 112 us -> 94 us (0.84)
  the two profiles are of different devices: /device:TPU:160 before, /device:TPU:8 now
where the time goes in v2:
time: 94 us; the launch traced here: 93.4 us
  starting transfers between devices  31.1 us (33%)
  waiting for transfers between devices  21.6 us (23%)
  Pallas kernels  18.3 us (19%)
  blocking collectives  16.2 us (17%)
  local copies, waits for them, and re-layouts  5.26 us (6%)
    all_to_all x1, blocking collectives, on_device(): lax.all_to_all(both.reshape(16, HD, HD), ('x', 'y'), 0, 0)  16.2 us
    pallas_call x13, Pallas kernels, call(): pl.pallas_call(body, out_shape=shapes, in_specs=specs, out_specs=out_spec...  14 us
    ppermute x11, starting transfers between devices, shift(): lax.ppermute(array, axis, [(i, (i + by) % size) for i in range(size)])  13 us
    ppermute x11, waiting for transfers between devices, shift(): lax.ppermute(array, axis, [(i, (i + by) % size) for i in range(size)])  9.6 us
    all_to_all x1, starting transfers between devices, on_device(): over_z = lax.all_to_all(summed, 'z_hi', 0, 0)  7.56 us
    all_to_all x1, waiting for transfers between devices, on_device(): over_z = lax.all_to_all(summed, 'z_hi', 0, 0)  7.5 us
    all_to_all x1, starting transfers between devices, on_device(): cot = lax.all_to_all(cot_parts, seq, 0, 0).reshape(length, 2 * HD)  5.65 us
    unnamed x32, local copies, waits for them, and re-layouts  5.26 us
  transfers between devices with their start and end apart: 14, of which 6 were waited for; matrix products, arithmetic and copies ran while one was open for 0% of the time, Pallas kernels for 17%

profile of v2, /device:TPU:8, one launch (start us, length us, event | category | flops | bytes accessed | tf_op | source)
XLA Modules:
  0.0 93.4 jit_solution(7744477697481956677)
XLA Ops:
  0.6 1.0 %copy-done.4 = bf16[1,128,2048]{2,1,0:T(8,128)(2,1)S(1)} copy-done((bf16[1,128,2048]{2,1,0:T(8,128)(2,1)S(1)}, bf16[1,128,2048]{2,1,0:T(8,128)(2,1)}, u32[]{:S(2)}) %copy-start.4) | copy-done | bytes 524312
  1.7 0.8 shard_map.77
  2.5 5.7 %all-to-all-start = ((bf16[8,128,256]{2,1,0:T(8,128)(2,1)}), bf16[8,128,256]{2,1,0:T(8,128)(2,1)S(1)}, u32[]{:S(2)}, u32[]{:S(2)}) async-start(bf16[8,128,256]{2,1,0:T(8,128)(2,1)} %shard_map.77), calls=%async_computation | async-start | bytes 1048576 | tf_op jit(solution)/shard_map/all_to_all | solution.py:244
  8.2 1.2 %copy-done.3 = bf16[1,128,4096]{2,1,0:T(8,128)(2,1)S(1)} copy-done((bf16[1,128,4096]{2,1,0:T(8,128)(2,1)S(1)}, bf16[1,128,4096]{2,1,0:T(8,128)(2,1)}, u32[]{:S(2)}) %copy-start.3) | copy-done | bytes 1048600
  9.5 1.3 %shard_map.80 = (bf16[128,1024]{1,0:T(8,128)(2,1)S(1)}, bf16[128,1024]{1,0:T(8,128)(2,1)}, bf16[128,1024]{1,0:T(8,128)(2,1)S(1)}, bf16[128,1024]{1,0:T(8,128)(2,1)S(1)}) custom-call(s32[3]{0:T(128)S(1)} %pad_add_fusion.refs_0_, bf16[128,4096]{1,0:T(8,128)(2,1)S(1)} %bitcast.17), custom_call_target="tpu_custom_call" | custom-call | bytes 2097152 | tf_op jit(solution)/shard_map/pallas_call | solution.py:214
  10.8 2.0 %collective-permute-start.3 = (bf16[128,1024]{1,0:T(8,128)(2,1)}, bf16[128,1024]{1,0:T(8,128)(2,1)S(1)}, u32[]{:S(2)}, u32[]{:S(2)}) collective-permute-start(bf16[128,1024]{1,0:T(8,128)(2,1)} %get-tuple-element.12), channel_id=1, source_target_pairs={{0,32},{32,64},{64,96},{96,0},{1,33},{33,65},{65,97},{97,1},{2,34}... | collective-permute-start | bytes 786440 | tf_op jit(solution)/shard_map/ppermute | solution.py:232
  12.8 2.7 %collective-permute-start.4 = (bf16[128,1024]{1,0:T(8,128)(2,1)S(1)}, bf16[128,1024]{1,0:T(8,128)(2,1)S(1)}, u32[]{:S(2)}, u32[]{:S(2)}) collective-permute-start(bf16[128,1024]{1,0:T(8,128)(2,1)S(1)} %get-tuple-element.13), channel_id=1, source_target_pairs={{0,64},{32,96},{64,0},{96,32},{1,65},{33,97},{65,1},{97,33},{2,66}... | collective-permute-start | bytes 786440 | tf_op jit(solution)/shard_map/ppermute | solution.py:232
  15.5 1.5 %collective-permute-start.5 = (bf16[128,1024]{1,0:T(8,128)(2,1)S(1)}, bf16[128,1024]{1,0:T(8,128)(2,1)S(1)}, u32[]{:S(2)}, u32[]{:S(2)}) collective-permute-start(bf16[128,1024]{1,0:T(8,128)(2,1)S(1)} %get-tuple-element.14), channel_id=1, source_target_pairs={{0,96},{32,0},{64,32},{96,64},{1,97},{33,1},{65,33},{97,65},{2,98}... | collective-permute-start | bytes 786440 | tf_op jit(solution)/shard_map/ppermute | solution.py:232
  16.9 1.5 %collective-permute-start.6 = (bf16[128,1024]{1,0:T(8,128)(2,1)S(1)}, bf16[128,1024]{1,0:T(8,128)(2,1)}, u32[]{:S(2)}, u32[]{:S(2)}) collective-permute-start(bf16[128,1024]{1,0:T(8,128)(2,1)S(1)} %get-tuple-element.11.refs_5_), channel_id=1, source_target_pairs={{0,128},{128,0},{1,129},{129,1},{2,130},{130,2},{3,131},{131,3},{4... | collective-permute-start | bytes 786440 | tf_op jit(solution)/shard_map/ppermute | solution.py:232
  18.4 4.4 %shard_map.76.refs_0_ = bf16[2,1024,1024]{2,1,0:T(8,128)(2,1)} custom-call(bf16[1024,256]{1,0:T(8,128)(2,1)} %bitcast.20, bf16[1024,128]{1,0:T(8,128)(2,1)} %bitcast.22), custom_call_target="tpu_custom_call" | custom-call | flops 34359738368 | bytes 5242880 | tf_op jit(solution)/shard_map/pallas_call | solution.py:100
  22.8 2.2 %copy-done.1 = bf16[2,1024,1024]{2,1,0:T(8,128)(2,1)S(1)} copy-done((bf16[2,1024,1024]{2,1,0:T(8,128)(2,1)S(1)}, bf16[2,1024,1024]{2,1,0:T(8,128)(2,1)}, u32[]{:S(2)}) %copy-start.1) | copy-done | bytes 4194328
  25.0 0.9 shard_map.78.refs_5_.refs_0_.refs_1_
  26.0 2.6 %collective-permute-start.1 = (bf16[128,1024]{1,0:T(8,128)(2,1)S(1)}, bf16[128,1024]{1,0:T(8,128)(2,1)}, u32[]{:S(2)}, u32[]{:S(2)}) collective-permute-start(bf16[128,1024]{1,0:T(8,128)(2,1)S(1)} %shard_map.78.refs_5_.refs_0_.refs_1_), channel_id=1, source_target_pairs={{0,64},{32,96},{64,0},{96,32},{1,65},{33,97},{65,1},{97,33},{2,66}... | collective-permute-start | bytes 786440 | tf_op jit(solution)/shard_map/ppermute | solution.py:232
  28.6 0.7 collective-permute-done.4.refs_1_
  29.3 1.9 %collective-permute-start.7 = (bf16[128,1024]{1,0:T(8,128)(2,1)S(1)}, bf16[128,1024]{1,0:T(8,128)(2,1)S(1)}, u32[]{:S(2)}, u32[]{:S(2)}) collective-permute-start(bf16[128,1024]{1,0:T(8,128)(2,1)S(1)} %shard_map.81.refs_6_), channel_id=1, source_target_pairs={{0,128},{128,0},{1,129},{129,1},{2,130},{130,2},{3,131},{131,3},{4... | collective-permute-start | bytes 786440 | tf_op jit(solution)/shard_map/ppermute | solution.py:232
  31.3 0.2 collective-permute-start.8
  31.5 3.8 %collective-permute-done.refs_2_ = bf16[128,1024]{1,0:T(8,128)(2,1)S(1)} collective-permute-done((bf16[128,1024]{1,0:T(8,128)(2,1)S(1)}, bf16[128,1024]{1,0:T(8,128)(2,1)S(1)}, u32[]{:S(2)}, u32[]{:S(2)}) %collective-permute-start) | collective-permute-done | bytes 262176 | tf_op jit(solution)/shard_map/ppermute | solution.py:232
  35.2 0.6 collective-permute-start.9
  35.8 4.7 %shard_map.79.refs_13_ = bf16[1024,384]{1,0:T(8,128)(2,1)} custom-call(bf16[2,1024,1024]{2,1,0:T(8,128)(2,1)S(1)} %copy-done.2, bf16[1024,256]{1,0:T(8,128)(2,1)S(1)} %bitcast.21, bf16[1024,128]{1,0:T(8,128)(2,1)S(1)} %bitcast.23, bf16[1024,128]{1,0:T(8,128)(2,1)S(1)} %bitcast.24, bf16[1024,256]{1,0:T(8,128)(2,1)S(1)} %bitcast.16, ...), custom_call_target="tpu_custom_call" | custom-call | flops 34359738368 | bytes 6291456 | tf_op jit(solution)/shard_map/pallas_call | solution.py:214
  40.5 4.9 %all-to-all-start.1 = ((bf16[8,128,384]{2,1,0:T(8,128)(2,1)}), bf16[8,128,384]{2,1,0:T(8,128)(2,1)S(1)}, u32[]{:S(2)}, u32[]{:S(2)}) async-start(bf16[8,128,384]{2,1,0:T(8,128)(2,1)} %bitcast.5), calls=%async_computation.1 | async-start | bytes 1572864 | tf_op jit(solution)/shard_map/all_to_all | solution.py:275
  45.4 0.7 copy-done.13
  46.1 0.1 copy-done.14
  46.2 3.2 %collective-permute-done.9.refs_12_ = bf16[128,1024]{1,0:T(8,128)(2,1)} collective-permute-done((bf16[128,1024]{1,0:T(8,128)(2,1)S(1)}, bf16[128,1024]{1,0:T(8,128)(2,1)}, u32[]{:S(2)}, u32[]{:S(2)}) %collective-permute-start.9) | collective-permute-done | bytes 262176 | tf_op jit(solution)/shard_map/ppermute | solution.py:232
  49.4 3.7 %shard_map.84 = (f32[4,4,128,128]{3,2,1,0:T(8,128)S(1)}, bf16[4,4,128,128]{3,2,1,0:T(8,128)(2,1)S(1)}) custom-call(s32[3]{0:T(128)S(1)} %pad_add_fusion.refs_0_, bf16[128,1024]{1,0:T(8,128)(2,1)} %copy-done, bf16[128,1024]{1,0:T(8,128)(2,1)} %copy-done.12, bf16[128,1024]{1,0:T(8,128)(2,1)} %collective-permute-done.1.refs_3_, bf16[128,1024]{1,0:T(8,128)(2,1)} %copy-done.13, ...), custom_call_target="tpu_custom_call" | custom-call | flops 34359738368 | bytes 5242880 | tf_op jit(solution)/shard_map/pallas_call | solution.py:214
  53.1 4.5 %all-to-all-done.1.refs_0_ = bf16[8,128,384]{2,1,0:T(8,128)(2,1)S(1)} async-done(((bf16[8,128,384]{2,1,0:T(8,128)(2,1)}), bf16[8,128,384]{2,1,0:T(8,128)(2,1)S(1)}, u32[]{:S(2)}, u32[]{:S(2)}) %all-to-all-start.1) | async-done | bytes 786464 | tf_op jit(solution)/shard_map/all_to_all | solution.py:275
  57.7 1.9 %collective-permute-done.10.refs_1_ = bf16[4,4,128,128]{3,2,1,0:T(8,128)(2,1)S(1)} collective-permute-done((bf16[4,4,128,128]{3,2,1,0:T(8,128)(2,1)S(1)}, bf16[4,4,128,128]{3,2,1,0:T(8,128)(2,1)S(1)}, u32[]{:S(2)}, u32[]{:S(2)}) %collective-permute-start.10) | collective-permute-done | bytes 524320 | tf_op jit(solution)/shard_map/ppermute | solution.py:232
  59.7 16.2 %all_to_all.20 = bf16[16,128,128]{2,1,0:T(8,128)(2,1)S(1)} all-to-all(bf16[16,128,128]{2,1,0:T(8,128)(2,1)S(1)} %bitcast.14), channel_id=1, replica_groups=mesh['z_lo'=2,'x'=4,'z_hi'=4,'y'=4,'core'=2] {'x','y'}, dimensions={0} | all-to-all | bytes 1048576 | tf_op jit(solution)/shard_map/all_to_all | solution.py:278
  75.9 0.7 shard_map.88
  76.6 7.6 %all-to-all-start.3 = ((bf16[4,128,128]{2,1,0:T(8,128)(2,1)}), bf16[4,128,128]{2,1,0:T(8,128)(2,1)S(1)}, u32[]{:S(2)}, u32[]{:S(2)}) async-start(bf16[4,128,128]{2,1,0:T(8,128)(2,1)} %shard_map.88), calls=%async_computation.3 | async-start | bytes 262144 | tf_op jit(solution)/shard_map/all_to_all | solution.py:280
  84.1 1.0 %shard_map.87 = (bf16[128,2048]{1,0:T(8,128)(2,1)}, bf16[128,1024]{1,0:T(8,128)(2,1)}) custom-call(bf16[8,128,384]{2,1,0:T(8,128)(2,1)S(1)} %all-to-all-done.1.refs_0_, bf16[4,4,128,128]{3,2,1,0:T(8,128)(2,1)S(1)} %shard_map.86.refs_1_), custom_call_target="tpu_custom_call" | custom-call | bytes 1048576 | tf_op jit(solution)/shard_map/pallas_call | solution.py:214
  85.2 7.5 %all-to-all-done.3.refs_0_ = bf16[4,128,128]{2,1,0:T(8,128)(2,1)S(1)} async-done(((bf16[4,128,128]{2,1,0:T(8,128)(2,1)}), bf16[4,128,128]{2,1,0:T(8,128)(2,1)S(1)}, u32[]{:S(2)}, u32[]{:S(2)}) %all-to-all-start.3) | async-done | bytes 131104 | tf_op jit(solution)/shard_map/all_to_all | solution.py:280
  92.7 0.7 shard_map.89
  (44 shorter events, 0.3 us)
Async XLA Ops:
  0.6 1.0 %copy-start.4 = (bf16[1,128,2048]{2,1,0:T(8,128)(2,1)S(1)}, bf16[1,128,2048]{2,1,0:T(8,128)(2,1)}, u32[]{:S(2)}) copy-start(bf16[1,128,2048]{2,1,0:T(8,128)(2,1)} %param.8) | copy-start | bytes 1572868
  2.5 20.3 %all-to-all-start = ((bf16[8,128,256]{2,1,0:T(8,128)(2,1)}), bf16[8,128,256]{2,1,0:T(8,128)(2,1)S(1)}, u32[]{:S(2)}, u32[]{:S(2)}) async-start(bf16[8,128,256]{2,1,0:T(8,128)(2,1)} %shard_map.77), calls=%async_computation | async-start | bytes 1048576 | tf_op jit(solution)/shard_map/all_to_all | solution.py:244
  8.2 1.2 %copy-start.3 = (bf16[1,128,4096]{2,1,0:T(8,128)(2,1)S(1)}, bf16[1,128,4096]{2,1,0:T(8,128)(2,1)}, u32[]{:S(2)}) copy-start(bf16[1,128,4096]{2,1,0:T(8,128)(2,1)} %param.9) | copy-start | bytes 3145732
  10.8 12.0 %copy-start.11 = (bf16[128,1024]{1,0:T(8,128)(2,1)}, bf16[128,1024]{1,0:T(8,128)(2,1)S(1)}, u32[]{:S(2)}) copy-start(bf16[128,1024]{1,0:T(8,128)(2,1)S(1)} %get-tuple-element.11.refs_5_) | copy-start | bytes 786436
  10.8 15.2 %collective-permute-start.3 = (bf16[128,1024]{1,0:T(8,128)(2,1)}, bf16[128,1024]{1,0:T(8,128)(2,1)S(1)}, u32[]{:S(2)}, u32[]{:S(2)}) collective-permute-start(bf16[128,1024]{1,0:T(8,128)(2,1)} %get-tuple-element.12), channel_id=1, source_target_pairs={{0,32},{32,64},{64,96},{96,0},{1,33},{33,65},{65,97},{97,1},{2,34}... | collective-permute-start | bytes 786440 | tf_op jit(solution)/shard_map/ppermute | solution.py:232
  12.8 16.5 %collective-permute-start.4 = (bf16[128,1024]{1,0:T(8,128)(2,1)S(1)}, bf16[128,1024]{1,0:T(8,128)(2,1)S(1)}, u32[]{:S(2)}, u32[]{:S(2)}) collective-permute-start(bf16[128,1024]{1,0:T(8,128)(2,1)S(1)} %get-tuple-element.13), channel_id=1, source_target_pairs={{0,64},{32,96},{64,0},{96,32},{1,65},{33,97},{65,1},{97,33},{2,66}... | collective-permute-start | bytes 786440 | tf_op jit(solution)/shard_map/ppermute | solution.py:232
  15.5 13.9 %collective-permute-start.5 = (bf16[128,1024]{1,0:T(8,128)(2,1)S(1)}, bf16[128,1024]{1,0:T(8,128)(2,1)S(1)}, u32[]{:S(2)}, u32[]{:S(2)}) collective-permute-start(bf16[128,1024]{1,0:T(8,128)(2,1)S(1)} %get-tuple-element.14), channel_id=1, source_target_pairs={{0,96},{32,0},{64,32},{96,64},{1,97},{33,1},{65,33},{97,65},{2,98}... | collective-permute-start | bytes 786440 | tf_op jit(solution)/shard_map/ppermute | solution.py:232
  16.9 14.4 %collective-permute-start.6 = (bf16[128,1024]{1,0:T(8,128)(2,1)S(1)}, bf16[128,1024]{1,0:T(8,128)(2,1)}, u32[]{:S(2)}, u32[]{:S(2)}) collective-permute-start(bf16[128,1024]{1,0:T(8,128)(2,1)S(1)} %get-tuple-element.11.refs_5_), channel_id=1, source_target_pairs={{0,128},{128,0},{1,129},{129,1},{2,130},{130,2},{3,131},{131,3},{4... | collective-permute-start | bytes 786440 | tf_op jit(solution)/shard_map/ppermute | solution.py:232
  18.4 17.4 %copy-start.8 = (bf16[1,1024,256]{2,1,0:T(8,128)(2,1)S(1)}, bf16[1,1024,256]{2,1,0:T(8,128)(2,1)}, u32[]{:S(2)}) copy-start(bf16[1,1024,256]{2,1,0:T(8,128)(2,1)} %param.5) | copy-start | bytes 1572868
  18.4 17.4 %copy-start.9 = (bf16[1,1024,128]{2,1,0:T(8,128)(2,1)S(1)}, bf16[1,1024,128]{2,1,0:T(8,128)(2,1)}, u32[]{:S(2)}) copy-start(bf16[1,1024,128]{2,1,0:T(8,128)(2,1)} %param.6) | copy-start | bytes 786436
  18.4 17.4 %copy-start.10 = (bf16[1,1024,128]{2,1,0:T(8,128)(2,1)S(1)}, bf16[1,1024,128]{2,1,0:T(8,128)(2,1)}, u32[]{:S(2)}) copy-start(bf16[1,1024,128]{2,1,0:T(8,128)(2,1)} %param.7) | copy-start | bytes 786436
  22.8 2.2 %copy-start.1 = (bf16[2,1024,1024]{2,1,0:T(8,128)(2,1)S(1)}, bf16[2,1024,1024]{2,1,0:T(8,128)(2,1)}, u32[]{:S(2)}) copy-start(bf16[2,1024,1024]{2,1,0:T(8,128)(2,1)} %shard_map.76.refs_0_) | copy-start | bytes 12582916
  25.0 10.8 %copy-start.2 = (bf16[2,1024,1024]{2,1,0:T(8,128)(2,1)S(1)}, bf16[2,1024,1024]{2,1,0:T(8,128)(2,1)}, u32[]{:S(2)}) copy-start(bf16[2,1024,1024]{2,1,0:T(8,128)(2,1)} %shard_map.76.refs_0_) | copy-start | bytes 12582916
  25.9 14.6 %copy-start = (bf16[128,1024]{1,0:T(8,128)(2,1)}, bf16[128,1024]{1,0:T(8,128)(2,1)S(1)}, u32[]{:S(2)}) copy-start(bf16[128,1024]{1,0:T(8,128)(2,1)S(1)} %shard_map.78.refs_5_.refs_0_.refs_1_) | copy-start | bytes 786436
  25.9 9.3 %collective-permute-start = (bf16[128,1024]{1,0:T(8,128)(2,1)S(1)}, bf16[128,1024]{1,0:T(8,128)(2,1)S(1)}, u32[]{:S(2)}, u32[]{:S(2)}) collective-permute-start(bf16[128,1024]{1,0:T(8,128)(2,1)S(1)} %shard_map.78.refs_5_.refs_0_.refs_1_), channel_id=1, source_target_pairs={{0,96},{32,0},{64,32},{96,64},{1,97},{33,1},{65,33},{97,65},{2,98}... | collective-permute-start | bytes 786440 | tf_op jit(solution)/shard_map/ppermute | solution.py:232
  26.0 19.3 %collective-permute-start.1 = (bf16[128,1024]{1,0:T(8,128)(2,1)S(1)}, bf16[128,1024]{1,0:T(8,128)(2,1)}, u32[]{:S(2)}, u32[]{:S(2)}) collective-permute-start(bf16[128,1024]{1,0:T(8,128)(2,1)S(1)} %shard_map.78.refs_5_.refs_0_.refs_1_), channel_id=1, source_target_pairs={{0,64},{32,96},{64,0},{96,32},{1,65},{33,97},{65,1},{97,33},{2,66}... | collective-permute-start | bytes 786440 | tf_op jit(solution)/shard_map/ppermute | solution.py:232
  28.6 11.9 %copy-start.7 = (bf16[128,1024]{1,0:T(8,128)(2,1)}, bf16[128,1024]{1,0:T(8,128)(2,1)S(1)}, u32[]{:S(2)}) copy-start(bf16[128,1024]{1,0:T(8,128)(2,1)S(1)} %shard_map.81.refs_6_) | copy-start | bytes 786436
  29.3 16.0 %collective-permute-start.2 = (bf16[128,1024]{1,0:T(8,128)(2,1)S(1)}, bf16[128,1024]{1,0:T(8,128)(2,1)S(1)}, u32[]{:S(2)}, u32[]{:S(2)}) collective-permute-start(bf16[128,1024]{1,0:T(8,128)(2,1)S(1)} %shard_map.78.refs_5_.refs_0_.refs_1_), channel_id=1, source_target_pairs={{0,32},{32,64},{64,96},{96,0},{1,33},{33,65},{65,97},{97,1},{2,34}... | collective-permute-start | bytes 786440 | tf_op jit(solution)/shard_map/ppermute | solution.py:232
  29.3 11.2 %copy-start.6 = (bf16[128,1024]{1,0:T(8,128)(2,1)}, bf16[128,1024]{1,0:T(8,128)(2,1)S(1)}, u32[]{:S(2)}) copy-start(bf16[128,1024]{1,0:T(8,128)(2,1)S(1)} %shard_map.82.refs_7_) | copy-start | bytes 786436
  29.3 16.1 %collective-permute-start.7 = (bf16[128,1024]{1,0:T(8,128)(2,1)S(1)}, bf16[128,1024]{1,0:T(8,128)(2,1)S(1)}, u32[]{:S(2)}, u32[]{:S(2)}) collective-permute-start(bf16[128,1024]{1,0:T(8,128)(2,1)S(1)} %shard_map.81.refs_6_), channel_id=1, source_target_pairs={{0,128},{128,0},{1,129},{129,1},{2,130},{130,2},{3,131},{131,3},{4... | collective-permute-start | bytes 786440 | tf_op jit(solution)/shard_map/ppermute | solution.py:232
  31.3 9.2 %copy-start.5 = (bf16[128,1024]{1,0:T(8,128)(2,1)}, bf16[128,1024]{1,0:T(8,128)(2,1)S(1)}, u32[]{:S(2)}) copy-start(bf16[128,1024]{1,0:T(8,128)(2,1)S(1)} %shard_map.83.refs_8_) | copy-start | bytes 786436
  31.3 14.1 %collective-permute-start.8 = (bf16[128,1024]{1,0:T(8,128)(2,1)S(1)}, bf16[128,1024]{1,0:T(8,128)(2,1)S(1)}, u32[]{:S(2)}, u32[]{:S(2)}) collective-permute-start(bf16[128,1024]{1,0:T(8,128)(2,1)S(1)} %shard_map.82.refs_7_), channel_id=1, source_target_pairs={{0,128},{128,0},{1,129},{129,1},{2,130},{130,2},{3,131},{131,3},{4... | collective-permute-start | bytes 786440 | tf_op jit(solution)/shard_map/ppermute | solution.py:232
  35.2 5.3 %copy-start.12 = (bf16[128,1024]{1,0:T(8,128)(2,1)}, bf16[128,1024]{1,0:T(8,128)(2,1)S(1)}, u32[]{:S(2)}) copy-start(bf16[128,1024]{1,0:T(8,128)(2,1)S(1)} %collective-permute-done.refs_2_) | copy-start | bytes 786436
  35.2 14.2 %collective-permute-start.9 = (bf16[128,1024]{1,0:T(8,128)(2,1)S(1)}, bf16[128,1024]{1,0:T(8,128)(2,1)}, u32[]{:S(2)}, u32[]{:S(2)}) collective-permute-start(bf16[128,1024]{1,0:T(8,128)(2,1)S(1)} %shard_map.83.refs_8_), channel_id=1, source_target_pairs={{0,128},{128,0},{1,129},{129,1},{2,130},{130,2},{3,131},{131,3},{4... | collective-permute-start | bytes 786440 | tf_op jit(solution)/shard_map/ppermute | solution.py:232
  40.5 17.2 %all-to-all-start.1 = ((bf16[8,128,384]{2,1,0:T(8,128)(2,1)}), bf16[8,128,384]{2,1,0:T(8,128)(2,1)S(1)}, u32[]{:S(2)}, u32[]{:S(2)}) async-start(bf16[8,128,384]{2,1,0:T(8,128)(2,1)} %bitcast.5), calls=%async_computation.1 | async-start | bytes 1572864 | tf_op jit(solution)/shard_map/all_to_all | solution.py:275
  45.4 0.7 copy-start.13
  45.4 0.8 copy-start.14
  46.2 3.2 %copy-start.15 = (bf16[128,1024]{1,0:T(8,128)(2,1)}, bf16[128,1024]{1,0:T(8,128)(2,1)S(1)}, u32[]{:S(2)}) copy-start(bf16[128,1024]{1,0:T(8,128)(2,1)S(1)} %collective-permute-done.8.refs_11_) | copy-start | bytes 786436
  57.7 1.9 %collective-permute-start.10 = (bf16[4,4,128,128]{3,2,1,0:T(8,128)(2,1)S(1)}, bf16[4,4,128,128]{3,2,1,0:T(8,128)(2,1)S(1)}, u32[]{:S(2)}, u32[]{:S(2)}) collective-permute-start(bf16[4,4,128,128]{3,2,1,0:T(8,128)(2,1)S(1)} %shard_map.85), channel_id=1, source_target_pairs={{0,1},{1,0},{2,3},{3,2},{4,5},{5,4},{6,7},{7,6},{8,9},{9,8},{10,11... | collective-permute-start | bytes 1572872 | tf_op jit(solution)/shard_map/ppermute | solution.py:232
  76.6 16.1 %all-to-all-start.3 = ((bf16[4,128,128]{2,1,0:T(8,128)(2,1)}), bf16[4,128,128]{2,1,0:T(8,128)(2,1)S(1)}, u32[]{:S(2)}, u32[]{:S(2)}) async-start(bf16[4,128,128]{2,1,0:T(8,128)(2,1)} %shard_map.88), calls=%async_computation.3 | async-start | bytes 262144 | tf_op jit(solution)/shard_map/all_to_all | solution.py:280

commit v3 on v2

--- a/solution.py
+++ b/solution.py
@@ -64,11 +64,18 @@
         out_ref[:, jstart:jstop] = total.T.astype(BF16)
 
 
-def grads_kernel(p_ref, q_ref, k_ref, v_ref, cot_ref, out_ref, kt_ref, dk_ref):
+def grads_kernel(place_ref, p_ref, q_ref, k_ref, v_ref, cot_ref, out_ref, kt_ref, dk_ref):
     length = k_ref.shape[0]
+    tok = out_ref.shape[2]
     inv_root = 1.0 / math.sqrt(HD)
     kt_ref[...] = k_ref[...].T
     dk_ref[...] = jnp.zeros_like(dk_ref)
+
+    def put(rows, first, cols):
+        for part in range(rows.shape[0] // tok):
+            block = first // tok + part
+            step = lax.rem(block % 4 + 4 - place_ref[0], 4)
+            out_ref[step, block // 4, :, cols] = rows[part * tok : (part + 1) * tok]
 
     for head in range(2):
         cols = slice(head * HD, (head + 1) * HD)
@@ -82,8 +89,8 @@
             score_grad = (probs * (dprobs - row_dot)).astype(BF16)
             dk_ref[:stop] += dot(score_grad, q_ref[start:stop, cols], NN)
             dq_t = dot(kt_ref[:, :stop], score_grad, NN) * inv_root
-            out_ref[start:stop, cols] = dq_t.T.astype(BF16)
-    out_ref[:, 2 * HD :] = (dk_ref[...] * inv_root).astype(BF16)
+            put(dq_t.T.astype(BF16), start, cols)
+    put((dk_ref[...] * inv_root).astype(BF16), 0, slice(2 * HD, 3 * HD))
 
 
 def params():
@@ -114,8 +121,9 @@
     length = cot.shape[0]
     return call(
         grads_kernel,
-        shape_of(length, 3 * HD),
+        shape_of(4, 2, length // 8, 3 * HD),
         probs, q, k, v, cot,
+        place=place,
         after=[after],
         flops=LONG,
         nbytes=6 << 20,
@@ -135,28 +143,41 @@
         ref[...] = f_ref[:, pl.ds(start, width)]
 
 
+def join_kernel(*refs):
+    for index, ref in enumerate(refs[:-1]):
+        refs[-1][index] = ref[...]
+
+
 def gate_kernel():
     pass
 
 
-def product_kernel(place_ref, *refs):
-    v_refs, f_refs, (keep_ref, send_ref, v_ref, f_ref, sems) = refs[:4], refs[4:12], refs[12:]
-    x, core, z_lo = place_ref[0], place_ref[1], place_ref[2]
-    tok = f_refs[0].shape[0]
-    copies = []
+def near_kernel(place_ref, *refs):
+    v_refs, f_refs, (part_ref, other_ref, v_ref, f_ref) = refs[:4], refs[4:8], refs[8:]
+    x, z_lo = place_ref[0], place_ref[2]
+    tok, half = f_refs[0].shape[0], other_ref.shape[1]
     for step, ref in enumerate(v_refs):
         rows = pl.ds(pl.multiple_of(lax.rem(x + step, 4) * HD, HD), HD)
-        copies.append(pltpu.make_async_copy(ref, v_ref.at[rows], sems.at[step]))
-    for index, ref in enumerate(f_refs):
-        block = lax.rem(z_lo + index // 4, 2) * 4 + lax.rem(x + 4 - index % 4, 4)
-        rows = pl.ds(pl.multiple_of(block * tok, tok), tok)
-        copies.append(pltpu.make_async_copy(ref, f_ref.at[rows], sems.at[4 + index]))
-    for copy in copies:
-        copy.start()
-    for copy in copies:
-        copy.wait()
+        v_ref[rows, :] = ref[:, pl.ds(pl.multiple_of(z_lo * half, half), half)]
+        other_ref[rows, :] = ref[:, pl.ds(pl.multiple_of((1 - z_lo) * half, half), half)]
+    for step, ref in enumerate(f_refs):
+        block = lax.rem(x + 4 - step, 4)
+        f_ref[pl.ds(pl.multiple_of(block * tok, tok), tok), :] = ref[...]
     for y in range(4):
-        total = dot(v_ref[...], f_ref[:, y * 2 * HD : (y + 1) * 2 * HD], NN)
+        cols = slice(y * 2 * HD, (y + 1) * 2 * HD)
+        part_ref[:, cols] = dot(v_ref[...], f_ref[:, cols], NN)
+
+
+def far_kernel(place_ref, part_ref, v_ref, *refs):
+    own_ref, next_ref, rest_ref, keep_ref, send_ref, f_ref = refs
+    x, core = place_ref[0], place_ref[1]
+    tok = own_ref.shape[0]
+    for step, ref in enumerate((own_ref, next_ref, rest_ref.at[0], rest_ref.at[1])):
+        block = lax.rem(x + 4 - step, 4)
+        f_ref[pl.ds(pl.multiple_of(block * tok, tok), tok), :] = ref[...]
+    for y in range(4):
+        cols = slice(y * 2 * HD, (y + 1) * 2 * HD)
+        total = part_ref[:, cols] + dot(v_ref[...], f_ref[:, cols], NN)
         mine = jnp.where(core == 0, total[:, :HD], total[:, HD:])
         other = jnp.where(core == 0, total[:, HD:], total[:, :HD]).astype(BF16)
         for e in range(4):
@@ -183,10 +204,26 @@
     out_ref[...] = total.T
 
 
-def assemble_kernel(got_ref, q_ref, k_ref):
-    for src in range(8):
-        q_ref[:, src * 2 * HD : (src + 1) * 2 * HD] = got_ref[src, :, : 2 * HD]
-        k_ref[:, src * HD : (src + 1) * HD] = got_ref[src, :, 2 * HD :]
+def pack_rows_kernel(place_ref, own_ref, a_ref, b_ref, c_ref, out_ref):
+    other = 1 - place_ref[2]
+    out_ref[0] = own_ref[0, other]
+    for step, ref in enumerate((a_ref, b_ref, c_ref)):
+        out_ref[step + 1] = ref[other]
+
+
+def assemble_kernel(place_ref, own_ref, a_ref, b_ref, c_ref, far_ref, q_ref, k_ref):
+    x, z_lo = place_ref[0], place_ref[2]
+
+    def put(rows, z, step):
+        src = z * 4 + lax.rem(x + 4 - step, 4)
+        q_ref[:, pl.ds(pl.multiple_of(src * 2 * HD, 2 * HD), 2 * HD)] = rows[:, : 2 * HD]
+        k_ref[:, pl.ds(pl.multiple_of(src * HD, HD), HD)] = rows[:, 2 * HD :]
+
+    put(own_ref[0, z_lo], z_lo, 0)
+    for step, ref in enumerate((a_ref, b_ref, c_ref)):
+        put(ref[z_lo], z_lo, step + 1)
+    for step in range(4):
+        put(far_ref[step], 1 - z_lo, step)
 
 
 def call(
@@ -250,39 +287,53 @@
     far = shift(parts[0], "z_lo", 2, 1)
 
     probs = probs_of(q, k)
-    dv = call(value_kernel, shape_of(HD, length), probs, cot, flops=1 << 29, nbytes=5 << 20)
-    near = [call(gate_kernel, [], after=[dv], behind=[part]) for part in near]
-    feats = [parts[0], *near, far] + [shift(part, "z_lo", 2, 1) for part in near]
+    dv = call(
+        value_kernel, shape_of(HD, length), probs, cot, after=[far], flops=1 << 29, nbytes=5 << 20
+    )
+    first = call(gate_kernel, [], after=[dv], behind=near[:1])
+    rest = call(join_kernel, shape_of(2, tok, width), *near[1:], after=[dv], nbytes=2 << 20)
+    near = [parts[0], first, *near[1:]]
+    far = [far, shift(first, "z_lo", 2, 1), shift(rest, "z_lo", 2, 1)]
 
     values = [dv] + [shift(dv, "x", 4, -step) for step in range(1, 4)]
 
     moved = grads_of(place, probs, q, k, v, cot, dv)
-    keep, send = call(
-        product_kernel,
-        (shape_of(4, 4, HD, HD, dtype=F32), shape_of(4, 4, HD, HD)),
-        *[in_hbm(block) for block in values + feats],
+    half = length // 2
+    part, other = call(
+        near_kernel,
+        [shape_of(4 * HD, width, dtype=F32), shape_of(4 * HD, half)],
+        *values, *near,
         place=place,
         after=[moved],
-        anywhere=True,
+        flops=0,
+        nbytes=0,
+        scratch=[pltpu.VMEM((4 * HD, half), BF16), pltpu.VMEM((half, width), BF16)],
+    )
+    keep, send = call(
+        far_kernel,
+        [shape_of(4, 4, HD, HD, dtype=F32), shape_of(4, 4, HD, HD)],
+        part, other, *far,
+        place=place,
         flops=LONG,
         nbytes=5 << 20,
-        scratch=[
-            pltpu.VMEM((4 * HD, length), BF16),
-            pltpu.VMEM((length, width), BF16),
-            pltpu.SemaphoreType.DMA((12,)),
-        ],
-    )
-    got = lax.all_to_all(moved.reshape(8, tok, 3 * HD), seq, 0, 0)
-    send = call(gate_kernel, [], after=[got], behind=[send])
+        scratch=[pltpu.VMEM((half, width), BF16)],
+    )
+    got_x = [shift(moved[step], "x", 4, step) for step in range(1, 4)]
+    send = call(gate_kernel, [], after=got_x, behind=[send])
     both = call(add_kernel, shape_of(4, 4, HD, HD), keep, shift(send, "core", 2, 1))
     over_y = lax.all_to_all(both.reshape(16, HD, HD), ("x", "y"), 0, 0).reshape(4, 4, HD, HD)
     summed = call(sum_kernel, shape_of(4, HD, HD), over_y, flops=LONG)
     over_z = lax.all_to_all(summed, "z_hi", 0, 0)
+    packed = call(
+        pack_rows_kernel, shape_of(4, tok, 3 * HD), moved, *got_x, place=place, after=[both]
+    )
+    got_z = shift(packed, "z_lo", 2, 1)
     query_grad, key_grad = call(
         assemble_kernel,
         (shape_of(tok, 16 * HD), shape_of(tok, 8 * HD)),
-        got,
-        after=[both],
+        moved, *got_x, got_z,
+        place=place,
+        after=[summed],
     )
     weight_grad = call(last_kernel, shape_of(HD, HD, dtype=F32), over_z)
     return query_grad[None], key_grad[None], weight_grad

time: 94 us -> 88.7 us (0.944)
  the two profiles are of different devices: /device:TPU:8 before, /device:TPU:32 now
where the time goes in v3:
time: 88.7 us; the launch traced here: 88.2 us
  starting transfers between devices  33 us (37%)
  waiting for transfers between devices  30.6 us (34%)
  Pallas kernels  18.3 us (21%)
  local copies, waits for them, and re-layouts  5.47 us (6%)
    ppermute x14, starting transfers between devices, shift(): lax.ppermute(array, axis, [(i, (i + by) % size) for i in range(size)])  14.8 us
    pallas_call x14, Pallas kernels, call(): pl.pallas_call(body, out_shape=shapes, in_specs=specs, out_specs=out_spec...  13.9 us
    ppermute x14, waiting for transfers between devices, shift(): lax.ppermute(array, axis, [(i, (i + by) % size) for i in range(size)])  12.6 us
    all_to_all x1, waiting for transfers between devices, on_device(): lax.all_to_all(both.reshape(16, HD, HD), ('x', 'y'), 0, 0)  11.1 us
    all_to_all x1, starting transfers between devices, on_device(): over_z = lax.all_to_all(summed, 'z_hi', 0, 0)  7.56 us
    all_to_all x1, waiting for transfers between devices, on_device(): over_z = lax.all_to_all(summed, 'z_hi', 0, 0)  6.95 us
    all_to_all x1, starting transfers between devices, on_device(): cot = lax.all_to_all(cot_parts, seq, 0, 0).reshape(length, 2 * HD)  5.76 us
    unnamed x14, local copies, waits for them, and re-layouts  5.41 us
  transfers between devices with their start and end apart: 17, of which 9 were waited for; matrix products, arithmetic and copies ran while one was open for 0% of the time, Pallas kernels for 18%

profile of v3, /device:TPU:32, one launch (start us, length us, event | category | flops | bytes accessed | tf_op | source)
XLA Modules:
  0.0 88.2 jit_solution(2210199562195024924)
XLA Ops:
  0.6 1.0 %copy-done.3 = bf16[1,128,2048]{2,1,0:T(8,128)(2,1)S(1)} copy-done((bf16[1,128,2048]{2,1,0:T(8,128)(2,1)S(1)}, bf16[1,128,2048]{2,1,0:T(8,128)(2,1)}, u32[]{:S(2)}) %copy-start.3) | copy-done | bytes 524312
  1.7 0.8 shard_map.77
  2.5 5.8 %all-to-all-start = ((bf16[8,128,256]{2,1,0:T(8,128)(2,1)}), bf16[8,128,256]{2,1,0:T(8,128)(2,1)S(1)}, u32[]{:S(2)}, u32[]{:S(2)}) async-start(bf16[8,128,256]{2,1,0:T(8,128)(2,1)} %shard_map.77), calls=%async_computation | async-start | bytes 1048576 | tf_op jit(solution)/shard_map/all_to_all | solution.py:281
  8.3 1.2 %copy-done.2 = bf16[1,128,4096]{2,1,0:T(8,128)(2,1)S(1)} copy-done((bf16[1,128,4096]{2,1,0:T(8,128)(2,1)S(1)}, bf16[1,128,4096]{2,1,0:T(8,128)(2,1)}, u32[]{:S(2)}) %copy-start.2) | copy-done | bytes 1048600
  10.2 1.5 %collective-permute-start.7 = (bf16[128,1024]{1,0:T(8,128)(2,1)S(1)}, bf16[128,1024]{1,0:T(8,128)(2,1)S(1)}, u32[]{:S(2)}, u32[]{:S(2)}) collective-permute-start(bf16[128,1024]{1,0:T(8,128)(2,1)S(1)} %get-tuple-element.14), channel_id=1, source_target_pairs={{0,32},{32,64},{64,96},{96,0},{1,33},{33,65},{65,97},{97,1},{2,34}... | collective-permute-start | bytes 786440 | tf_op jit(solution)/shard_map/ppermute | solution.py:269
  11.7 2.7 %collective-permute-start.8 = (bf16[128,1024]{1,0:T(8,128)(2,1)S(1)}, bf16[128,1024]{1,0:T(8,128)(2,1)S(1)}, u32[]{:S(2)}, u32[]{:S(2)}) collective-permute-start(bf16[128,1024]{1,0:T(8,128)(2,1)S(1)} %get-tuple-element.15), channel_id=1, source_target_pairs={{0,64},{32,96},{64,0},{96,32},{1,65},{33,97},{65,1},{97,33},{2,66}... | collective-permute-start | bytes 786440 | tf_op jit(solution)/shard_map/ppermute | solution.py:269
  14.4 1.5 %collective-permute-start.9 = (bf16[128,1024]{1,0:T(8,128)(2,1)S(1)}, bf16[128,1024]{1,0:T(8,128)(2,1)S(1)}, u32[]{:S(2)}, u32[]{:S(2)}) collective-permute-start(bf16[128,1024]{1,0:T(8,128)(2,1)S(1)} %get-tuple-element.16), channel_id=1, source_target_pairs={{0,96},{32,0},{64,32},{96,64},{1,97},{33,1},{65,33},{97,65},{2,98}... | collective-permute-start | bytes 786440 | tf_op jit(solution)/shard_map/ppermute | solution.py:269
  16.4 4.4 %shard_map.76.refs_0_.refs_1_ = bf16[2,1024,1024]{2,1,0:T(8,128)(2,1)} custom-call(bf16[1024,256]{1,0:T(8,128)(2,1)} %bitcast.24, bf16[1024,128]{1,0:T(8,128)(2,1)} %bitcast.26), custom_call_target="tpu_custom_call" | custom-call | flops 34359738368 | bytes 5242880 | tf_op jit(solution)/shard_map/pallas_call | solution.py:107
  20.8 1.7 %collective-permute-done.refs_2_.refs_3_ = bf16[128,1024]{1,0:T(8,128)(2,1)S(1)} collective-permute-done((bf16[128,1024]{1,0:T(8,128)(2,1)S(1)}, bf16[128,1024]{1,0:T(8,128)(2,1)S(1)}, u32[]{:S(2)}, u32[]{:S(2)}) %collective-permute-start) | collective-permute-done | bytes 262176 | tf_op jit(solution)/shard_map/ppermute | solution.py:269
  22.5 2.2 %copy-done = bf16[2,1024,1024]{2,1,0:T(8,128)(2,1)S(1)} copy-done((bf16[2,1024,1024]{2,1,0:T(8,128)(2,1)S(1)}, bf16[2,1024,1024]{2,1,0:T(8,128)(2,1)}, u32[]{:S(2)}) %copy-start) | copy-done | bytes 4194328
  24.7 0.9 %shard_map.79.refs_6_.refs_0_.refs_1_.refs_2_ = bf16[128,1024]{1,0:T(8,128)(2,1)S(1)} custom-call(bf16[2,1024,1024]{2,1,0:T(8,128)(2,1)S(1)} %copy-done, bf16[1024,256]{1,0:T(8,128)(2,1)S(1)} %bitcast.19, bf16[128,1024]{1,0:T(8,128)(2,1)S(1)} %collective-permute-done.refs_2_.refs_3_), custom_call_target="tpu_custom_call" | custom-call | flops 536870912 | bytes 5242880 | tf_op jit(solution)/shard_map/pallas_call | solution.py:251
  26.3 1.4 %collective-permute-start.5 = (bf16[128,1024]{1,0:T(8,128)(2,1)S(1)}, bf16[128,1024]{1,0:T(8,128)(2,1)S(1)}, u32[]{:S(2)}, u32[]{:S(2)}) collective-permute-start(bf16[128,1024]{1,0:T(8,128)(2,1)S(1)} %shard_map.79.refs_6_.refs_0_.refs_1_.refs_2_), channel_id=1, source_target_pairs={{0,64},{32,96},{64,0},{96,32},{1,65},{33,97},{65,1},{97,33},{2,66}... | collective-permute-start | bytes 786440 | tf_op jit(solution)/shard_map/ppermute | solution.py:269
  27.7 1.5 %collective-permute-start.4 = (bf16[128,1024]{1,0:T(8,128)(2,1)S(1)}, bf16[128,1024]{1,0:T(8,128)(2,1)S(1)}, u32[]{:S(2)}, u32[]{:S(2)}) collective-permute-start(bf16[128,1024]{1,0:T(8,128)(2,1)S(1)} %shard_map.79.refs_6_.refs_0_.refs_1_.refs_2_), channel_id=1, source_target_pairs={{0,96},{32,0},{64,32},{96,64},{1,97},{33,1},{65,33},{97,65},{2,98}... | collective-permute-start | bytes 786440 | tf_op jit(solution)/shard_map/ppermute | solution.py:269
  29.3 1.4 %collective-permute-start.10 = (bf16[128,1024]{1,0:T(8,128)(2,1)S(1)}, bf16[128,1024]{1,0:T(8,128)(2,1)S(1)}, u32[]{:S(2)}, u32[]{:S(2)}) collective-permute-start(bf16[128,1024]{1,0:T(8,128)(2,1)S(1)} %shard_map.81.refs_6_), channel_id=1, source_target_pairs={{0,128},{128,0},{1,129},{129,1},{2,130},{130,2},{3,131},{131,3},{4... | collective-permute-start | bytes 786440 | tf_op jit(solution)/shard_map/ppermute | solution.py:269
  30.7 0.9 %collective-permute-start.11 = (bf16[2,128,1024]{2,1,0:T(8,128)(2,1)S(1)}, bf16[2,128,1024]{2,1,0:T(8,128)(2,1)S(1)}, u32[]{:S(2)}, u32[]{:S(2)}) collective-permute-start(bf16[2,128,1024]{2,1,0:T(8,128)(2,1)S(1)} %shard_map.83), channel_id=1, source_target_pairs={{0,128},{128,0},{1,129},{129,1},{2,130},{130,2},{3,131},{131,3},{4... | collective-permute-start | bytes 1572872 | tf_op jit(solution)/shard_map/ppermute | solution.py:269
  31.6 0.9 %copy-done.6 = bf16[1,1024,128]{2,1,0:T(8,128)(2,1)S(1)} copy-done((bf16[1,1024,128]{2,1,0:T(8,128)(2,1)S(1)}, bf16[1,1024,128]{2,1,0:T(8,128)(2,1)}, u32[]{:S(2)}) %copy-start.6) | copy-done | bytes 262168
  32.6 4.3 %shard_map.80.refs_9_.refs_1_ = bf16[4,2,128,384]{3,2,1,0:T(8,128)(2,1)S(1)} custom-call(s32[3]{0:T(128)S(1)} %pad_add_fusion.refs_0_, bf16[2,1024,1024]{2,1,0:T(8,128)(2,1)S(1)} %copy-done.1, bf16[1024,256]{1,0:T(8,128)(2,1)S(1)} %bitcast.25, bf16[1024,128]{1,0:T(8,128)(2,1)S(1)} %bitcast.27, bf16[1024,128]{1,0:T(8,128)(2,1)S(1)} %bitcast.28, ...), custom_call_target="tpu_custom_call" | custom-call | flops 34359738368 | bytes 6291456 | tf_op jit(solution)/shard_map/pallas_call | solution.py:251
  37.0 1.2 %collective-permute-start.3 = (bf16[2,128,384]{2,1,0:T(8,128)(2,1)S(1)}, bf16[2,128,384]{2,1,0:T(8,128)(2,1)S(1)}, u32[]{:S(2)}, u32[]{:S(2)}) collective-permute-start(bf16[2,128,384]{2,1,0:T(8,128)(2,1)S(1)} %get-tuple-element.23), channel_id=1, source_target_pairs={{0,96},{32,0},{64,32},{96,64},{1,97},{33,1},{65,33},{97,65},{2,98}... | collective-permute-start | bytes 589832 | tf_op jit(solution)/shard_map/ppermute | solution.py:269
  38.1 1.5 %collective-permute-done.5.refs_3_ = bf16[128,1024]{1,0:T(8,128)(2,1)S(1)} collective-permute-done((bf16[128,1024]{1,0:T(8,128)(2,1)S(1)}, bf16[128,1024]{1,0:T(8,128)(2,1)S(1)}, u32[]{:S(2)}, u32[]{:S(2)}) %collective-permute-start.5) | collective-permute-done | bytes 262176 | tf_op jit(solution)/shard_map/ppermute | solution.py:269
  40.2 0.8 collective-permute-start.1
  41.1 1.4 %shard_map.82 = (f32[512,1024]{1,0:T(8,128)S(1)}, bf16[512,512]{1,0:T(8,128)(2,1)S(1)}) custom-call(s32[3]{0:T(128)S(1)} %pad_add_fusion.refs_0_, bf16[128,1024]{1,0:T(8,128)(2,1)S(1)} %shard_map.79.refs_6_.refs_0_.refs_1_.refs_2_, bf16[128,1024]{1,0:T(8,128)(2,1)S(1)} %collective-permute-done.4.refs_2_, ...), custom_call_target="tpu_custom_call" | custom-call | tf_op jit(solution)/shard_map/pallas_call | solution.py:251
  42.5 4.7 %collective-permute-done.11.refs_5_ = bf16[2,128,1024]{2,1,0:T(8,128)(2,1)S(1)} collective-permute-done((bf16[2,128,1024]{2,1,0:T(8,128)(2,1)S(1)}, bf16[2,128,1024]{2,1,0:T(8,128)(2,1)S(1)}, u32[]{:S(2)}, u32[]{:S(2)}) %collective-permute-start.11) | collective-permute-done | bytes 524320 | tf_op jit(solution)/shard_map/ppermute | solution.py:269
  47.1 1.3 %shard_map.84 = (f32[4,4,128,128]{3,2,1,0:T(8,128)S(1)}, bf16[4,4,128,128]{3,2,1,0:T(8,128)(2,1)S(1)}) custom-call(s32[3]{0:T(128)S(1)} %pad_add_fusion.refs_0_, f32[512,1024]{1,0:T(8,128)S(1)} %get-tuple-element.17.refs_1_, bf16[512,512]{1,0:T(8,128)(2,1)S(1)} %get-tuple-element.18.refs_2_, bf16[128,1024]{1,0:T(8,128)(2,1)S(1)} %collective-permute-done.refs_2_.refs_3_, ...), custom_call_target="tpu_custom_call" | custom-call | flops 34359738368 | bytes 5242880 | tf_op jit(solution)/shard_map/pallas_call | solution.py:251
  49.0 2.1 %collective-permute-done.1.refs_0_.refs_2_ = bf16[2,128,384]{2,1,0:T(8,128)(2,1)S(1)} collective-permute-done((bf16[2,128,384]{2,1,0:T(8,128)(2,1)S(1)}, bf16[2,128,384]{2,1,0:T(8,128)(2,1)S(1)}, u32[]{:S(2)}, u32[]{:S(2)}) %collective-permute-start.1) | collective-permute-done | bytes 196640 | tf_op jit(solution)/shard_map/ppermute | solution.py:269
  51.2 1.9 %collective-permute-done.12.refs_1_ = bf16[4,4,128,128]{3,2,1,0:T(8,128)(2,1)S(1)} collective-permute-done((bf16[4,4,128,128]{3,2,1,0:T(8,128)(2,1)S(1)}, bf16[4,4,128,128]{3,2,1,0:T(8,128)(2,1)S(1)}, u32[]{:S(2)}, u32[]{:S(2)}) %collective-permute-start.12) | collective-permute-done | bytes 524320 | tf_op jit(solution)/shard_map/ppermute | solution.py:269
  53.1 0.9 %shard_map.86.refs_5_ = bf16[4,4,128,128]{3,2,1,0:T(8,128)(2,1)} custom-call(f32[4,4,128,128]{3,2,1,0:T(8,128)S(1)} %get-tuple-element.19.refs_0_, bf16[4,4,128,128]{3,2,1,0:T(8,128)(2,1)S(1)} %collective-permute-done.12.refs_1_), custom_call_target="tpu_custom_call" | custom-call | bytes 1048576 | tf_op jit(solution)/shard_map/pallas_call | solution.py:251
  54.0 4.9 %all-to-all-start.1 = ((bf16[16,128,128]{2,1,0:T(8,128)(2,1)}), bf16[16,128,128]{2,1,0:T(8,128)(2,1)S(1)}, u32[]{:S(2)}, u32[]{:S(2)}) async-start(bf16[16,128,128]{2,1,0:T(8,128)(2,1)} %bitcast.12), calls=%async_computation.1 | async-start | bytes 1048576 | tf_op jit(solution)/shard_map/all_to_all | solution.py:324
  59.6 11.1 %all-to-all-done.1 = bf16[16,128,128]{2,1,0:T(8,128)(2,1)S(1)} async-done(((bf16[16,128,128]{2,1,0:T(8,128)(2,1)}), bf16[16,128,128]{2,1,0:T(8,128)(2,1)S(1)}, u32[]{:S(2)}, u32[]{:S(2)}) %all-to-all-start.1) | async-done | bytes 524320 | tf_op jit(solution)/shard_map/all_to_all | solution.py:324
  71.4 7.6 %all-to-all-start.2 = ((bf16[4,128,128]{2,1,0:T(8,128)(2,1)}), bf16[4,128,128]{2,1,0:T(8,128)(2,1)S(1)}, u32[]{:S(2)}, u32[]{:S(2)}) async-start(bf16[4,128,128]{2,1,0:T(8,128)(2,1)} %shard_map.88.refs_6_), calls=%async_computation.2 | async-start | bytes 262144 | tf_op jit(solution)/shard_map/all_to_all | solution.py:326
  79.0 1.5 %shard_map.89 = (bf16[128,2048]{1,0:T(8,128)(2,1)}, bf16[128,1024]{1,0:T(8,128)(2,1)}) custom-call(s32[3]{0:T(128)S(1)} %pad_add_fusion.refs_0_, bf16[4,2,128,384]{3,2,1,0:T(8,128)(2,1)S(1)} %shard_map.80.refs_9_.refs_1_, bf16[2,128,384]{2,1,0:T(8,128)(2,1)S(1)} %collective-permute-done.1.refs_0_.refs_2_, ...), custom_call_target="tpu_custom_call" | custom-call | bytes 1048576 | tf_op jit(solution)/shard_map/pallas_call | solution.py:251
  80.5 7.0 %all-to-all-done.2.refs_0_ = bf16[4,128,128]{2,1,0:T(8,128)(2,1)S(1)} async-done(((bf16[4,128,128]{2,1,0:T(8,128)(2,1)}), bf16[4,128,128]{2,1,0:T(8,128)(2,1)S(1)}, u32[]{:S(2)}, u32[]{:S(2)}) %all-to-all-start.2) | async-done | bytes 131104 | tf_op jit(solution)/shard_map/all_to_all | solution.py:326
  87.5 0.7 shard_map.90
  (33 shorter events, 4.6 us)
Async XLA Ops:
  0.6 1.0 %copy-start.3 = (bf16[1,128,2048]{2,1,0:T(8,128)(2,1)S(1)}, bf16[1,128,2048]{2,1,0:T(8,128)(2,1)}, u32[]{:S(2)}) copy-start(bf16[1,128,2048]{2,1,0:T(8,128)(2,1)} %param.8) | copy-start | bytes 1572868
  2.5 20.0 %all-to-all-start = ((bf16[8,128,256]{2,1,0:T(8,128)(2,1)}), bf16[8,128,256]{2,1,0:T(8,128)(2,1)S(1)}, u32[]{:S(2)}, u32[]{:S(2)}) async-start(bf16[8,128,256]{2,1,0:T(8,128)(2,1)} %shard_map.77), calls=%async_computation | async-start | bytes 1048576 | tf_op jit(solution)/shard_map/all_to_all | solution.py:281
  8.3 1.2 %copy-start.2 = (bf16[1,128,4096]{2,1,0:T(8,128)(2,1)S(1)}, bf16[1,128,4096]{2,1,0:T(8,128)(2,1)}, u32[]{:S(2)}) copy-start(bf16[1,128,4096]{2,1,0:T(8,128)(2,1)} %param.9) | copy-start | bytes 3145732
  10.2 17.5 %collective-permute-start.7 = (bf16[128,1024]{1,0:T(8,128)(2,1)S(1)}, bf16[128,1024]{1,0:T(8,128)(2,1)S(1)}, u32[]{:S(2)}, u32[]{:S(2)}) collective-permute-start(bf16[128,1024]{1,0:T(8,128)(2,1)S(1)} %get-tuple-element.14), channel_id=1, source_target_pairs={{0,32},{32,64},{64,96},{96,0},{1,33},{33,65},{65,97},{97,1},{2,34}... | collective-permute-start | bytes 786440 | tf_op jit(solution)/shard_map/ppermute | solution.py:269
  11.7 17.5 %collective-permute-start.8 = (bf16[128,1024]{1,0:T(8,128)(2,1)S(1)}, bf16[128,1024]{1,0:T(8,128)(2,1)S(1)}, u32[]{:S(2)}, u32[]{:S(2)}) collective-permute-start(bf16[128,1024]{1,0:T(8,128)(2,1)S(1)} %get-tuple-element.15), channel_id=1, source_target_pairs={{0,64},{32,96},{64,0},{96,32},{1,65},{33,97},{65,1},{97,33},{2,66}... | collective-permute-start | bytes 786440 | tf_op jit(solution)/shard_map/ppermute | solution.py:269
  14.4 16.2 %collective-permute-start.9 = (bf16[128,1024]{1,0:T(8,128)(2,1)S(1)}, bf16[128,1024]{1,0:T(8,128)(2,1)S(1)}, u32[]{:S(2)}, u32[]{:S(2)}) collective-permute-start(bf16[128,1024]{1,0:T(8,128)(2,1)S(1)} %get-tuple-element.16), channel_id=1, source_target_pairs={{0,96},{32,0},{64,32},{96,64},{1,97},{33,1},{65,33},{97,65},{2,98}... | collective-permute-start | bytes 786440 | tf_op jit(solution)/shard_map/ppermute | solution.py:269
  15.9 6.6 %collective-permute-start = (bf16[128,1024]{1,0:T(8,128)(2,1)S(1)}, bf16[128,1024]{1,0:T(8,128)(2,1)S(1)}, u32[]{:S(2)}, u32[]{:S(2)}) collective-permute-start(bf16[128,1024]{1,0:T(8,128)(2,1)S(1)} %get-tuple-element.13.refs_5_), channel_id=1, source_target_pairs={{0,128},{128,0},{1,129},{129,1},{2,130},{130,2},{3,131},{131,3},{4... | collective-permute-start | bytes 786440 | tf_op jit(solution)/shard_map/ppermute | solution.py:269
  16.4 15.2 %copy-start.4 = (bf16[1,1024,256]{2,1,0:T(8,128)(2,1)S(1)}, bf16[1,1024,256]{2,1,0:T(8,128)(2,1)}, u32[]{:S(2)}) copy-start(bf16[1,1024,256]{2,1,0:T(8,128)(2,1)} %param.5) | copy-start | bytes 1572868
  16.4 15.2 %copy-start.5 = (bf16[1,1024,128]{2,1,0:T(8,128)(2,1)S(1)}, bf16[1,1024,128]{2,1,0:T(8,128)(2,1)}, u32[]{:S(2)}) copy-start(bf16[1,1024,128]{2,1,0:T(8,128)(2,1)} %param.6) | copy-start | bytes 786436
  22.5 2.2 %copy-start = (bf16[2,1024,1024]{2,1,0:T(8,128)(2,1)S(1)}, bf16[2,1024,1024]{2,1,0:T(8,128)(2,1)}, u32[]{:S(2)}) copy-start(bf16[2,1024,1024]{2,1,0:T(8,128)(2,1)} %shard_map.76.refs_0_.refs_1_) | copy-start | bytes 12582916
  24.7 6.9 %copy-start.1 = (bf16[2,1024,1024]{2,1,0:T(8,128)(2,1)S(1)}, bf16[2,1024,1024]{2,1,0:T(8,128)(2,1)}, u32[]{:S(2)}) copy-start(bf16[2,1024,1024]{2,1,0:T(8,128)(2,1)} %shard_map.76.refs_0_.refs_1_) | copy-start | bytes 12582916
  25.6 11.3 %collective-permute-start.6 = (bf16[128,1024]{1,0:T(8,128)(2,1)S(1)}, bf16[128,1024]{1,0:T(8,128)(2,1)S(1)}, u32[]{:S(2)}, u32[]{:S(2)}) collective-permute-start(bf16[128,1024]{1,0:T(8,128)(2,1)S(1)} %shard_map.79.refs_6_.refs_0_.refs_1_.refs_2_), channel_id=1, source_target_pairs={{0,32},{32,64},{64,96},{96,0},{1,33},{33,65},{65,97},{97,1},{2,34}... | collective-permute-start | bytes 786440 | tf_op jit(solution)/shard_map/ppermute | solution.py:269
  26.3 13.4 %collective-permute-start.5 = (bf16[128,1024]{1,0:T(8,128)(2,1)S(1)}, bf16[128,1024]{1,0:T(8,128)(2,1)S(1)}, u32[]{:S(2)}, u32[]{:S(2)}) collective-permute-start(bf16[128,1024]{1,0:T(8,128)(2,1)S(1)} %shard_map.79.refs_6_.refs_0_.refs_1_.refs_2_), channel_id=1, source_target_pairs={{0,64},{32,96},{64,0},{96,32},{1,65},{33,97},{65,1},{97,33},{2,66}... | collective-permute-start | bytes 786440 | tf_op jit(solution)/shard_map/ppermute | solution.py:269
  27.7 12.5 %collective-permute-start.4 = (bf16[128,1024]{1,0:T(8,128)(2,1)S(1)}, bf16[128,1024]{1,0:T(8,128)(2,1)S(1)}, u32[]{:S(2)}, u32[]{:S(2)}) collective-permute-start(bf16[128,1024]{1,0:T(8,128)(2,1)S(1)} %shard_map.79.refs_6_.refs_0_.refs_1_.refs_2_), channel_id=1, source_target_pairs={{0,96},{32,0},{64,32},{96,64},{1,97},{33,1},{65,33},{97,65},{2,98}... | collective-permute-start | bytes 786440 | tf_op jit(solution)/shard_map/ppermute | solution.py:269
  29.3 13.2 %collective-permute-start.10 = (bf16[128,1024]{1,0:T(8,128)(2,1)S(1)}, bf16[128,1024]{1,0:T(8,128)(2,1)S(1)}, u32[]{:S(2)}, u32[]{:S(2)}) collective-permute-start(bf16[128,1024]{1,0:T(8,128)(2,1)S(1)} %shard_map.81.refs_6_), channel_id=1, source_target_pairs={{0,128},{128,0},{1,129},{129,1},{2,130},{130,2},{3,131},{131,3},{4... | collective-permute-start | bytes 786440 | tf_op jit(solution)/shard_map/ppermute | solution.py:269
  30.7 16.4 %collective-permute-start.11 = (bf16[2,128,1024]{2,1,0:T(8,128)(2,1)S(1)}, bf16[2,128,1024]{2,1,0:T(8,128)(2,1)S(1)}, u32[]{:S(2)}, u32[]{:S(2)}) collective-permute-start(bf16[2,128,1024]{2,1,0:T(8,128)(2,1)S(1)} %shard_map.83), channel_id=1, source_target_pairs={{0,128},{128,0},{1,129},{129,1},{2,130},{130,2},{3,131},{131,3},{4... | collective-permute-start | bytes 1572872 | tf_op jit(solution)/shard_map/ppermute | solution.py:269
  31.6 1.0 %copy-start.6 = (bf16[1,1024,128]{2,1,0:T(8,128)(2,1)S(1)}, bf16[1,1024,128]{2,1,0:T(8,128)(2,1)}, u32[]{:S(2)}) copy-start(bf16[1,1024,128]{2,1,0:T(8,128)(2,1)} %param.7) | copy-start | bytes 786436
  37.0 11.5 %collective-permute-start.3 = (bf16[2,128,384]{2,1,0:T(8,128)(2,1)S(1)}, bf16[2,128,384]{2,1,0:T(8,128)(2,1)S(1)}, u32[]{:S(2)}, u32[]{:S(2)}) collective-permute-start(bf16[2,128,384]{2,1,0:T(8,128)(2,1)S(1)} %get-tuple-element.23), channel_id=1, source_target_pairs={{0,96},{32,0},{64,32},{96,64},{1,97},{33,1},{65,33},{97,65},{2,98}... | collective-permute-start | bytes 589832 | tf_op jit(solution)/shard_map/ppermute | solution.py:269
  39.6 9.3 %collective-permute-start.2 = (bf16[2,128,384]{2,1,0:T(8,128)(2,1)S(1)}, bf16[2,128,384]{2,1,0:T(8,128)(2,1)S(1)}, u32[]{:S(2)}, u32[]{:S(2)}) collective-permute-start(bf16[2,128,384]{2,1,0:T(8,128)(2,1)S(1)} %get-tuple-element.24), channel_id=1, source_target_pairs={{0,64},{32,96},{64,0},{96,32},{1,65},{33,97},{65,1},{97,33},{2,66}... | collective-permute-start | bytes 589832 | tf_op jit(solution)/shard_map/ppermute | solution.py:269
  40.2 10.9 %collective-permute-start.1 = (bf16[2,128,384]{2,1,0:T(8,128)(2,1)S(1)}, bf16[2,128,384]{2,1,0:T(8,128)(2,1)S(1)}, u32[]{:S(2)}, u32[]{:S(2)}) collective-permute-start(bf16[2,128,384]{2,1,0:T(8,128)(2,1)S(1)} %get-tuple-element.25), channel_id=1, source_target_pairs={{0,32},{32,64},{64,96},{96,0},{1,33},{33,65},{65,97},{97,1},{2,34}... | collective-permute-start | bytes 589832 | tf_op jit(solution)/shard_map/ppermute | solution.py:269
  51.1 1.9 %collective-permute-start.12 = (bf16[4,4,128,128]{3,2,1,0:T(8,128)(2,1)S(1)}, bf16[4,4,128,128]{3,2,1,0:T(8,128)(2,1)S(1)}, u32[]{:S(2)}, u32[]{:S(2)}) collective-permute-start(bf16[4,4,128,128]{3,2,1,0:T(8,128)(2,1)S(1)} %shard_map.85), channel_id=1, source_target_pairs={{0,1},{1,0},{2,3},{3,2},{4,5},{5,4},{6,7},{7,6},{8,9},{9,8},{10,11... | collective-permute-start | bytes 1572872 | tf_op jit(solution)/shard_map/ppermute | solution.py:269
  54.0 16.7 %all-to-all-start.1 = ((bf16[16,128,128]{2,1,0:T(8,128)(2,1)}), bf16[16,128,128]{2,1,0:T(8,128)(2,1)S(1)}, u32[]{:S(2)}, u32[]{:S(2)}) async-start(bf16[16,128,128]{2,1,0:T(8,128)(2,1)} %bitcast.12), calls=%async_computation.1 | async-start | bytes 1048576 | tf_op jit(solution)/shard_map/all_to_all | solution.py:324
  59.5 19.5 %collective-permute-start.13 = (bf16[4,128,384]{2,1,0:T(8,128)(2,1)S(1)}, bf16[4,128,384]{2,1,0:T(8,128)(2,1)S(1)}, u32[]{:S(2)}, u32[]{:S(2)}) collective-permute-start(bf16[4,128,384]{2,1,0:T(8,128)(2,1)S(1)} %shard_map.87), channel_id=1, source_target_pairs={{0,128},{128,0},{1,129},{129,1},{2,130},{130,2},{3,131},{131,3},{4... | collective-permute-start | bytes 1179656 | tf_op jit(solution)/shard_map/ppermute | solution.py:269
  71.4 16.1 %all-to-all-start.2 = ((bf16[4,128,128]{2,1,0:T(8,128)(2,1)}), bf16[4,128,128]{2,1,0:T(8,128)(2,1)S(1)}, u32[]{:S(2)}, u32[]{:S(2)}) async-start(bf16[4,128,128]{2,1,0:T(8,128)(2,1)} %shard_map.88.refs_6_), calls=%async_computation.2 | async-start | bytes 262144 | tf_op jit(solution)/shard_map/all_to_all | solution.py:326

commit v4 on v3

--- a/solution.py
+++ b/solution.py
@@ -189,19 +189,28 @@
     out_ref[...] = (keep_ref[...] + got_ref[...].astype(F32)).astype(BF16)
 
 
-def sum_kernel(got_ref, out_ref):
-    for x in range(4):
-        total = got_ref[x, 0].astype(F32)
+def sum_kernel(place_ref, got_ref, keep_ref, send_ref):
+    z_hi = place_ref[3]
+    beside = z_hi + 1 - 2 * lax.rem(z_hi, 2)
+
+    def summed(block):
+        total = got_ref[block, 0].astype(F32)
         for y in range(1, 4):
-            total += got_ref[x, y].astype(F32)
-        out_ref[x] = total.astype(BF16)
-
-
-def last_kernel(got_ref, out_ref):
-    total = got_ref[0].astype(F32)
-    for z in range(1, 4):
-        total += got_ref[z].astype(F32)
-    out_ref[...] = total.T
+            total += got_ref[block, y].astype(F32)
+        return total
+
+    for index in range(2):
+        send_ref[index] = summed(beside + index * (3 - 2 * beside)).astype(BF16)
+        keep_ref[index] = summed(z_hi + index * (3 - 2 * z_hi))
+
+
+def pair_kernel(keep_ref, got_ref, own_ref, send_ref):
+    own_ref[...] = keep_ref[0] + got_ref[0].astype(F32)
+    send_ref[...] = keep_ref[1] + got_ref[1].astype(F32)
+
+
+def last_kernel(own_ref, got_ref, out_ref):
+    out_ref[...] = (own_ref[...] + got_ref[...]).T
 
 
 def pack_rows_kernel(place_ref, own_ref, a_ref, b_ref, c_ref, out_ref):
@@ -273,7 +282,7 @@
     q, k, v = queries[0], key_heads[0], value_heads[0]
     length = q.shape[0]
     seq = ("z_lo", "x")
-    place = jnp.stack([lax.axis_index(a) for a in ("x", "core", "z_lo")]).astype(jnp.int32)
+    place = jnp.stack([lax.axis_index(a) for a in ("x", "core", "z_lo", "z_hi")]).astype(jnp.int32)
     tok = grad_out.shape[1]
     width = features.shape[2] // 4
 
@@ -322,8 +331,16 @@
     send = call(gate_kernel, [], after=got_x, behind=[send])
     both = call(add_kernel, shape_of(4, 4, HD, HD), keep, shift(send, "core", 2, 1))
     over_y = lax.all_to_all(both.reshape(16, HD, HD), ("x", "y"), 0, 0).reshape(4, 4, HD, HD)
-    summed = call(sum_kernel, shape_of(4, HD, HD), over_y, flops=LONG)
-    over_z = lax.all_to_all(summed, "z_hi", 0, 0)
+    keep, send = call(
+        sum_kernel,
+        [shape_of(2, HD, HD, dtype=F32), shape_of(2, HD, HD)],
+        over_y,
+        place=place,
+        flops=LONG,
+    )
+    got = lax.ppermute(send, "z_hi", [(z, z ^ 1) for z in range(4)])
+    own, send = call(pair_kernel, [shape_of(HD, HD, dtype=F32)] * 2, keep, got)
+    got = lax.ppermute(send, "z_hi", [(z, 3 - z) for z in range(4)])
     packed = call(
         pack_rows_kernel, shape_of(4, tok, 3 * HD), moved, *got_x, place=place, after=[both]
     )
@@ -333,9 +350,9 @@
         (shape_of(tok, 16 * HD), shape_of(tok, 8 * HD)),
         moved, *got_x, got_z,
         place=place,
-        after=[summed],
-    )
-    weight_grad = call(last_kernel, shape_of(HD, HD, dtype=F32), over_z)
+        after=[own],
+    )
+    weight_grad = call(last_kernel, shape_of(HD, HD, dtype=F32), own, got)
     return query_grad[None], key_grad[None], weight_grad
 
 

time: 88.7 us -> 85.5 us (0.964)
  waiting for transfers between devices: 30.6 us -> 26.6 us
  starting transfers between devices: 33 us -> 33.9 us
    ppermute x0 -> x2, starting transfers between devices: none -> 8.49 us  [the longest x1 5.14 us: on_device(): got = lax.ppermute(send, 'z_hi', [(z, 3 - z) for z in range(4)])]
    all_to_all x1 -> x0, starting transfers between devices: 7.56 us -> none  [on_device(): over_z = lax.all_to_all(summed, 'z_hi', 0, 0)]
    all_to_all x1 -> x0, waiting for transfers between devices: 6.95 us -> none  [on_device(): over_z = lax.all_to_all(summed, 'z_hi', 0, 0)]
    ppermute x0 -> x2, waiting for transfers between devices: none -> 2.94 us  [the longest x1 2.25 us: on_device(): got = lax.ppermute(send, 'z_hi', [(z, z ^ 1) for z in range(4)])]
    pallas_call x14 -> x15, Pallas kernels: 13.9 us -> 13.8 us  [call(): pl.pallas_call(body, out_shape=shapes, in_specs=specs, out_specs=out_spec...]
  transfers between devices with their start and end apart: 17 -> 18, of which waited for: 9 -> 10; matrix products, arithmetic and copies ran while one was open for 0% -> 0% of each run, Pallas kernels for 18% -> 18%
where the time goes in v4:
time: 85.5 us; the launch traced here: 85 us
  starting transfers between devices  33.9 us (40%)
  waiting for transfers between devices  26.6 us (31%)
  Pallas kernels  18.2 us (21%)
  local copies, waits for them, and re-layouts  5.47 us (6%)
    ppermute x14, starting transfers between devices, shift(): lax.ppermute(array, axis, [(i, (i + by) % size) for i in range(size)])  14.8 us
    pallas_call x15, Pallas kernels, call(): pl.pallas_call(body, out_shape=shapes, in_specs=specs, out_specs=out_spec...  13.8 us
    ppermute x14, waiting for transfers between devices, shift(): lax.ppermute(array, axis, [(i, (i + by) % size) for i in range(size)])  12.6 us
    all_to_all x1, waiting for transfers between devices, on_device(): lax.all_to_all(both.reshape(16, HD, HD), ('x', 'y'), 0, 0)  11.1 us
    all_to_all x1, starting transfers between devices, on_device(): cot = lax.all_to_all(cot_parts, seq, 0, 0).reshape(length, 2 * HD)  5.76 us
    unnamed x14, local copies, waits for them, and re-layouts  5.41 us
    ppermute x1, starting transfers between devices, on_device(): got = lax.ppermute(send, 'z_hi', [(z, 3 - z) for z in range(4)])  5.14 us
    all_to_all x1, starting transfers between devices, on_device(): lax.all_to_all(both.reshape(16, HD, HD), ('x', 'y'), 0, 0)  4.91 us
  transfers between devices with their start and end apart: 18, of which 10 were waited for; matrix products, arithmetic and copies ran while one was open for 0% of the time, Pallas kernels for 18%

profile of v4, /device:TPU:32, one launch (start us, length us, event | category | flops | bytes accessed | tf_op | source)
XLA Modules:
  0.0 85.0 jit_solution(7941338187257382817)
XLA Ops:
  0.6 1.0 %copy-done.3 = bf16[1,128,2048]{2,1,0:T(8,128)(2,1)S(1)} copy-done((bf16[1,128,2048]{2,1,0:T(8,128)(2,1)S(1)}, bf16[1,128,2048]{2,1,0:T(8,128)(2,1)}, u32[]{:S(2)}) %copy-start.3) | copy-done | bytes 524312
  1.7 0.8 shard_map.77
  2.5 5.8 %all-to-all-start = ((bf16[8,128,256]{2,1,0:T(8,128)(2,1)}), bf16[8,128,256]{2,1,0:T(8,128)(2,1)S(1)}, u32[]{:S(2)}, u32[]{:S(2)}) async-start(bf16[8,128,256]{2,1,0:T(8,128)(2,1)} %shard_map.77), calls=%async_computation | async-start | bytes 1048576 | tf_op jit(solution)/shard_map/all_to_all | solution.py:290
  8.3 1.2 %copy-done.2 = bf16[1,128,4096]{2,1,0:T(8,128)(2,1)S(1)} copy-done((bf16[1,128,4096]{2,1,0:T(8,128)(2,1)S(1)}, bf16[1,128,4096]{2,1,0:T(8,128)(2,1)}, u32[]{:S(2)}) %copy-start.2) | copy-done | bytes 1048600
  10.2 1.5 %collective-permute-start.7 = (bf16[128,1024]{1,0:T(8,128)(2,1)S(1)}, bf16[128,1024]{1,0:T(8,128)(2,1)S(1)}, u32[]{:S(2)}, u32[]{:S(2)}) collective-permute-start(bf16[128,1024]{1,0:T(8,128)(2,1)S(1)} %get-tuple-element.18), channel_id=1, source_target_pairs={{0,32},{32,64},{64,96},{96,0},{1,33},{33,65},{65,97},{97,1},{2,34}... | collective-permute-start | bytes 786440 | tf_op jit(solution)/shard_map/ppermute | solution.py:278
  11.7 2.7 %collective-permute-start.8 = (bf16[128,1024]{1,0:T(8,128)(2,1)S(1)}, bf16[128,1024]{1,0:T(8,128)(2,1)S(1)}, u32[]{:S(2)}, u32[]{:S(2)}) collective-permute-start(bf16[128,1024]{1,0:T(8,128)(2,1)S(1)} %get-tuple-element.19), channel_id=1, source_target_pairs={{0,64},{32,96},{64,0},{96,32},{1,65},{33,97},{65,1},{97,33},{2,66}... | collective-permute-start | bytes 786440 | tf_op jit(solution)/shard_map/ppermute | solution.py:278
  14.4 1.5 %collective-permute-start.9 = (bf16[128,1024]{1,0:T(8,128)(2,1)S(1)}, bf16[128,1024]{1,0:T(8,128)(2,1)S(1)}, u32[]{:S(2)}, u32[]{:S(2)}) collective-permute-start(bf16[128,1024]{1,0:T(8,128)(2,1)S(1)} %get-tuple-element.20), channel_id=1, source_target_pairs={{0,96},{32,0},{64,32},{96,64},{1,97},{33,1},{65,33},{97,65},{2,98}... | collective-permute-start | bytes 786440 | tf_op jit(solution)/shard_map/ppermute | solution.py:278
  16.4 4.4 %shard_map.76.refs_0_.refs_1_ = bf16[2,1024,1024]{2,1,0:T(8,128)(2,1)} custom-call(bf16[1024,256]{1,0:T(8,128)(2,1)} %bitcast.25, bf16[1024,128]{1,0:T(8,128)(2,1)} %bitcast.27), custom_call_target="tpu_custom_call" | custom-call | flops 34359738368 | bytes 5242880 | tf_op jit(solution)/shard_map/pallas_call | solution.py:107
  20.8 1.7 %collective-permute-done.refs_2_.refs_3_ = bf16[128,1024]{1,0:T(8,128)(2,1)S(1)} collective-permute-done((bf16[128,1024]{1,0:T(8,128)(2,1)S(1)}, bf16[128,1024]{1,0:T(8,128)(2,1)S(1)}, u32[]{:S(2)}, u32[]{:S(2)}) %collective-permute-start) | collective-permute-done | bytes 262176 | tf_op jit(solution)/shard_map/ppermute | solution.py:278
  22.5 2.2 %copy-done = bf16[2,1024,1024]{2,1,0:T(8,128)(2,1)S(1)} copy-done((bf16[2,1024,1024]{2,1,0:T(8,128)(2,1)S(1)}, bf16[2,1024,1024]{2,1,0:T(8,128)(2,1)}, u32[]{:S(2)}) %copy-start) | copy-done | bytes 4194328
  24.7 0.9 %shard_map.79.refs_6_.refs_0_.refs_1_.refs_2_ = bf16[128,1024]{1,0:T(8,128)(2,1)S(1)} custom-call(bf16[2,1024,1024]{2,1,0:T(8,128)(2,1)S(1)} %copy-done, bf16[1024,256]{1,0:T(8,128)(2,1)S(1)} %bitcast.20, bf16[128,1024]{1,0:T(8,128)(2,1)S(1)} %collective-permute-done.refs_2_.refs_3_), custom_call_target="tpu_custom_call" | custom-call | flops 536870912 | bytes 5242880 | tf_op jit(solution)/shard_map/pallas_call | solution.py:260
  26.3 1.4 %collective-permute-start.5 = (bf16[128,1024]{1,0:T(8,128)(2,1)S(1)}, bf16[128,1024]{1,0:T(8,128)(2,1)S(1)}, u32[]{:S(2)}, u32[]{:S(2)}) collective-permute-start(bf16[128,1024]{1,0:T(8,128)(2,1)S(1)} %shard_map.79.refs_6_.refs_0_.refs_1_.refs_2_), channel_id=1, source_target_pairs={{0,64},{32,96},{64,0},{96,32},{1,65},{33,97},{65,1},{97,33},{2,66}... | collective-permute-start | bytes 786440 | tf_op jit(solution)/shard_map/ppermute | solution.py:278
  27.7 1.5 %collective-permute-start.4 = (bf16[128,1024]{1,0:T(8,128)(2,1)S(1)}, bf16[128,1024]{1,0:T(8,128)(2,1)S(1)}, u32[]{:S(2)}, u32[]{:S(2)}) collective-permute-start(bf16[128,1024]{1,0:T(8,128)(2,1)S(1)} %shard_map.79.refs_6_.refs_0_.refs_1_.refs_2_), channel_id=1, source_target_pairs={{0,96},{32,0},{64,32},{96,64},{1,97},{33,1},{65,33},{97,65},{2,98}... | collective-permute-start | bytes 786440 | tf_op jit(solution)/shard_map/ppermute | solution.py:278
  29.3 1.4 %collective-permute-start.10 = (bf16[128,1024]{1,0:T(8,128)(2,1)S(1)}, bf16[128,1024]{1,0:T(8,128)(2,1)S(1)}, u32[]{:S(2)}, u32[]{:S(2)}) collective-permute-start(bf16[128,1024]{1,0:T(8,128)(2,1)S(1)} %shard_map.81.refs_6_), channel_id=1, source_target_pairs={{0,128},{128,0},{1,129},{129,1},{2,130},{130,2},{3,131},{131,3},{4... | collective-permute-start | bytes 786440 | tf_op jit(solution)/shard_map/ppermute | solution.py:278
  30.7 0.9 %collective-permute-start.11 = (bf16[2,128,1024]{2,1,0:T(8,128)(2,1)S(1)}, bf16[2,128,1024]{2,1,0:T(8,128)(2,1)S(1)}, u32[]{:S(2)}, u32[]{:S(2)}) collective-permute-start(bf16[2,128,1024]{2,1,0:T(8,128)(2,1)S(1)} %shard_map.83), channel_id=1, source_target_pairs={{0,128},{128,0},{1,129},{129,1},{2,130},{130,2},{3,131},{131,3},{4... | collective-permute-start | bytes 1572872 | tf_op jit(solution)/shard_map/ppermute | solution.py:278
  31.6 0.9 %copy-done.6 = bf16[1,1024,128]{2,1,0:T(8,128)(2,1)S(1)} copy-done((bf16[1,1024,128]{2,1,0:T(8,128)(2,1)S(1)}, bf16[1,1024,128]{2,1,0:T(8,128)(2,1)}, u32[]{:S(2)}) %copy-start.6) | copy-done | bytes 262168
  32.6 4.3 %shard_map.80.refs_9_.refs_1_ = bf16[4,2,128,384]{3,2,1,0:T(8,128)(2,1)S(1)} custom-call(s32[4]{0:T(128)S(1)} %pad_add_fusion.refs_0_, bf16[2,1024,1024]{2,1,0:T(8,128)(2,1)S(1)} %copy-done.1, bf16[1024,256]{1,0:T(8,128)(2,1)S(1)} %bitcast.26, bf16[1024,128]{1,0:T(8,128)(2,1)S(1)} %bitcast.28, bf16[1024,128]{1,0:T(8,128)(2,1)S(1)} %bitcast.29, ...), custom_call_target="tpu_custom_call" | custom-call | flops 34359738368 | bytes 6291456 | tf_op jit(solution)/shard_map/pallas_call | solution.py:260
  37.0 1.2 %collective-permute-start.3 = (bf16[2,128,384]{2,1,0:T(8,128)(2,1)S(1)}, bf16[2,128,384]{2,1,0:T(8,128)(2,1)S(1)}, u32[]{:S(2)}, u32[]{:S(2)}) collective-permute-start(bf16[2,128,384]{2,1,0:T(8,128)(2,1)S(1)} %get-tuple-element.31), channel_id=1, source_target_pairs={{0,96},{32,0},{64,32},{96,64},{1,97},{33,1},{65,33},{97,65},{2,98}... | collective-permute-start | bytes 589832 | tf_op jit(solution)/shard_map/ppermute | solution.py:278
  38.1 1.5 %collective-permute-done.5.refs_3_ = bf16[128,1024]{1,0:T(8,128)(2,1)S(1)} collective-permute-done((bf16[128,1024]{1,0:T(8,128)(2,1)S(1)}, bf16[128,1024]{1,0:T(8,128)(2,1)S(1)}, u32[]{:S(2)}, u32[]{:S(2)}) %collective-permute-start.5) | collective-permute-done | bytes 262176 | tf_op jit(solution)/shard_map/ppermute | solution.py:278
  40.2 0.8 collective-permute-start.1
  41.1 1.4 %shard_map.82 = (f32[512,1024]{1,0:T(8,128)S(1)}, bf16[512,512]{1,0:T(8,128)(2,1)S(1)}) custom-call(s32[4]{0:T(128)S(1)} %pad_add_fusion.refs_0_, bf16[128,1024]{1,0:T(8,128)(2,1)S(1)} %shard_map.79.refs_6_.refs_0_.refs_1_.refs_2_, bf16[128,1024]{1,0:T(8,128)(2,1)S(1)} %collective-permute-done.4.refs_2_, ...), custom_call_target="tpu_custom_call" | custom-call | tf_op jit(solution)/shard_map/pallas_call | solution.py:260
  42.5 4.7 %collective-permute-done.11.refs_5_ = bf16[2,128,1024]{2,1,0:T(8,128)(2,1)S(1)} collective-permute-done((bf16[2,128,1024]{2,1,0:T(8,128)(2,1)S(1)}, bf16[2,128,1024]{2,1,0:T(8,128)(2,1)S(1)}, u32[]{:S(2)}, u32[]{:S(2)}) %collective-permute-start.11) | collective-permute-done | bytes 524320 | tf_op jit(solution)/shard_map/ppermute | solution.py:278
  47.1 1.3 %shard_map.84 = (f32[4,4,128,128]{3,2,1,0:T(8,128)S(1)}, bf16[4,4,128,128]{3,2,1,0:T(8,128)(2,1)S(1)}) custom-call(s32[4]{0:T(128)S(1)} %pad_add_fusion.refs_0_, f32[512,1024]{1,0:T(8,128)S(1)} %get-tuple-element.21.refs_1_, bf16[512,512]{1,0:T(8,128)(2,1)S(1)} %get-tuple-element.22.refs_2_, bf16[128,1024]{1,0:T(8,128)(2,1)S(1)} %collective-permute-done.refs_2_.refs_3_, ...), custom_call_target="tpu_custom_call" | custom-call | flops 34359738368 | bytes 5242880 | tf_op jit(solution)/shard_map/pallas_call | solution.py:260
  49.0 2.1 %collective-permute-done.1.refs_0_.refs_2_ = bf16[2,128,384]{2,1,0:T(8,128)(2,1)S(1)} collective-permute-done((bf16[2,128,384]{2,1,0:T(8,128)(2,1)S(1)}, bf16[2,128,384]{2,1,0:T(8,128)(2,1)S(1)}, u32[]{:S(2)}, u32[]{:S(2)}) %collective-permute-start.1) | collective-permute-done | bytes 196640 | tf_op jit(solution)/shard_map/ppermute | solution.py:278
  51.2 1.9 %collective-permute-done.12.refs_1_ = bf16[4,4,128,128]{3,2,1,0:T(8,128)(2,1)S(1)} collective-permute-done((bf16[4,4,128,128]{3,2,1,0:T(8,128)(2,1)S(1)}, bf16[4,4,128,128]{3,2,1,0:T(8,128)(2,1)S(1)}, u32[]{:S(2)}, u32[]{:S(2)}) %collective-permute-start.12) | collective-permute-done | bytes 524320 | tf_op jit(solution)/shard_map/ppermute | solution.py:278
  53.1 0.9 %shard_map.86.refs_5_ = bf16[4,4,128,128]{3,2,1,0:T(8,128)(2,1)} custom-call(f32[4,4,128,128]{3,2,1,0:T(8,128)S(1)} %get-tuple-element.23.refs_0_, bf16[4,4,128,128]{3,2,1,0:T(8,128)(2,1)S(1)} %collective-permute-done.12.refs_1_), custom_call_target="tpu_custom_call" | custom-call | bytes 1048576 | tf_op jit(solution)/shard_map/pallas_call | solution.py:260
  54.0 4.9 %all-to-all-start.1 = ((bf16[16,128,128]{2,1,0:T(8,128)(2,1)}), bf16[16,128,128]{2,1,0:T(8,128)(2,1)S(1)}, u32[]{:S(2)}, u32[]{:S(2)}) async-start(bf16[16,128,128]{2,1,0:T(8,128)(2,1)} %bitcast.13), calls=%async_computation.1 | async-start | bytes 1048576 | tf_op jit(solution)/shard_map/all_to_all | solution.py:333
  59.6 11.1 %all-to-all-done.1 = bf16[16,128,128]{2,1,0:T(8,128)(2,1)S(1)} async-done(((bf16[16,128,128]{2,1,0:T(8,128)(2,1)}), bf16[16,128,128]{2,1,0:T(8,128)(2,1)S(1)}, u32[]{:S(2)}, u32[]{:S(2)}) %all-to-all-start.1) | async-done | bytes 524320 | tf_op jit(solution)/shard_map/all_to_all | solution.py:333
  71.3 3.4 %collective-permute-start.14 = (bf16[2,128,128]{2,1,0:T(8,128)(2,1)S(1)}, bf16[2,128,128]{2,1,0:T(8,128)(2,1)S(1)}, u32[]{:S(2)}, u32[]{:S(2)}) collective-permute-start(bf16[2,128,128]{2,1,0:T(8,128)(2,1)S(1)} %get-tuple-element.26), channel_id=1, source_target_pairs={{0,8},{8,0},{16,24},{24,16},{1,9},{9,1},{17,25},{25,17},{2,10},{10... | collective-permute-start | bytes 196616 | tf_op jit(solution)/shard_map/ppermute | solution.py:341
  74.6 2.2 %collective-permute-done.14.refs_1_ = bf16[2,128,128]{2,1,0:T(8,128)(2,1)S(1)} collective-permute-done((bf16[2,128,128]{2,1,0:T(8,128)(2,1)S(1)}, bf16[2,128,128]{2,1,0:T(8,128)(2,1)S(1)}, u32[]{:S(2)}, u32[]{:S(2)}) %collective-permute-start.14) | collective-permute-done | bytes 65568 | tf_op jit(solution)/shard_map/ppermute | solution.py:341
  76.9 5.1 %collective-permute-start.15 = (f32[128,128]{1,0:T(8,128)S(1)}, f32[128,128]{1,0:T(8,128)S(1)}, u32[]{:S(2)}, u32[]{:S(2)}) collective-permute-start(f32[128,128]{1,0:T(8,128)S(1)} %get-tuple-element.30), channel_id=1, source_target_pairs={{0,24},{8,16},{16,8},{24,0},{1,25},{9,17},{17,9},{25,1},{2,26},{10... | collective-permute-start | bytes 196616 | tf_op jit(solution)/shard_map/ppermute | solution.py:343
  82.0 1.5 %shard_map.90 = (bf16[128,2048]{1,0:T(8,128)(2,1)}, bf16[128,1024]{1,0:T(8,128)(2,1)}) custom-call(s32[4]{0:T(128)S(1)} %pad_add_fusion.refs_0_, bf16[4,2,128,384]{3,2,1,0:T(8,128)(2,1)S(1)} %shard_map.80.refs_9_.refs_1_, bf16[2,128,384]{2,1,0:T(8,128)(2,1)S(1)} %collective-permute-done.1.refs_0_.refs_2_, ...), custom_call_target="tpu_custom_call" | custom-call | bytes 1048576 | tf_op jit(solution)/shard_map/pallas_call | solution.py:260
  (36 shorter events, 5.9 us)
Async XLA Ops:
  0.6 1.0 %copy-start.3 = (bf16[1,128,2048]{2,1,0:T(8,128)(2,1)S(1)}, bf16[1,128,2048]{2,1,0:T(8,128)(2,1)}, u32[]{:S(2)}) copy-start(bf16[1,128,2048]{2,1,0:T(8,128)(2,1)} %param.8) | copy-start | bytes 1572868
  2.5 20.0 %all-to-all-start = ((bf16[8,128,256]{2,1,0:T(8,128)(2,1)}), bf16[8,128,256]{2,1,0:T(8,128)(2,1)S(1)}, u32[]{:S(2)}, u32[]{:S(2)}) async-start(bf16[8,128,256]{2,1,0:T(8,128)(2,1)} %shard_map.77), calls=%async_computation | async-start | bytes 1048576 | tf_op jit(solution)/shard_map/all_to_all | solution.py:290
  8.3 1.2 %copy-start.2 = (bf16[1,128,4096]{2,1,0:T(8,128)(2,1)S(1)}, bf16[1,128,4096]{2,1,0:T(8,128)(2,1)}, u32[]{:S(2)}) copy-start(bf16[1,128,4096]{2,1,0:T(8,128)(2,1)} %param.9) | copy-start | bytes 3145732
  10.2 17.5 %collective-permute-start.7 = (bf16[128,1024]{1,0:T(8,128)(2,1)S(1)}, bf16[128,1024]{1,0:T(8,128)(2,1)S(1)}, u32[]{:S(2)}, u32[]{:S(2)}) collective-permute-start(bf16[128,1024]{1,0:T(8,128)(2,1)S(1)} %get-tuple-element.18), channel_id=1, source_target_pairs={{0,32},{32,64},{64,96},{96,0},{1,33},{33,65},{65,97},{97,1},{2,34}... | collective-permute-start | bytes 786440 | tf_op jit(solution)/shard_map/ppermute | solution.py:278
  11.7 17.5 %collective-permute-start.8 = (bf16[128,1024]{1,0:T(8,128)(2,1)S(1)}, bf16[128,1024]{1,0:T(8,128)(2,1)S(1)}, u32[]{:S(2)}, u32[]{:S(2)}) collective-permute-start(bf16[128,1024]{1,0:T(8,128)(2,1)S(1)} %get-tuple-element.19), channel_id=1, source_target_pairs={{0,64},{32,96},{64,0},{96,32},{1,65},{33,97},{65,1},{97,33},{2,66}... | collective-permute-start | bytes 786440 | tf_op jit(solution)/shard_map/ppermute | solution.py:278
  14.4 16.2 %collective-permute-start.9 = (bf16[128,1024]{1,0:T(8,128)(2,1)S(1)}, bf16[128,1024]{1,0:T(8,128)(2,1)S(1)}, u32[]{:S(2)}, u32[]{:S(2)}) collective-permute-start(bf16[128,1024]{1,0:T(8,128)(2,1)S(1)} %get-tuple-element.20), channel_id=1, source_target_pairs={{0,96},{32,0},{64,32},{96,64},{1,97},{33,1},{65,33},{97,65},{2,98}... | collective-permute-start | bytes 786440 | tf_op jit(solution)/shard_map/ppermute | solution.py:278
  15.9 6.6 %collective-permute-start = (bf16[128,1024]{1,0:T(8,128)(2,1)S(1)}, bf16[128,1024]{1,0:T(8,128)(2,1)S(1)}, u32[]{:S(2)}, u32[]{:S(2)}) collective-permute-start(bf16[128,1024]{1,0:T(8,128)(2,1)S(1)} %get-tuple-element.17.refs_5_), channel_id=1, source_target_pairs={{0,128},{128,0},{1,129},{129,1},{2,130},{130,2},{3,131},{131,3},{4... | collective-permute-start | bytes 786440 | tf_op jit(solution)/shard_map/ppermute | solution.py:278
  16.4 15.2 %copy-start.4 = (bf16[1,1024,256]{2,1,0:T(8,128)(2,1)S(1)}, bf16[1,1024,256]{2,1,0:T(8,128)(2,1)}, u32[]{:S(2)}) copy-start(bf16[1,1024,256]{2,1,0:T(8,128)(2,1)} %param.5) | copy-start | bytes 1572868
  16.4 15.2 %copy-start.5 = (bf16[1,1024,128]{2,1,0:T(8,128)(2,1)S(1)}, bf16[1,1024,128]{2,1,0:T(8,128)(2,1)}, u32[]{:S(2)}) copy-start(bf16[1,1024,128]{2,1,0:T(8,128)(2,1)} %param.6) | copy-start | bytes 786436
  22.5 2.2 %copy-start = (bf16[2,1024,1024]{2,1,0:T(8,128)(2,1)S(1)}, bf16[2,1024,1024]{2,1,0:T(8,128)(2,1)}, u32[]{:S(2)}) copy-start(bf16[2,1024,1024]{2,1,0:T(8,128)(2,1)} %shard_map.76.refs_0_.refs_1_) | copy-start | bytes 12582916
  24.7 6.9 %copy-start.1 = (bf16[2,1024,1024]{2,1,0:T(8,128)(2,1)S(1)}, bf16[2,1024,1024]{2,1,0:T(8,128)(2,1)}, u32[]{:S(2)}) copy-start(bf16[2,1024,1024]{2,1,0:T(8,128)(2,1)} %shard_map.76.refs_0_.refs_1_) | copy-start | bytes 12582916
  25.6 11.3 %collective-permute-start.6 = (bf16[128,1024]{1,0:T(8,128)(2,1)S(1)}, bf16[128,1024]{1,0:T(8,128)(2,1)S(1)}, u32[]{:S(2)}, u32[]{:S(2)}) collective-permute-start(bf16[128,1024]{1,0:T(8,128)(2,1)S(1)} %shard_map.79.refs_6_.refs_0_.refs_1_.refs_2_), channel_id=1, source_target_pairs={{0,32},{32,64},{64,96},{96,0},{1,33},{33,65},{65,97},{97,1},{2,34}... | collective-permute-start | bytes 786440 | tf_op jit(solution)/shard_map/ppermute | solution.py:278
  26.3 13.4 %collective-permute-start.5 = (bf16[128,1024]{1,0:T(8,128)(2,1)S(1)}, bf16[128,1024]{1,0:T(8,128)(2,1)S(1)}, u32[]{:S(2)}, u32[]{:S(2)}) collective-permute-start(bf16[128,1024]{1,0:T(8,128)(2,1)S(1)} %shard_map.79.refs_6_.refs_0_.refs_1_.refs_2_), channel_id=1, source_target_pairs={{0,64},{32,96},{64,0},{96,32},{1,65},{33,97},{65,1},{97,33},{2,66}... | collective-permute-start | bytes 786440 | tf_op jit(solution)/shard_map/ppermute | solution.py:278
  27.7 12.5 %collective-permute-start.4 = (bf16[128,1024]{1,0:T(8,128)(2,1)S(1)}, bf16[128,1024]{1,0:T(8,128)(2,1)S(1)}, u32[]{:S(2)}, u32[]{:S(2)}) collective-permute-start(bf16[128,1024]{1,0:T(8,128)(2,1)S(1)} %shard_map.79.refs_6_.refs_0_.refs_1_.refs_2_), channel_id=1, source_target_pairs={{0,96},{32,0},{64,32},{96,64},{1,97},{33,1},{65,33},{97,65},{2,98}... | collective-permute-start | bytes 786440 | tf_op jit(solution)/shard_map/ppermute | solution.py:278
  29.3 13.2 %collective-permute-start.10 = (bf16[128,1024]{1,0:T(8,128)(2,1)S(1)}, bf16[128,1024]{1,0:T(8,128)(2,1)S(1)}, u32[]{:S(2)}, u32[]{:S(2)}) collective-permute-start(bf16[128,1024]{1,0:T(8,128)(2,1)S(1)} %shard_map.81.refs_6_), channel_id=1, source_target_pairs={{0,128},{128,0},{1,129},{129,1},{2,130},{130,2},{3,131},{131,3},{4... | collective-permute-start | bytes 786440 | tf_op jit(solution)/shard_map/ppermute | solution.py:278
  30.7 16.4 %collective-permute-start.11 = (bf16[2,128,1024]{2,1,0:T(8,128)(2,1)S(1)}, bf16[2,128,1024]{2,1,0:T(8,128)(2,1)S(1)}, u32[]{:S(2)}, u32[]{:S(2)}) collective-permute-start(bf16[2,128,1024]{2,1,0:T(8,128)(2,1)S(1)} %shard_map.83), channel_id=1, source_target_pairs={{0,128},{128,0},{1,129},{129,1},{2,130},{130,2},{3,131},{131,3},{4... | collective-permute-start | bytes 1572872 | tf_op jit(solution)/shard_map/ppermute | solution.py:278
  31.6 1.0 %copy-start.6 = (bf16[1,1024,128]{2,1,0:T(8,128)(2,1)S(1)}, bf16[1,1024,128]{2,1,0:T(8,128)(2,1)}, u32[]{:S(2)}) copy-start(bf16[1,1024,128]{2,1,0:T(8,128)(2,1)} %param.7) | copy-start | bytes 786436
  37.0 11.5 %collective-permute-start.3 = (bf16[2,128,384]{2,1,0:T(8,128)(2,1)S(1)}, bf16[2,128,384]{2,1,0:T(8,128)(2,1)S(1)}, u32[]{:S(2)}, u32[]{:S(2)}) collective-permute-start(bf16[2,128,384]{2,1,0:T(8,128)(2,1)S(1)} %get-tuple-element.31), channel_id=1, source_target_pairs={{0,96},{32,0},{64,32},{96,64},{1,97},{33,1},{65,33},{97,65},{2,98}... | collective-permute-start | bytes 589832 | tf_op jit(solution)/shard_map/ppermute | solution.py:278
  39.6 9.3 %collective-permute-start.2 = (bf16[2,128,384]{2,1,0:T(8,128)(2,1)S(1)}, bf16[2,128,384]{2,1,0:T(8,128)(2,1)S(1)}, u32[]{:S(2)}, u32[]{:S(2)}) collective-permute-start(bf16[2,128,384]{2,1,0:T(8,128)(2,1)S(1)} %get-tuple-element.32), channel_id=1, source_target_pairs={{0,64},{32,96},{64,0},{96,32},{1,65},{33,97},{65,1},{97,33},{2,66}... | collective-permute-start | bytes 589832 | tf_op jit(solution)/shard_map/ppermute | solution.py:278
  40.2 10.9 %collective-permute-start.1 = (bf16[2,128,384]{2,1,0:T(8,128)(2,1)S(1)}, bf16[2,128,384]{2,1,0:T(8,128)(2,1)S(1)}, u32[]{:S(2)}, u32[]{:S(2)}) collective-permute-start(bf16[2,128,384]{2,1,0:T(8,128)(2,1)S(1)} %get-tuple-element.33), channel_id=1, source_target_pairs={{0,32},{32,64},{64,96},{96,0},{1,33},{33,65},{65,97},{97,1},{2,34}... | collective-permute-start | bytes 589832 | tf_op jit(solution)/shard_map/ppermute | solution.py:278
  51.1 1.9 %collective-permute-start.12 = (bf16[4,4,128,128]{3,2,1,0:T(8,128)(2,1)S(1)}, bf16[4,4,128,128]{3,2,1,0:T(8,128)(2,1)S(1)}, u32[]{:S(2)}, u32[]{:S(2)}) collective-permute-start(bf16[4,4,128,128]{3,2,1,0:T(8,128)(2,1)S(1)} %shard_map.85), channel_id=1, source_target_pairs={{0,1},{1,0},{2,3},{3,2},{4,5},{5,4},{6,7},{7,6},{8,9},{9,8},{10,11... | collective-permute-start | bytes 1572872 | tf_op jit(solution)/shard_map/ppermute | solution.py:278
  54.0 16.7 %all-to-all-start.1 = ((bf16[16,128,128]{2,1,0:T(8,128)(2,1)}), bf16[16,128,128]{2,1,0:T(8,128)(2,1)S(1)}, u32[]{:S(2)}, u32[]{:S(2)}) async-start(bf16[16,128,128]{2,1,0:T(8,128)(2,1)} %bitcast.13), calls=%async_computation.1 | async-start | bytes 1048576 | tf_op jit(solution)/shard_map/all_to_all | solution.py:333
  59.5 22.6 %collective-permute-start.13 = (bf16[4,128,384]{2,1,0:T(8,128)(2,1)S(1)}, bf16[4,128,384]{2,1,0:T(8,128)(2,1)S(1)}, u32[]{:S(2)}, u32[]{:S(2)}) collective-permute-start(bf16[4,128,384]{2,1,0:T(8,128)(2,1)S(1)} %shard_map.87), channel_id=1, source_target_pairs={{0,128},{128,0},{1,129},{129,1},{2,130},{130,2},{3,131},{131,3},{4... | collective-permute-start | bytes 1179656 | tf_op jit(solution)/shard_map/ppermute | solution.py:278
  71.3 5.6 %collective-permute-start.14 = (bf16[2,128,128]{2,1,0:T(8,128)(2,1)S(1)}, bf16[2,128,128]{2,1,0:T(8,128)(2,1)S(1)}, u32[]{:S(2)}, u32[]{:S(2)}) collective-permute-start(bf16[2,128,128]{2,1,0:T(8,128)(2,1)S(1)} %get-tuple-element.26), channel_id=1, source_target_pairs={{0,8},{8,0},{16,24},{24,16},{1,9},{9,1},{17,25},{25,17},{2,10},{10... | collective-permute-start | bytes 196616 | tf_op jit(solution)/shard_map/ppermute | solution.py:341
  76.9 7.4 %collective-permute-start.15 = (f32[128,128]{1,0:T(8,128)S(1)}, f32[128,128]{1,0:T(8,128)S(1)}, u32[]{:S(2)}, u32[]{:S(2)}) collective-permute-start(f32[128,128]{1,0:T(8,128)S(1)} %get-tuple-element.30), channel_id=1, source_target_pairs={{0,24},{8,16},{16,8},{24,0},{1,25},{9,17},{17,9},{25,1},{2,26},{10... | collective-permute-start | bytes 196616 | tf_op jit(solution)/shard_map/ppermute | solution.py:343

commit v5 on v4

--- a/solution.py
+++ b/solution.py
@@ -20,6 +20,11 @@
 
 def dot(a, b, dims):
     return lax.dot_general(a, b, dims, preferred_element_type=F32)
+
+
+def packed_row(start):
+    block = start // BLK
+    return block * (block + 1) // 2 * BLK
 
 
 def probs_kernel(q_ref, k_ref, p_ref, buf_ref, sems):
@@ -40,8 +45,9 @@
                 scores = last
             weights = jnp.exp(scores - jnp.max(scores, axis=0, keepdims=True))
             scale = 1.0 / jnp.sum(weights, axis=0, keepdims=True)
-            buf_ref[head, :stop, start:stop] = (weights * scale).astype(BF16)
-            part = (head, pl.ds(0, stop), pl.ds(start, BLK))
+            first = packed_row(start)
+            buf_ref[head, first : first + stop] = (weights * scale).astype(BF16)
+            part = (head, pl.ds(first, stop))
             copies.append(
                 pltpu.make_async_copy(buf_ref.at[part], p_ref.at[part], sems.at[len(copies)])
             )
@@ -50,18 +56,33 @@
         copy.wait()
 
 
-def value_kernel(p_ref, cot_ref, out_ref):
+def value_kernel(place_ref, p_ref, cot_ref, *refs):
+    out_refs, dv_ref = refs[:4], refs[4]
     length = cot_ref.shape[0]
     for jstart in range(0, length, BLK):
         jstop = jstart + BLK
         total = jnp.zeros((BLK, HD), F32)
         for head in range(2):
-            total += dot(
-                p_ref[head, jstart:jstop, jstart:],
-                cot_ref[jstart:, head * HD : (head + 1) * HD],
-                NN,
-            )
-        out_ref[:, jstart:jstop] = total.T.astype(BF16)
+            for start in range(jstart, length, BLK):
+                first = packed_row(start) + jstart
+                total += dot(
+                    p_ref[head, first : first + BLK],
+                    cot_ref[start : start + BLK, head * HD : (head + 1) * HD],
+                    NN,
+                )
+        dv_ref[:, jstart:jstop] = total.T.astype(BF16)
+    tok = length // 8
+    for step, ref in enumerate(out_refs):
+        x = lax.rem(place_ref[0] + step, 4)
+        for z in range(2):
+            start = pl.multiple_of((z * 4 + x) * tok, tok)
+            ref[:, z * tok : (z + 1) * tok] = dv_ref[:, pl.ds(start, tok)]
+
+
+def columns_kernel(place_ref, *refs):
+    for step, ref in enumerate(refs[:4]):
+        block = lax.rem(place_ref[0] + 4 - step, 4)
+        refs[4][pl.ds(pl.multiple_of(block * HD, HD), HD), :] = ref[...]
 
 
 def grads_kernel(place_ref, p_ref, q_ref, k_ref, v_ref, cot_ref, out_ref, kt_ref, dk_ref):
@@ -82,7 +103,8 @@
         for start in range(0, length, BLK):
             stop = start + BLK
             dprobs = dot(v_ref[:stop], cot_ref[start:stop, cols], NT)
-            probs = p_ref[head, :stop, start:stop].astype(F32)
+            first = packed_row(start)
+            probs = p_ref[head, first : first + stop].astype(F32)
             row_dot = jnp.sum(probs * dprobs, axis=0, keepdims=True) / jnp.sum(
                 probs, axis=0, keepdims=True
             )
@@ -103,13 +125,14 @@
 
 def probs_of(q, k):
     length = k.shape[0]
+    rows = packed_row(length)
     vmem = pl.BlockSpec(memory_space=pltpu.VMEM)
     return pl.pallas_call(
         probs_kernel,
         in_specs=[vmem, vmem],
         out_specs=pl.BlockSpec(memory_space=pl.ANY),
-        out_shape=pltpu.HBM((2, length, length), BF16),
-        scratch_shapes=[pltpu.VMEM((2, length, length), BF16), pltpu.SemaphoreType.DMA((8,))],
+        out_shape=pltpu.HBM((2, rows, BLK), BF16),
+        scratch_shapes=[pltpu.VMEM((2, rows, BLK), BF16), pltpu.SemaphoreType.DMA((8,))],
         compiler_params=params(),
         cost_estimate=pl.CostEstimate(
             flops=LONG, bytes_accessed=5 << 20, transcendentals=length * length
@@ -137,10 +160,11 @@
 
 
 def pack_features_kernel(place_ref, f_ref, *out_refs):
-    width = out_refs[0].shape[1]
     for step, ref in enumerate(out_refs):
-        start = pl.multiple_of(lax.rem(place_ref[0] + step, 4) * width, width)
-        ref[...] = f_ref[:, pl.ds(start, width)]
+        y = lax.rem(place_ref[4] + step, 4)
+        for z in range(4):
+            start = pl.multiple_of((z * 4 + y) * 2 * HD, 2 * HD)
+            ref[:, z * 2 * HD : (z + 1) * 2 * HD] = f_ref[:, pl.ds(start, 2 * HD)]
 
 
 def join_kernel(*refs):
@@ -154,35 +178,35 @@
 
 def near_kernel(place_ref, *refs):
     v_refs, f_refs, (part_ref, other_ref, v_ref, f_ref) = refs[:4], refs[4:8], refs[8:]
-    x, z_lo = place_ref[0], place_ref[2]
-    tok, half = f_refs[0].shape[0], other_ref.shape[1]
+    y, z_lo = place_ref[4], place_ref[2]
+    tok = f_refs[0].shape[0]
     for step, ref in enumerate(v_refs):
-        rows = pl.ds(pl.multiple_of(lax.rem(x + step, 4) * HD, HD), HD)
-        v_ref[rows, :] = ref[:, pl.ds(pl.multiple_of(z_lo * half, half), half)]
-        other_ref[rows, :] = ref[:, pl.ds(pl.multiple_of((1 - z_lo) * half, half), half)]
+        cols = pl.ds(pl.multiple_of(lax.rem(y + step, 4) * tok, tok), tok)
+        v_ref[:, cols] = ref[:, pl.ds(pl.multiple_of(z_lo * tok, tok), tok)]
+        other_ref[:, cols] = ref[:, pl.ds(pl.multiple_of((1 - z_lo) * tok, tok), tok)]
     for step, ref in enumerate(f_refs):
-        block = lax.rem(x + 4 - step, 4)
+        block = lax.rem(y + 4 - step, 4)
         f_ref[pl.ds(pl.multiple_of(block * tok, tok), tok), :] = ref[...]
-    for y in range(4):
-        cols = slice(y * 2 * HD, (y + 1) * 2 * HD)
+    for z in range(4):
+        cols = slice(z * 2 * HD, (z + 1) * 2 * HD)
         part_ref[:, cols] = dot(v_ref[...], f_ref[:, cols], NN)
 
 
 def far_kernel(place_ref, part_ref, v_ref, *refs):
-    own_ref, next_ref, rest_ref, keep_ref, send_ref, f_ref = refs
-    x, core = place_ref[0], place_ref[1]
+    own_ref, rest_ref, keep_ref, send_ref, f_ref = refs
+    y, core = place_ref[4], place_ref[1]
     tok = own_ref.shape[0]
-    for step, ref in enumerate((own_ref, next_ref, rest_ref.at[0], rest_ref.at[1])):
-        block = lax.rem(x + 4 - step, 4)
+    for step, ref in enumerate((own_ref, *(rest_ref.at[i] for i in range(3)))):
+        block = lax.rem(y + 4 - step, 4)
         f_ref[pl.ds(pl.multiple_of(block * tok, tok), tok), :] = ref[...]
-    for y in range(4):
-        cols = slice(y * 2 * HD, (y + 1) * 2 * HD)
+    for z in range(4):
+        cols = slice(z * 2 * HD, (z + 1) * 2 * HD)
         total = part_ref[:, cols] + dot(v_ref[...], f_ref[:, cols], NN)
         mine = jnp.where(core == 0, total[:, :HD], total[:, HD:])
         other = jnp.where(core == 0, total[:, HD:], total[:, :HD]).astype(BF16)
         for e in range(4):
-            keep_ref[e, y] = mine[e * HD : (e + 1) * HD]
-            send_ref[e, y] = other[e * HD : (e + 1) * HD]
+            keep_ref[e, z] = mine[e * HD : (e + 1) * HD]
+            send_ref[e, z] = other[e * HD : (e + 1) * HD]
 
 
 def add_kernel(keep_ref, got_ref, out_ref):
@@ -194,9 +218,9 @@
     beside = z_hi + 1 - 2 * lax.rem(z_hi, 2)
 
     def summed(block):
-        total = got_ref[block, 0].astype(F32)
-        for y in range(1, 4):
-            total += got_ref[block, y].astype(F32)
+        total = got_ref[0, block].astype(F32)
+        for x in range(1, 4):
+            total += got_ref[x, block].astype(F32)
         return total
 
     for index in range(2):
@@ -282,7 +306,7 @@
     q, k, v = queries[0], key_heads[0], value_heads[0]
     length = q.shape[0]
     seq = ("z_lo", "x")
-    place = jnp.stack([lax.axis_index(a) for a in ("x", "core", "z_lo", "z_hi")]).astype(jnp.int32)
+    place = jnp.stack([lax.axis_index(a) for a in ("x", "core", "z_lo", "z_hi", "y")]).astype(jnp.int32)
     tok = grad_out.shape[1]
     width = features.shape[2] // 4
 
@@ -290,21 +314,34 @@
     cot = lax.all_to_all(cot_parts, seq, 0, 0).reshape(length, 2 * HD)
 
     parts = call(
-        pack_features_kernel, [shape_of(tok, width)] * 4, features[0], place=place, nbytes=2 << 20
-    )
-    near = [shift(parts[step], "x", 4, step) for step in range(1, 4)]
+        pack_features_kernel,
+        [shape_of(tok, width)] * 4,
+        features[0],
+        place=place,
+        after=[cot_parts],
+        nbytes=2 << 20,
+    )
+    near = [shift(parts[step], "y", 4, step) for step in range(1, 4)]
     far = shift(parts[0], "z_lo", 2, 1)
 
     probs = probs_of(q, k)
-    dv = call(
-        value_kernel, shape_of(HD, length), probs, cot, after=[far], flops=1 << 29, nbytes=5 << 20
-    )
-    first = call(gate_kernel, [], after=[dv], behind=near[:1])
-    rest = call(join_kernel, shape_of(2, tok, width), *near[1:], after=[dv], nbytes=2 << 20)
-    near = [parts[0], first, *near[1:]]
-    far = [far, shift(first, "z_lo", 2, 1), shift(rest, "z_lo", 2, 1)]
-
-    values = [dv] + [shift(dv, "x", 4, -step) for step in range(1, 4)]
+    pieces = call(
+        value_kernel,
+        [shape_of(HD, 2 * tok)] * 4,
+        probs, cot,
+        place=place,
+        flops=1 << 29,
+        nbytes=5 << 20,
+        scratch=[pltpu.VMEM((HD, length), BF16)],
+    )
+    dv = pieces[0]
+    pieces = [dv] + [shift(pieces[step], "x", 4, step) for step in range(1, 4)]
+    columns = call(columns_kernel, shape_of(4 * HD, 2 * tok), *pieces, place=place)
+    rest = call(join_kernel, shape_of(3, tok, width), *near, after=[dv, far], nbytes=2 << 20)
+    near = [parts[0], *near]
+    far = [far, shift(rest, "z_lo", 2, 1)]
+
+    values = [columns] + [shift(columns, "y", 4, -step) for step in range(1, 4)]
 
     moved = grads_of(place, probs, q, k, v, cot, dv)
     half = length // 2
@@ -330,11 +367,11 @@
     got_x = [shift(moved[step], "x", 4, step) for step in range(1, 4)]
     send = call(gate_kernel, [], after=got_x, behind=[send])
     both = call(add_kernel, shape_of(4, 4, HD, HD), keep, shift(send, "core", 2, 1))
-    over_y = lax.all_to_all(both.reshape(16, HD, HD), ("x", "y"), 0, 0).reshape(4, 4, HD, HD)
+    over_x = lax.all_to_all(both, "x", 0, 0)
     keep, send = call(
         sum_kernel,
         [shape_of(2, HD, HD, dtype=F32), shape_of(2, HD, HD)],
-        over_y,
+        over_x,
         place=place,
         flops=LONG,
     )

time: 85.5 us -> 83.6 us (0.978)
  the two profiles are of different devices: /device:TPU:32 before, /device:TPU:8 now
where the time goes in v5:
time: 83.6 us; the launch traced here: 83.3 us
  starting transfers between devices  38 us (45%)
  waiting for transfers between devices  22.2 us (27%)
  Pallas kernels  19.2 us (23%)
  local copies, waits for them, and re-layouts  3.02 us (4%)
    ppermute x16, starting transfers between devices, shift(): lax.ppermute(array, axis, [(i, (i + by) % size) for i in range(size)])  20.3 us
    pallas_call x15, Pallas kernels, call(): pl.pallas_call(body, out_shape=shapes, in_specs=specs, out_specs=out_spec...  15.2 us
    ppermute x16, waiting for transfers between devices, shift(): lax.ppermute(array, axis, [(i, (i + by) % size) for i in range(size)])  9.82 us
    all_to_all x1, waiting for transfers between devices, on_device(): over_x = lax.all_to_all(both, 'x', 0, 0)  9.09 us
    all_to_all x1, starting transfers between devices, on_device(): cot = lax.all_to_all(cot_parts, seq, 0, 0).reshape(length, 2 * HD)  5.65 us
    ppermute x1, starting transfers between devices, on_device(): got = lax.ppermute(send, 'z_hi', [(z, 3 - z) for z in range(4)])  4.77 us
    pallas_call x1, Pallas kernels, probs_of(): pl.pallas_call(probs_kernel, in_specs=[vmem, vmem], out_specs=pl.BlockSpe...  4.08 us
    all_to_all x1, starting transfers between devices, on_device(): over_x = lax.all_to_all(both, 'x', 0, 0)  3.9 us
  transfers between devices with their start and end apart: 20, of which 9 were waited for; matrix products, arithmetic and copies ran while one was open for 0% of the time, Pallas kernels for 20%

profile of v5, /device:TPU:8, one launch (start us, length us, event | category | flops | bytes accessed | tf_op | source)
XLA Modules:
  0.0 83.3 jit_solution(3639648358871299596)
XLA Ops:
  0.7 1.1 %copy-done.3 = bf16[1,128,2048]{2,1,0:T(8,128)(2,1)S(1)} copy-done((bf16[1,128,2048]{2,1,0:T(8,128)(2,1)S(1)}, bf16[1,128,2048]{2,1,0:T(8,128)(2,1)}, u32[]{:S(2)}) %copy-start.3) | copy-done | bytes 524312
  2.6 5.7 %all-to-all-start = ((bf16[8,128,256]{2,1,0:T(8,128)(2,1)}), bf16[8,128,256]{2,1,0:T(8,128)(2,1)S(1)}, u32[]{:S(2)}, u32[]{:S(2)}) async-start(bf16[8,128,256]{2,1,0:T(8,128)(2,1)} %shard_map.77.refs_2_), calls=%async_computation | async-start | bytes 1048576 | tf_op jit(solution)/shard_map/all_to_all | solution.py:314
  9.0 1.7 %collective-permute-start.9 = (bf16[128,1024]{1,0:T(8,128)(2,1)S(1)}, bf16[128,1024]{1,0:T(8,128)(2,1)S(1)}, u32[]{:S(2)}, u32[]{:S(2)}) collective-permute-start(bf16[128,1024]{1,0:T(8,128)(2,1)S(1)} %get-tuple-element.26), channel_id=1, source_target_pairs={{0,2},{2,4},{4,6},{6,0},{1,3},{3,5},{5,7},{7,1},{8,10},{10,12},{12... | collective-permute-start | bytes 786440 | tf_op jit(solution)/shard_map/ppermute | solution.py:302
  10.7 0.9 %collective-permute-start.10 = (bf16[128,1024]{1,0:T(8,128)(2,1)S(1)}, bf16[128,1024]{1,0:T(8,128)(2,1)S(1)}, u32[]{:S(2)}, u32[]{:S(2)}) collective-permute-start(bf16[128,1024]{1,0:T(8,128)(2,1)S(1)} %get-tuple-element.27), channel_id=1, source_target_pairs={{0,4},{2,6},{4,0},{6,2},{1,5},{3,7},{5,1},{7,3},{8,12},{10,14},{12... | collective-permute-start | bytes 786440 | tf_op jit(solution)/shard_map/ppermute | solution.py:302
  11.6 2.4 %collective-permute-start.11 = (bf16[128,1024]{1,0:T(8,128)(2,1)S(1)}, bf16[128,1024]{1,0:T(8,128)(2,1)S(1)}, u32[]{:S(2)}, u32[]{:S(2)}) collective-permute-start(bf16[128,1024]{1,0:T(8,128)(2,1)S(1)} %get-tuple-element.28), channel_id=1, source_target_pairs={{0,6},{2,0},{4,2},{6,4},{1,7},{3,1},{5,3},{7,5},{8,14},{10,8},{12,... | collective-permute-start | bytes 786440 | tf_op jit(solution)/shard_map/ppermute | solution.py:302
  14.0 2.0 %collective-permute-start.12 = (bf16[128,1024]{1,0:T(8,128)(2,1)S(1)}, bf16[128,1024]{1,0:T(8,128)(2,1)S(1)}, u32[]{:S(2)}, u32[]{:S(2)}) collective-permute-start(bf16[128,1024]{1,0:T(8,128)(2,1)S(1)} %get-tuple-element.25.refs_5_), channel_id=1, source_target_pairs={{0,128},{128,0},{1,129},{129,1},{2,130},{130,2},{3,131},{131,3},{4... | collective-permute-start | bytes 786440 | tf_op jit(solution)/shard_map/ppermute | solution.py:302
  16.1 4.1 %shard_map.76.refs_1_ = bf16[2,2560,256]{2,1,0:T(8,128)(2,1)} custom-call(bf16[1024,256]{1,0:T(8,128)(2,1)} %bitcast.23, bf16[1024,128]{1,0:T(8,128)(2,1)} %bitcast.25), custom_call_target="tpu_custom_call" | custom-call | flops 34359738368 | bytes 5242880 | tf_op jit(solution)/shard_map/pallas_call | solution.py:130
  20.2 1.7 %copy-done = bf16[2,2560,256]{2,1,0:T(8,128)(2,1)S(1)} copy-done((bf16[2,2560,256]{2,1,0:T(8,128)(2,1)S(1)}, bf16[2,2560,256]{2,1,0:T(8,128)(2,1)}, u32[]{:S(2)}) %copy-start) | copy-done | bytes 2621464
  21.9 1.5 %shard_map.78 = (bf16[128,256]{1,0:T(8,128)(2,1)S(1)}, bf16[128,256]{1,0:T(8,128)(2,1)S(1)}, bf16[128,256]{1,0:T(8,128)(2,1)S(1)}, bf16[128,256]{1,0:T(8,128)(2,1)S(1)}) custom-call(s32[5]{0:T(128)S(1)} %stack.23.refs_0_, bf16[2,2560,256]{2,1,0:T(8,128)(2,1)S(1)} %copy-done, bf16[1024,256]{1,0:T(8,128)(2,1)S(1)} %bitcast.19), custom_call_target="tpu_custom_call" | custom-call | flops 536870912 | bytes 5242880 | tf_op jit(solution)/shard_map/pallas_call | solution.py:284
  23.4 1.5 %collective-permute-start.3 = (bf16[128,256]{1,0:T(8,128)(2,1)S(1)}, bf16[128,256]{1,0:T(8,128)(2,1)S(1)}, u32[]{:S(2)}, u32[]{:S(2)}) collective-permute-start(bf16[128,256]{1,0:T(8,128)(2,1)S(1)} %get-tuple-element.22), channel_id=1, source_target_pairs={{0,32},{32,64},{64,96},{96,0},{1,33},{33,65},{65,97},{97,1},{2,34}... | collective-permute-start | bytes 196616 | tf_op jit(solution)/shard_map/ppermute | solution.py:302
  25.0 2.7 %collective-permute-start.4 = (bf16[128,256]{1,0:T(8,128)(2,1)S(1)}, bf16[128,256]{1,0:T(8,128)(2,1)S(1)}, u32[]{:S(2)}, u32[]{:S(2)}) collective-permute-start(bf16[128,256]{1,0:T(8,128)(2,1)S(1)} %get-tuple-element.23), channel_id=1, source_target_pairs={{0,64},{32,96},{64,0},{96,32},{1,65},{33,97},{65,1},{97,33},{2,66}... | collective-permute-start | bytes 196616 | tf_op jit(solution)/shard_map/ppermute | solution.py:302
  27.7 1.5 %collective-permute-start.5 = (bf16[128,256]{1,0:T(8,128)(2,1)S(1)}, bf16[128,256]{1,0:T(8,128)(2,1)S(1)}, u32[]{:S(2)}, u32[]{:S(2)}) collective-permute-start(bf16[128,256]{1,0:T(8,128)(2,1)S(1)} %get-tuple-element.24), channel_id=1, source_target_pairs={{0,96},{32,0},{64,32},{96,64},{1,97},{33,1},{65,33},{97,65},{2,98}... | collective-permute-start | bytes 196616 | tf_op jit(solution)/shard_map/ppermute | solution.py:302
  29.8 0.9 %collective-permute-done.4.refs_3_ = bf16[128,256]{1,0:T(8,128)(2,1)S(1)} collective-permute-done((bf16[128,256]{1,0:T(8,128)(2,1)S(1)}, bf16[128,256]{1,0:T(8,128)(2,1)S(1)}, u32[]{:S(2)}, u32[]{:S(2)}) %collective-permute-start.4) | collective-permute-done | bytes 65568 | tf_op jit(solution)/shard_map/ppermute | solution.py:302
  30.7 1.2 %collective-permute-done.5.refs_4_ = bf16[128,256]{1,0:T(8,128)(2,1)S(1)} collective-permute-done((bf16[128,256]{1,0:T(8,128)(2,1)S(1)}, bf16[128,256]{1,0:T(8,128)(2,1)S(1)}, u32[]{:S(2)}, u32[]{:S(2)}) %collective-permute-start.5) | collective-permute-done | bytes 65568 | tf_op jit(solution)/shard_map/ppermute | solution.py:302
  32.5 1.4 %collective-permute-start.6 = (bf16[512,256]{1,0:T(8,128)(2,1)S(1)}, bf16[512,256]{1,0:T(8,128)(2,1)S(1)}, u32[]{:S(2)}, u32[]{:S(2)}) collective-permute-start(bf16[512,256]{1,0:T(8,128)(2,1)S(1)} %shard_map.80.refs_1_), channel_id=1, source_target_pairs={{0,6},{2,0},{4,2},{6,4},{1,7},{3,1},{5,3},{7,5},{8,14},{10,8},{12,... | collective-permute-start | bytes 786440 | tf_op jit(solution)/shard_map/ppermute | solution.py:302
  33.9 1.6 %collective-permute-start.8 = (bf16[512,256]{1,0:T(8,128)(2,1)S(1)}, bf16[512,256]{1,0:T(8,128)(2,1)S(1)}, u32[]{:S(2)}, u32[]{:S(2)}) collective-permute-start(bf16[512,256]{1,0:T(8,128)(2,1)S(1)} %shard_map.80.refs_1_), channel_id=1, source_target_pairs={{0,2},{2,4},{4,6},{6,0},{1,3},{3,5},{5,7},{7,1},{8,10},{10,12},{12... | collective-permute-start | bytes 786440 | tf_op jit(solution)/shard_map/ppermute | solution.py:302
  35.5 4.3 %shard_map.79.refs_9_.refs_1_ = bf16[4,2,128,384]{3,2,1,0:T(8,128)(2,1)S(1)} custom-call(s32[5]{0:T(128)S(1)} %stack.23.refs_0_, bf16[2,2560,256]{2,1,0:T(8,128)(2,1)S(1)} %copy-done.1, bf16[1024,256]{1,0:T(8,128)(2,1)S(1)} %bitcast.24, bf16[1024,128]{1,0:T(8,128)(2,1)S(1)} %bitcast.26, bf16[1024,128]{1,0:T(8,128)(2,1)S(1)} %bitcast.27, ...), custom_call_target="tpu_custom_call" | custom-call | flops 34359738368 | bytes 6291456 | tf_op jit(solution)/shard_map/pallas_call | solution.py:284
  39.9 1.0 %collective-permute-start = (bf16[2,128,384]{2,1,0:T(8,128)(2,1)S(1)}, bf16[2,128,384]{2,1,0:T(8,128)(2,1)S(1)}, u32[]{:S(2)}, u32[]{:S(2)}) collective-permute-start(bf16[2,128,384]{2,1,0:T(8,128)(2,1)S(1)} %get-tuple-element.41), channel_id=1, source_target_pairs={{0,32},{32,64},{64,96},{96,0},{1,33},{33,65},{65,97},{97,1},{2,34}... | collective-permute-start | bytes 589832 | tf_op jit(solution)/shard_map/ppermute | solution.py:302
  40.9 2.5 %collective-permute-done.6.refs_2_ = bf16[512,256]{1,0:T(8,128)(2,1)S(1)} collective-permute-done((bf16[512,256]{1,0:T(8,128)(2,1)S(1)}, bf16[512,256]{1,0:T(8,128)(2,1)S(1)}, u32[]{:S(2)}, u32[]{:S(2)}) %collective-permute-start.6) | collective-permute-done | bytes 262176 | tf_op jit(solution)/shard_map/ppermute | solution.py:302
  43.4 1.9 %collective-permute-start.1 = (bf16[2,128,384]{2,1,0:T(8,128)(2,1)S(1)}, bf16[2,128,384]{2,1,0:T(8,128)(2,1)S(1)}, u32[]{:S(2)}, u32[]{:S(2)}) collective-permute-start(bf16[2,128,384]{2,1,0:T(8,128)(2,1)S(1)} %get-tuple-element.40), channel_id=1, source_target_pairs={{0,64},{32,96},{64,0},{96,32},{1,65},{33,97},{65,1},{97,33},{2,66}... | collective-permute-start | bytes 589832 | tf_op jit(solution)/shard_map/ppermute | solution.py:302
  45.3 1.0 %collective-permute-start.2 = (bf16[2,128,384]{2,1,0:T(8,128)(2,1)S(1)}, bf16[2,128,384]{2,1,0:T(8,128)(2,1)S(1)}, u32[]{:S(2)}, u32[]{:S(2)}) collective-permute-start(bf16[2,128,384]{2,1,0:T(8,128)(2,1)S(1)} %get-tuple-element.39), channel_id=1, source_target_pairs={{0,96},{32,0},{64,32},{96,64},{1,97},{33,1},{65,33},{97,65},{2,98}... | collective-permute-start | bytes 589832 | tf_op jit(solution)/shard_map/ppermute | solution.py:302
  46.3 1.5 %shard_map.82 = (f32[512,1024]{1,0:T(8,128)S(1)}, bf16[512,512]{1,0:T(8,128)(2,1)S(1)}) custom-call(s32[5]{0:T(128)S(1)} %stack.23.refs_0_, bf16[512,256]{1,0:T(8,128)(2,1)S(1)} %shard_map.80.refs_1_, bf16[512,256]{1,0:T(8,128)(2,1)S(1)} %collective-permute-done.6.refs_2_, bf16[512,256]{1,0:T(8,128)(2,1)S(1)} %collective-permute-done.7.refs_3_, ...), custom_call_target="tpu_custom_call" | custom-call | tf_op jit(solution)/shard_map/pallas_call | solution.py:284
  47.8 1.3 %shard_map.84 = (f32[4,4,128,128]{3,2,1,0:T(8,128)S(1)}, bf16[4,4,128,128]{3,2,1,0:T(8,128)(2,1)S(1)}) custom-call(s32[5]{0:T(128)S(1)} %stack.23.refs_0_, f32[512,1024]{1,0:T(8,128)S(1)} %get-tuple-element.29.refs_1_, bf16[512,512]{1,0:T(8,128)(2,1)S(1)} %get-tuple-element.30.refs_2_, bf16[128,1024]{1,0:T(8,128)(2,1)S(1)} %collective-permute-done.12.refs_4_.refs_3_, ...), custom_call_target="tpu_custom_call" | custom-call | flops 34359738368 | bytes 5242880 | tf_op jit(solution)/shard_map/pallas_call | solution.py:284
  49.1 1.4 %collective-permute-done.1.refs_1_.refs_3_ = bf16[2,128,384]{2,1,0:T(8,128)(2,1)S(1)} collective-permute-done((bf16[2,128,384]{2,1,0:T(8,128)(2,1)S(1)}, bf16[2,128,384]{2,1,0:T(8,128)(2,1)S(1)}, u32[]{:S(2)}, u32[]{:S(2)}) %collective-permute-start.1) | collective-permute-done | bytes 196640 | tf_op jit(solution)/shard_map/ppermute | solution.py:302
  50.5 1.9 %collective-permute-done.2.refs_2_.refs_4_ = bf16[2,128,384]{2,1,0:T(8,128)(2,1)S(1)} collective-permute-done((bf16[2,128,384]{2,1,0:T(8,128)(2,1)S(1)}, bf16[2,128,384]{2,1,0:T(8,128)(2,1)S(1)}, u32[]{:S(2)}, u32[]{:S(2)}) %collective-permute-start.2) | collective-permute-done | bytes 196640 | tf_op jit(solution)/shard_map/ppermute | solution.py:302
  52.4 1.9 %collective-permute-done.14.refs_1_ = bf16[4,4,128,128]{3,2,1,0:T(8,128)(2,1)S(1)} collective-permute-done((bf16[4,4,128,128]{3,2,1,0:T(8,128)(2,1)S(1)}, bf16[4,4,128,128]{3,2,1,0:T(8,128)(2,1)S(1)}, u32[]{:S(2)}, u32[]{:S(2)}) %collective-permute-start.14) | collective-permute-done | bytes 524320 | tf_op jit(solution)/shard_map/ppermute | solution.py:302
  55.3 3.9 %all-to-all-start.1 = ((bf16[4,4,128,128]{3,2,1,0:T(8,128)(2,1)}), bf16[4,4,128,128]{3,2,1,0:T(8,128)(2,1)S(1)}, u32[]{:S(2)}, u32[]{:S(2)}) async-start(bf16[4,4,128,128]{3,2,1,0:T(8,128)(2,1)} %shard_map.86.refs_5_), calls=%async_computation.1 | async-start | bytes 1048576 | tf_op jit(solution)/shard_map/all_to_all | solution.py:370
  59.9 9.1 %all-to-all-done.1.refs_1_ = bf16[4,4,128,128]{3,2,1,0:T(8,128)(2,1)S(1)} async-done(((bf16[4,4,128,128]{3,2,1,0:T(8,128)(2,1)}), bf16[4,4,128,128]{3,2,1,0:T(8,128)(2,1)S(1)}, u32[]{:S(2)}, u32[]{:S(2)}) %all-to-all-start.1) | async-done | bytes 524320 | tf_op jit(solution)/shard_map/all_to_all | solution.py:370
  69.6 3.4 %collective-permute-start.16 = (bf16[2,128,128]{2,1,0:T(8,128)(2,1)S(1)}, bf16[2,128,128]{2,1,0:T(8,128)(2,1)S(1)}, u32[]{:S(2)}, u32[]{:S(2)}) collective-permute-start(bf16[2,128,128]{2,1,0:T(8,128)(2,1)S(1)} %get-tuple-element.34), channel_id=1, source_target_pairs={{0,8},{8,0},{16,24},{24,16},{1,9},{9,1},{17,25},{25,17},{2,10},{10... | collective-permute-start | bytes 196616 | tf_op jit(solution)/shard_map/ppermute | solution.py:378
  72.9 2.6 %collective-permute-done.16.refs_1_ = bf16[2,128,128]{2,1,0:T(8,128)(2,1)S(1)} collective-permute-done((bf16[2,128,128]{2,1,0:T(8,128)(2,1)S(1)}, bf16[2,128,128]{2,1,0:T(8,128)(2,1)S(1)}, u32[]{:S(2)}, u32[]{:S(2)}) %collective-permute-start.16) | collective-permute-done | bytes 65568 | tf_op jit(solution)/shard_map/ppermute | solution.py:378
  75.5 4.8 %collective-permute-start.17 = (f32[128,128]{1,0:T(8,128)S(1)}, f32[128,128]{1,0:T(8,128)S(1)}, u32[]{:S(2)}, u32[]{:S(2)}) collective-permute-start(f32[128,128]{1,0:T(8,128)S(1)} %get-tuple-element.38), channel_id=1, source_target_pairs={{0,24},{8,16},{16,8},{24,0},{1,25},{9,17},{17,9},{25,1},{2,26},{10... | collective-permute-start | bytes 196616 | tf_op jit(solution)/shard_map/ppermute | solution.py:380
  80.3 1.5 %shard_map.90 = (bf16[128,2048]{1,0:T(8,128)(2,1)}, bf16[128,1024]{1,0:T(8,128)(2,1)}) custom-call(s32[5]{0:T(128)S(1)} %stack.23.refs_0_, bf16[4,2,128,384]{3,2,1,0:T(8,128)(2,1)S(1)} %shard_map.79.refs_9_.refs_1_, bf16[2,128,384]{2,1,0:T(8,128)(2,1)S(1)} %collective-permute-done.refs_0_.refs_2_, ...), custom_call_target="tpu_custom_call" | custom-call | bytes 1048576 | tf_op jit(solution)/shard_map/pallas_call | solution.py:284
  (40 shorter events, 6.6 us)
Async XLA Ops:
  0.6 7.7 %copy-start.2 = (bf16[1,128,4096]{2,1,0:T(8,128)(2,1)S(1)}, bf16[1,128,4096]{2,1,0:T(8,128)(2,1)}, u32[]{:S(2)}) copy-start(bf16[1,128,4096]{2,1,0:T(8,128)(2,1)} %param.9) | copy-start | bytes 3145732
  0.6 1.1 %copy-start.3 = (bf16[1,128,2048]{2,1,0:T(8,128)(2,1)S(1)}, bf16[1,128,2048]{2,1,0:T(8,128)(2,1)}, u32[]{:S(2)}) copy-start(bf16[1,128,2048]{2,1,0:T(8,128)(2,1)} %param.8) | copy-start | bytes 1572868
  2.6 17.6 %all-to-all-start = ((bf16[8,128,256]{2,1,0:T(8,128)(2,1)}), bf16[8,128,256]{2,1,0:T(8,128)(2,1)S(1)}, u32[]{:S(2)}, u32[]{:S(2)}) async-start(bf16[8,128,256]{2,1,0:T(8,128)(2,1)} %shard_map.77.refs_2_), calls=%async_computation | async-start | bytes 1048576 | tf_op jit(solution)/shard_map/all_to_all | solution.py:314
  9.0 15.9 %collective-permute-start.9 = (bf16[128,1024]{1,0:T(8,128)(2,1)S(1)}, bf16[128,1024]{1,0:T(8,128)(2,1)S(1)}, u32[]{:S(2)}, u32[]{:S(2)}) collective-permute-start(bf16[128,1024]{1,0:T(8,128)(2,1)S(1)} %get-tuple-element.26), channel_id=1, source_target_pairs={{0,2},{2,4},{4,6},{6,0},{1,3},{3,5},{5,7},{7,1},{8,10},{10,12},{12... | collective-permute-start | bytes 786440 | tf_op jit(solution)/shard_map/ppermute | solution.py:302
  10.7 17.0 %collective-permute-start.10 = (bf16[128,1024]{1,0:T(8,128)(2,1)S(1)}, bf16[128,1024]{1,0:T(8,128)(2,1)S(1)}, u32[]{:S(2)}, u32[]{:S(2)}) collective-permute-start(bf16[128,1024]{1,0:T(8,128)(2,1)S(1)} %get-tuple-element.27), channel_id=1, source_target_pairs={{0,4},{2,6},{4,0},{6,2},{1,5},{3,7},{5,1},{7,3},{8,12},{10,14},{12... | collective-permute-start | bytes 786440 | tf_op jit(solution)/shard_map/ppermute | solution.py:302
  11.6 17.5 %collective-permute-start.11 = (bf16[128,1024]{1,0:T(8,128)(2,1)S(1)}, bf16[128,1024]{1,0:T(8,128)(2,1)S(1)}, u32[]{:S(2)}, u32[]{:S(2)}) collective-permute-start(bf16[128,1024]{1,0:T(8,128)(2,1)S(1)} %get-tuple-element.28), channel_id=1, source_target_pairs={{0,6},{2,0},{4,2},{6,4},{1,7},{3,1},{5,3},{7,5},{8,14},{10,8},{12,... | collective-permute-start | bytes 786440 | tf_op jit(solution)/shard_map/ppermute | solution.py:302
  14.0 15.1 %collective-permute-start.12 = (bf16[128,1024]{1,0:T(8,128)(2,1)S(1)}, bf16[128,1024]{1,0:T(8,128)(2,1)S(1)}, u32[]{:S(2)}, u32[]{:S(2)}) collective-permute-start(bf16[128,1024]{1,0:T(8,128)(2,1)S(1)} %get-tuple-element.25.refs_5_), channel_id=1, source_target_pairs={{0,128},{128,0},{1,129},{129,1},{2,130},{130,2},{3,131},{131,3},{4... | collective-permute-start | bytes 786440 | tf_op jit(solution)/shard_map/ppermute | solution.py:302
  20.2 1.7 %copy-start = (bf16[2,2560,256]{2,1,0:T(8,128)(2,1)S(1)}, bf16[2,2560,256]{2,1,0:T(8,128)(2,1)}, u32[]{:S(2)}) copy-start(bf16[2,2560,256]{2,1,0:T(8,128)(2,1)} %shard_map.76.refs_1_) | copy-start | bytes 7864324
  21.9 13.6 %copy-start.1 = (bf16[2,2560,256]{2,1,0:T(8,128)(2,1)S(1)}, bf16[2,2560,256]{2,1,0:T(8,128)(2,1)}, u32[]{:S(2)}) copy-start(bf16[2,2560,256]{2,1,0:T(8,128)(2,1)} %shard_map.76.refs_1_) | copy-start | bytes 7864324
  21.9 13.6 %copy-start.4 = (bf16[1,1024,256]{2,1,0:T(8,128)(2,1)S(1)}, bf16[1,1024,256]{2,1,0:T(8,128)(2,1)}, u32[]{:S(2)}) copy-start(bf16[1,1024,256]{2,1,0:T(8,128)(2,1)} %param.5) | copy-start | bytes 1572868
  21.9 13.6 %copy-start.5 = (bf16[1,1024,128]{2,1,0:T(8,128)(2,1)S(1)}, bf16[1,1024,128]{2,1,0:T(8,128)(2,1)}, u32[]{:S(2)}) copy-start(bf16[1,1024,128]{2,1,0:T(8,128)(2,1)} %param.6) | copy-start | bytes 786436
  21.9 13.6 %copy-start.6 = (bf16[1,1024,128]{2,1,0:T(8,128)(2,1)S(1)}, bf16[1,1024,128]{2,1,0:T(8,128)(2,1)}, u32[]{:S(2)}) copy-start(bf16[1,1024,128]{2,1,0:T(8,128)(2,1)} %param.7) | copy-start | bytes 786436
  23.4 6.4 %collective-permute-start.3 = (bf16[128,256]{1,0:T(8,128)(2,1)S(1)}, bf16[128,256]{1,0:T(8,128)(2,1)S(1)}, u32[]{:S(2)}, u32[]{:S(2)}) collective-permute-start(bf16[128,256]{1,0:T(8,128)(2,1)S(1)} %get-tuple-element.22), channel_id=1, source_target_pairs={{0,32},{32,64},{64,96},{96,0},{1,33},{33,65},{65,97},{97,1},{2,34}... | collective-permute-start | bytes 196616 | tf_op jit(solution)/shard_map/ppermute | solution.py:302
  25.0 5.8 %collective-permute-start.4 = (bf16[128,256]{1,0:T(8,128)(2,1)S(1)}, bf16[128,256]{1,0:T(8,128)(2,1)S(1)}, u32[]{:S(2)}, u32[]{:S(2)}) collective-permute-start(bf16[128,256]{1,0:T(8,128)(2,1)S(1)} %get-tuple-element.23), channel_id=1, source_target_pairs={{0,64},{32,96},{64,0},{96,32},{1,65},{33,97},{65,1},{97,33},{2,66}... | collective-permute-start | bytes 196616 | tf_op jit(solution)/shard_map/ppermute | solution.py:302
  27.7 4.3 %collective-permute-start.5 = (bf16[128,256]{1,0:T(8,128)(2,1)S(1)}, bf16[128,256]{1,0:T(8,128)(2,1)S(1)}, u32[]{:S(2)}, u32[]{:S(2)}) collective-permute-start(bf16[128,256]{1,0:T(8,128)(2,1)S(1)} %get-tuple-element.24), channel_id=1, source_target_pairs={{0,96},{32,0},{64,32},{96,64},{1,97},{33,1},{65,33},{97,65},{2,98}... | collective-permute-start | bytes 196616 | tf_op jit(solution)/shard_map/ppermute | solution.py:302
  29.2 18.6 %collective-permute-start.13 = (bf16[3,128,1024]{2,1,0:T(8,128)(2,1)S(1)}, bf16[3,128,1024]{2,1,0:T(8,128)(2,1)S(1)}, u32[]{:S(2)}, u32[]{:S(2)}) collective-permute-start(bf16[3,128,1024]{2,1,0:T(8,128)(2,1)S(1)} %shard_map.83), channel_id=1, source_target_pairs={{0,128},{128,0},{1,129},{129,1},{2,130},{130,2},{3,131},{131,3},{4... | collective-permute-start | bytes 2359304 | tf_op jit(solution)/shard_map/ppermute | solution.py:302
  32.5 10.9 %collective-permute-start.6 = (bf16[512,256]{1,0:T(8,128)(2,1)S(1)}, bf16[512,256]{1,0:T(8,128)(2,1)S(1)}, u32[]{:S(2)}, u32[]{:S(2)}) collective-permute-start(bf16[512,256]{1,0:T(8,128)(2,1)S(1)} %shard_map.80.refs_1_), channel_id=1, source_target_pairs={{0,6},{2,0},{4,2},{6,4},{1,7},{3,1},{5,3},{7,5},{8,14},{10,8},{12,... | collective-permute-start | bytes 786440 | tf_op jit(solution)/shard_map/ppermute | solution.py:302
  33.9 11.4 %collective-permute-start.7 = (bf16[512,256]{1,0:T(8,128)(2,1)S(1)}, bf16[512,256]{1,0:T(8,128)(2,1)S(1)}, u32[]{:S(2)}, u32[]{:S(2)}) collective-permute-start(bf16[512,256]{1,0:T(8,128)(2,1)S(1)} %shard_map.80.refs_1_), channel_id=1, source_target_pairs={{0,4},{2,6},{4,0},{6,2},{1,5},{3,7},{5,1},{7,3},{8,12},{10,14},{12... | collective-permute-start | bytes 786440 | tf_op jit(solution)/shard_map/ppermute | solution.py:302
  33.9 12.4 %collective-permute-start.8 = (bf16[512,256]{1,0:T(8,128)(2,1)S(1)}, bf16[512,256]{1,0:T(8,128)(2,1)S(1)}, u32[]{:S(2)}, u32[]{:S(2)}) collective-permute-start(bf16[512,256]{1,0:T(8,128)(2,1)S(1)} %shard_map.80.refs_1_), channel_id=1, source_target_pairs={{0,2},{2,4},{4,6},{6,0},{1,3},{3,5},{5,7},{7,1},{8,10},{10,12},{12... | collective-permute-start | bytes 786440 | tf_op jit(solution)/shard_map/ppermute | solution.py:302
  39.9 9.3 %collective-permute-start = (bf16[2,128,384]{2,1,0:T(8,128)(2,1)S(1)}, bf16[2,128,384]{2,1,0:T(8,128)(2,1)S(1)}, u32[]{:S(2)}, u32[]{:S(2)}) collective-permute-start(bf16[2,128,384]{2,1,0:T(8,128)(2,1)S(1)} %get-tuple-element.41), channel_id=1, source_target_pairs={{0,32},{32,64},{64,96},{96,0},{1,33},{33,65},{65,97},{97,1},{2,34}... | collective-permute-start | bytes 589832 | tf_op jit(solution)/shard_map/ppermute | solution.py:302
  43.4 7.2 %collective-permute-start.1 = (bf16[2,128,384]{2,1,0:T(8,128)(2,1)S(1)}, bf16[2,128,384]{2,1,0:T(8,128)(2,1)S(1)}, u32[]{:S(2)}, u32[]{:S(2)}) collective-permute-start(bf16[2,128,384]{2,1,0:T(8,128)(2,1)S(1)} %get-tuple-element.40), channel_id=1, source_target_pairs={{0,64},{32,96},{64,0},{96,32},{1,65},{33,97},{65,1},{97,33},{2,66}... | collective-permute-start | bytes 589832 | tf_op jit(solution)/shard_map/ppermute | solution.py:302
  45.3 7.1 %collective-permute-start.2 = (bf16[2,128,384]{2,1,0:T(8,128)(2,1)S(1)}, bf16[2,128,384]{2,1,0:T(8,128)(2,1)S(1)}, u32[]{:S(2)}, u32[]{:S(2)}) collective-permute-start(bf16[2,128,384]{2,1,0:T(8,128)(2,1)S(1)} %get-tuple-element.39), channel_id=1, source_target_pairs={{0,96},{32,0},{64,32},{96,64},{1,97},{33,1},{65,33},{97,65},{2,98}... | collective-permute-start | bytes 589832 | tf_op jit(solution)/shard_map/ppermute | solution.py:302
  52.4 1.9 %collective-permute-start.14 = (bf16[4,4,128,128]{3,2,1,0:T(8,128)(2,1)S(1)}, bf16[4,4,128,128]{3,2,1,0:T(8,128)(2,1)S(1)}, u32[]{:S(2)}, u32[]{:S(2)}) collective-permute-start(bf16[4,4,128,128]{3,2,1,0:T(8,128)(2,1)S(1)} %shard_map.85), channel_id=1, source_target_pairs={{0,1},{1,0},{2,3},{3,2},{4,5},{5,4},{6,7},{7,6},{8,9},{9,8},{10,11... | collective-permute-start | bytes 1572872 | tf_op jit(solution)/shard_map/ppermute | solution.py:302
  55.3 13.7 %all-to-all-start.1 = ((bf16[4,4,128,128]{3,2,1,0:T(8,128)(2,1)}), bf16[4,4,128,128]{3,2,1,0:T(8,128)(2,1)S(1)}, u32[]{:S(2)}, u32[]{:S(2)}) async-start(bf16[4,4,128,128]{3,2,1,0:T(8,128)(2,1)} %shard_map.86.refs_5_), calls=%async_computation.1 | async-start | bytes 1048576 | tf_op jit(solution)/shard_map/all_to_all | solution.py:370
  59.7 20.6 %collective-permute-start.15 = (bf16[4,128,384]{2,1,0:T(8,128)(2,1)S(1)}, bf16[4,128,384]{2,1,0:T(8,128)(2,1)S(1)}, u32[]{:S(2)}, u32[]{:S(2)}) collective-permute-start(bf16[4,128,384]{2,1,0:T(8,128)(2,1)S(1)} %shard_map.87), channel_id=1, source_target_pairs={{0,128},{128,0},{1,129},{129,1},{2,130},{130,2},{3,131},{131,3},{4... | collective-permute-start | bytes 1179656 | tf_op jit(solution)/shard_map/ppermute | solution.py:302
  69.6 6.0 %collective-permute-start.16 = (bf16[2,128,128]{2,1,0:T(8,128)(2,1)S(1)}, bf16[2,128,128]{2,1,0:T(8,128)(2,1)S(1)}, u32[]{:S(2)}, u32[]{:S(2)}) collective-permute-start(bf16[2,128,128]{2,1,0:T(8,128)(2,1)S(1)} %get-tuple-element.34), channel_id=1, source_target_pairs={{0,8},{8,0},{16,24},{24,16},{1,9},{9,1},{17,25},{25,17},{2,10},{10... | collective-permute-start | bytes 196616 | tf_op jit(solution)/shard_map/ppermute | solution.py:378
  75.5 7.0 %collective-permute-start.17 = (f32[128,128]{1,0:T(8,128)S(1)}, f32[128,128]{1,0:T(8,128)S(1)}, u32[]{:S(2)}, u32[]{:S(2)}) collective-permute-start(f32[128,128]{1,0:T(8,128)S(1)} %get-tuple-element.38), channel_id=1, source_target_pairs={{0,24},{8,16},{16,8},{24,0},{1,25},{9,17},{17,9},{25,1},{2,26},{10... | collective-permute-start | bytes 196616 | tf_op jit(solution)/shard_map/ppermute | solution.py:380

commit v6 on v5

--- a/solution.py
+++ b/solution.py
@@ -209,18 +209,21 @@
             send_ref[e, z] = other[e * HD : (e + 1) * HD]
 
 
-def add_kernel(keep_ref, got_ref, out_ref):
-    out_ref[...] = (keep_ref[...] + got_ref[...].astype(F32)).astype(BF16)
-
-
-def sum_kernel(place_ref, got_ref, keep_ref, send_ref):
+def add_kernel(place_ref, keep_ref, got_ref, *out_refs):
+    for step, ref in enumerate(out_refs):
+        e = lax.rem(place_ref[0] + step, 4)
+        ref[...] = (keep_ref[e] + got_ref[e].astype(F32)).astype(BF16)
+
+
+def sum_kernel(place_ref, *refs):
+    got_refs, (keep_ref, send_ref) = refs[:4], refs[4:]
     z_hi = place_ref[3]
     beside = z_hi + 1 - 2 * lax.rem(z_hi, 2)
 
     def summed(block):
-        total = got_ref[0, block].astype(F32)
-        for x in range(1, 4):
-            total += got_ref[x, block].astype(F32)
+        total = got_refs[0][block].astype(F32)
+        for ref in got_refs[1:]:
+            total += ref[block].astype(F32)
         return total
 
     for index in range(2):
@@ -244,7 +247,8 @@
         out_ref[step + 1] = ref[other]
 
 
-def assemble_kernel(place_ref, own_ref, a_ref, b_ref, c_ref, far_ref, q_ref, k_ref):
+def assemble_kernel(place_ref, own_ref, a_ref, b_ref, c_ref, far_ref, q_ref, k_ref, done_ref):
+    done_ref[...] = jnp.zeros_like(done_ref)
     x, z_lo = place_ref[0], place_ref[2]
 
     def put(rows, z, step):
@@ -366,12 +370,14 @@
     )
     got_x = [shift(moved[step], "x", 4, step) for step in range(1, 4)]
     send = call(gate_kernel, [], after=got_x, behind=[send])
-    both = call(add_kernel, shape_of(4, 4, HD, HD), keep, shift(send, "core", 2, 1))
-    over_x = lax.all_to_all(both, "x", 0, 0)
+    both = call(
+        add_kernel, [shape_of(4, HD, HD)] * 4, keep, shift(send, "core", 2, 1), place=place
+    )
+    over_x = [both[0]] + [shift(both[step], "x", 4, step) for step in range(1, 4)]
     keep, send = call(
         sum_kernel,
         [shape_of(2, HD, HD, dtype=F32), shape_of(2, HD, HD)],
-        over_x,
+        *over_x,
         place=place,
         flops=LONG,
     )
@@ -379,17 +385,17 @@
     own, send = call(pair_kernel, [shape_of(HD, HD, dtype=F32)] * 2, keep, got)
     got = lax.ppermute(send, "z_hi", [(z, 3 - z) for z in range(4)])
     packed = call(
-        pack_rows_kernel, shape_of(4, tok, 3 * HD), moved, *got_x, place=place, after=[both]
+        pack_rows_kernel, shape_of(4, tok, 3 * HD), moved, *got_x, place=place, after=[both[0]]
     )
     got_z = shift(packed, "z_lo", 2, 1)
-    query_grad, key_grad = call(
+    query_grad, key_grad, done = call(
         assemble_kernel,
-        (shape_of(tok, 16 * HD), shape_of(tok, 8 * HD)),
+        (shape_of(tok, 16 * HD), shape_of(tok, 8 * HD), shape_of(8, HD, dtype=F32)),
         moved, *got_x, got_z,
         place=place,
         after=[own],
     )
-    weight_grad = call(last_kernel, shape_of(HD, HD, dtype=F32), own, got)
+    weight_grad = call(last_kernel, shape_of(HD, HD, dtype=F32), own, got, after=[done])
     return query_grad[None], key_grad[None], weight_grad
 
 

time: 83.6 us -> 80.9 us (0.968)
  waiting for transfers between devices: 22.2 us -> 18.8 us
    all_to_all x1 -> x0, waiting for transfers between devices: 9.09 us -> none  [on_device(): over_x = lax.all_to_all(both, 'x', 0, 0)]
    ppermute x16 -> x19, waiting for transfers between devices: 9.82 us -> 15.5 us  [shift(): lax.ppermute(array, axis, [(i, (i + by) % size) for i in range(size)])]
    ppermute x16 -> x19, starting transfers between devices: 20.3 us -> 24.5 us  [shift(): lax.ppermute(array, axis, [(i, (i + by) % size) for i in range(size)])]
    all_to_all x1 -> x0, starting transfers between devices: 3.9 us -> none  [on_device(): over_x = lax.all_to_all(both, 'x', 0, 0)]
  transfers between devices with their start and end apart: 20 -> 22, of which waited for: 9 -> 10; matrix products, arithmetic and copies ran while one was open for 0% -> 0% of each run, Pallas kernels for 20% -> 21%
where the time goes in v6:
time: 80.9 us; the launch traced here: 80.3 us
  starting transfers between devices  38.7 us (48%)
  Pallas kernels  19 us (23%)
  waiting for transfers between devices  18.8 us (23%)
  local copies, waits for them, and re-layouts  3.02 us (4%)
    ppermute x19, starting transfers between devices, shift(): lax.ppermute(array, axis, [(i, (i + by) % size) for i in range(size)])  24.5 us
    ppermute x19, waiting for transfers between devices, shift(): lax.ppermute(array, axis, [(i, (i + by) % size) for i in range(size)])  15.5 us
    pallas_call x15, Pallas kernels, call(): pl.pallas_call(body, out_shape=shapes, in_specs=specs, out_specs=out_spec...  14.9 us
    all_to_all x1, starting transfers between devices, on_device(): cot = lax.all_to_all(cot_parts, seq, 0, 0).reshape(length, 2 * HD)  5.65 us
    ppermute x1, starting transfers between devices, on_device(): got = lax.ppermute(send, 'z_hi', [(z, 3 - z) for z in range(4)])  5.23 us
    pallas_call x1, Pallas kernels, probs_of(): pl.pallas_call(probs_kernel, in_specs=[vmem, vmem], out_specs=pl.BlockSpe...  4.09 us
    ppermute x1, starting transfers between devices, on_device(): got = lax.ppermute(send, 'z_hi', [(z, z ^ 1) for z in range(4)])  3.36 us
    unnamed x14, local copies, waits for them, and re-layouts  2.87 us
  transfers between devices with their start and end apart: 22, of which 10 were waited for; matrix products, arithmetic and copies ran while one was open for 0% of the time, Pallas kernels for 21%

profile of v6, /device:TPU:8, one launch (start us, length us, event | category | flops | bytes accessed | tf_op | source)
XLA Modules:
  0.0 80.3 jit_solution(9113456484744758988)
XLA Ops:
  0.7 1.1 %copy-done.3 = bf16[1,128,2048]{2,1,0:T(8,128)(2,1)S(1)} copy-done((bf16[1,128,2048]{2,1,0:T(8,128)(2,1)S(1)}, bf16[1,128,2048]{2,1,0:T(8,128)(2,1)}, u32[]{:S(2)}) %copy-start.3) | copy-done | bytes 524312
  2.6 5.7 %all-to-all-start = ((bf16[8,128,256]{2,1,0:T(8,128)(2,1)}), bf16[8,128,256]{2,1,0:T(8,128)(2,1)S(1)}, u32[]{:S(2)}, u32[]{:S(2)}) async-start(bf16[8,128,256]{2,1,0:T(8,128)(2,1)} %shard_map.77.refs_2_), calls=%async_computation | async-start | bytes 1048576 | tf_op jit(solution)/shard_map/all_to_all | solution.py:318
  9.0 1.7 %collective-permute-start.9 = (bf16[128,1024]{1,0:T(8,128)(2,1)S(1)}, bf16[128,1024]{1,0:T(8,128)(2,1)S(1)}, u32[]{:S(2)}, u32[]{:S(2)}) collective-permute-start(bf16[128,1024]{1,0:T(8,128)(2,1)S(1)} %get-tuple-element.31), channel_id=1, source_target_pairs={{0,2},{2,4},{4,6},{6,0},{1,3},{3,5},{5,7},{7,1},{8,10},{10,12},{12... | collective-permute-start | bytes 786440 | tf_op jit(solution)/shard_map/ppermute | solution.py:306
  10.7 0.9 %collective-permute-start.10 = (bf16[128,1024]{1,0:T(8,128)(2,1)S(1)}, bf16[128,1024]{1,0:T(8,128)(2,1)S(1)}, u32[]{:S(2)}, u32[]{:S(2)}) collective-permute-start(bf16[128,1024]{1,0:T(8,128)(2,1)S(1)} %get-tuple-element.32), channel_id=1, source_target_pairs={{0,4},{2,6},{4,0},{6,2},{1,5},{3,7},{5,1},{7,3},{8,12},{10,14},{12... | collective-permute-start | bytes 786440 | tf_op jit(solution)/shard_map/ppermute | solution.py:306
  11.6 2.4 %collective-permute-start.11 = (bf16[128,1024]{1,0:T(8,128)(2,1)S(1)}, bf16[128,1024]{1,0:T(8,128)(2,1)S(1)}, u32[]{:S(2)}, u32[]{:S(2)}) collective-permute-start(bf16[128,1024]{1,0:T(8,128)(2,1)S(1)} %get-tuple-element.33), channel_id=1, source_target_pairs={{0,6},{2,0},{4,2},{6,4},{1,7},{3,1},{5,3},{7,5},{8,14},{10,8},{12,... | collective-permute-start | bytes 786440 | tf_op jit(solution)/shard_map/ppermute | solution.py:306
  14.0 2.0 %collective-permute-start.12 = (bf16[128,1024]{1,0:T(8,128)(2,1)S(1)}, bf16[128,1024]{1,0:T(8,128)(2,1)S(1)}, u32[]{:S(2)}, u32[]{:S(2)}) collective-permute-start(bf16[128,1024]{1,0:T(8,128)(2,1)S(1)} %get-tuple-element.30.refs_5_), channel_id=1, source_target_pairs={{0,128},{128,0},{1,129},{129,1},{2,130},{130,2},{3,131},{131,3},{4... | collective-permute-start | bytes 786440 | tf_op jit(solution)/shard_map/ppermute | solution.py:306
  16.1 4.1 %shard_map.76.refs_1_ = bf16[2,2560,256]{2,1,0:T(8,128)(2,1)} custom-call(bf16[1024,256]{1,0:T(8,128)(2,1)} %bitcast.23, bf16[1024,128]{1,0:T(8,128)(2,1)} %bitcast.25), custom_call_target="tpu_custom_call" | custom-call | flops 34359738368 | bytes 5242880 | tf_op jit(solution)/shard_map/pallas_call | solution.py:130
  20.2 1.7 %copy-done = bf16[2,2560,256]{2,1,0:T(8,128)(2,1)S(1)} copy-done((bf16[2,2560,256]{2,1,0:T(8,128)(2,1)S(1)}, bf16[2,2560,256]{2,1,0:T(8,128)(2,1)}, u32[]{:S(2)}) %copy-start) | copy-done | bytes 2621464
  21.9 1.5 %shard_map.78 = (bf16[128,256]{1,0:T(8,128)(2,1)S(1)}, bf16[128,256]{1,0:T(8,128)(2,1)S(1)}, bf16[128,256]{1,0:T(8,128)(2,1)S(1)}, bf16[128,256]{1,0:T(8,128)(2,1)S(1)}) custom-call(s32[5]{0:T(128)S(1)} %stack.23.refs_0_, bf16[2,2560,256]{2,1,0:T(8,128)(2,1)S(1)} %copy-done, bf16[1024,256]{1,0:T(8,128)(2,1)S(1)} %bitcast.19), custom_call_target="tpu_custom_call" | custom-call | flops 536870912 | bytes 5242880 | tf_op jit(solution)/shard_map/pallas_call | solution.py:288
  23.4 1.5 %collective-permute-start.3 = (bf16[128,256]{1,0:T(8,128)(2,1)S(1)}, bf16[128,256]{1,0:T(8,128)(2,1)S(1)}, u32[]{:S(2)}, u32[]{:S(2)}) collective-permute-start(bf16[128,256]{1,0:T(8,128)(2,1)S(1)} %get-tuple-element.27), channel_id=1, source_target_pairs={{0,32},{32,64},{64,96},{96,0},{1,33},{33,65},{65,97},{97,1},{2,34}... | collective-permute-start | bytes 196616 | tf_op jit(solution)/shard_map/ppermute | solution.py:306
  25.0 2.7 %collective-permute-start.4 = (bf16[128,256]{1,0:T(8,128)(2,1)S(1)}, bf16[128,256]{1,0:T(8,128)(2,1)S(1)}, u32[]{:S(2)}, u32[]{:S(2)}) collective-permute-start(bf16[128,256]{1,0:T(8,128)(2,1)S(1)} %get-tuple-element.28), channel_id=1, source_target_pairs={{0,64},{32,96},{64,0},{96,32},{1,65},{33,97},{65,1},{97,33},{2,66}... | collective-permute-start | bytes 196616 | tf_op jit(solution)/shard_map/ppermute | solution.py:306
  27.7 1.5 %collective-permute-start.5 = (bf16[128,256]{1,0:T(8,128)(2,1)S(1)}, bf16[128,256]{1,0:T(8,128)(2,1)S(1)}, u32[]{:S(2)}, u32[]{:S(2)}) collective-permute-start(bf16[128,256]{1,0:T(8,128)(2,1)S(1)} %get-tuple-element.29), channel_id=1, source_target_pairs={{0,96},{32,0},{64,32},{96,64},{1,97},{33,1},{65,33},{97,65},{2,98}... | collective-permute-start | bytes 196616 | tf_op jit(solution)/shard_map/ppermute | solution.py:306
  30.7 1.2 %collective-permute-done.5.refs_4_ = bf16[128,256]{1,0:T(8,128)(2,1)S(1)} collective-permute-done((bf16[128,256]{1,0:T(8,128)(2,1)S(1)}, bf16[128,256]{1,0:T(8,128)(2,1)S(1)}, u32[]{:S(2)}, u32[]{:S(2)}) %collective-permute-start.5) | collective-permute-done | bytes 65568 | tf_op jit(solution)/shard_map/ppermute | solution.py:306
  32.5 1.4 %collective-permute-start.6 = (bf16[512,256]{1,0:T(8,128)(2,1)S(1)}, bf16[512,256]{1,0:T(8,128)(2,1)S(1)}, u32[]{:S(2)}, u32[]{:S(2)}) collective-permute-start(bf16[512,256]{1,0:T(8,128)(2,1)S(1)} %shard_map.80.refs_1_), channel_id=1, source_target_pairs={{0,6},{2,0},{4,2},{6,4},{1,7},{3,1},{5,3},{7,5},{8,14},{10,8},{12,... | collective-permute-start | bytes 786440 | tf_op jit(solution)/shard_map/ppermute | solution.py:306
  33.9 1.6 %collective-permute-start.8 = (bf16[512,256]{1,0:T(8,128)(2,1)S(1)}, bf16[512,256]{1,0:T(8,128)(2,1)S(1)}, u32[]{:S(2)}, u32[]{:S(2)}) collective-permute-start(bf16[512,256]{1,0:T(8,128)(2,1)S(1)} %shard_map.80.refs_1_), channel_id=1, source_target_pairs={{0,2},{2,4},{4,6},{6,0},{1,3},{3,5},{5,7},{7,1},{8,10},{10,12},{12... | collective-permute-start | bytes 786440 | tf_op jit(solution)/shard_map/ppermute | solution.py:306
  35.5 4.3 %shard_map.79.refs_9_.refs_1_ = bf16[4,2,128,384]{3,2,1,0:T(8,128)(2,1)S(1)} custom-call(s32[5]{0:T(128)S(1)} %stack.23.refs_0_, bf16[2,2560,256]{2,1,0:T(8,128)(2,1)S(1)} %copy-done.1, bf16[1024,256]{1,0:T(8,128)(2,1)S(1)} %bitcast.24, bf16[1024,128]{1,0:T(8,128)(2,1)S(1)} %bitcast.26, bf16[1024,128]{1,0:T(8,128)(2,1)S(1)} %bitcast.27, ...), custom_call_target="tpu_custom_call" | custom-call | flops 34359738368 | bytes 6291456 | tf_op jit(solution)/shard_map/pallas_call | solution.py:288
  39.9 1.0 %collective-permute-start = (bf16[2,128,384]{2,1,0:T(8,128)(2,1)S(1)}, bf16[2,128,384]{2,1,0:T(8,128)(2,1)S(1)}, u32[]{:S(2)}, u32[]{:S(2)}) collective-permute-start(bf16[2,128,384]{2,1,0:T(8,128)(2,1)S(1)} %get-tuple-element.51), channel_id=1, source_target_pairs={{0,32},{32,64},{64,96},{96,0},{1,33},{33,65},{65,97},{97,1},{2,34}... | collective-permute-start | bytes 589832 | tf_op jit(solution)/shard_map/ppermute | solution.py:306
  40.9 2.5 %collective-permute-done.6.refs_2_ = bf16[512,256]{1,0:T(8,128)(2,1)S(1)} collective-permute-done((bf16[512,256]{1,0:T(8,128)(2,1)S(1)}, bf16[512,256]{1,0:T(8,128)(2,1)S(1)}, u32[]{:S(2)}, u32[]{:S(2)}) %collective-permute-start.6) | collective-permute-done | bytes 262176 | tf_op jit(solution)/shard_map/ppermute | solution.py:306
  43.4 1.9 %collective-permute-start.1 = (bf16[2,128,384]{2,1,0:T(8,128)(2,1)S(1)}, bf16[2,128,384]{2,1,0:T(8,128)(2,1)S(1)}, u32[]{:S(2)}, u32[]{:S(2)}) collective-permute-start(bf16[2,128,384]{2,1,0:T(8,128)(2,1)S(1)} %get-tuple-element.50), channel_id=1, source_target_pairs={{0,64},{32,96},{64,0},{96,32},{1,65},{33,97},{65,1},{97,33},{2,66}... | collective-permute-start | bytes 589832 | tf_op jit(solution)/shard_map/ppermute | solution.py:306
  45.3 1.0 %collective-permute-start.2 = (bf16[2,128,384]{2,1,0:T(8,128)(2,1)S(1)}, bf16[2,128,384]{2,1,0:T(8,128)(2,1)S(1)}, u32[]{:S(2)}, u32[]{:S(2)}) collective-permute-start(bf16[2,128,384]{2,1,0:T(8,128)(2,1)S(1)} %get-tuple-element.49), channel_id=1, source_target_pairs={{0,96},{32,0},{64,32},{96,64},{1,97},{33,1},{65,33},{97,65},{2,98}... | collective-permute-start | bytes 589832 | tf_op jit(solution)/shard_map/ppermute | solution.py:306
  46.3 1.5 %shard_map.82 = (f32[512,1024]{1,0:T(8,128)S(1)}, bf16[512,512]{1,0:T(8,128)(2,1)S(1)}) custom-call(s32[5]{0:T(128)S(1)} %stack.23.refs_0_, bf16[512,256]{1,0:T(8,128)(2,1)S(1)} %shard_map.80.refs_1_, bf16[512,256]{1,0:T(8,128)(2,1)S(1)} %collective-permute-done.6.refs_2_, bf16[512,256]{1,0:T(8,128)(2,1)S(1)} %collective-permute-done.7.refs_3_, ...), custom_call_target="tpu_custom_call" | custom-call | tf_op jit(solution)/shard_map/pallas_call | solution.py:288
  47.8 1.3 %shard_map.84 = (f32[4,4,128,128]{3,2,1,0:T(8,128)S(1)}, bf16[4,4,128,128]{3,2,1,0:T(8,128)(2,1)S(1)}) custom-call(s32[5]{0:T(128)S(1)} %stack.23.refs_0_, f32[512,1024]{1,0:T(8,128)S(1)} %get-tuple-element.34.refs_1_, bf16[512,512]{1,0:T(8,128)(2,1)S(1)} %get-tuple-element.35.refs_2_, bf16[128,1024]{1,0:T(8,128)(2,1)S(1)} %collective-permute-done.12.refs_4_.refs_3_, ...), custom_call_target="tpu_custom_call" | custom-call | flops 34359738368 | bytes 5242880 | tf_op jit(solution)/shard_map/pallas_call | solution.py:288
  49.1 1.4 %collective-permute-done.1.refs_1_.refs_3_ = bf16[2,128,384]{2,1,0:T(8,128)(2,1)S(1)} collective-permute-done((bf16[2,128,384]{2,1,0:T(8,128)(2,1)S(1)}, bf16[2,128,384]{2,1,0:T(8,128)(2,1)S(1)}, u32[]{:S(2)}, u32[]{:S(2)}) %collective-permute-start.1) | collective-permute-done | bytes 196640 | tf_op jit(solution)/shard_map/ppermute | solution.py:306
  50.5 1.9 %collective-permute-done.2.refs_2_.refs_4_ = bf16[2,128,384]{2,1,0:T(8,128)(2,1)S(1)} collective-permute-done((bf16[2,128,384]{2,1,0:T(8,128)(2,1)S(1)}, bf16[2,128,384]{2,1,0:T(8,128)(2,1)S(1)}, u32[]{:S(2)}, u32[]{:S(2)}) %collective-permute-start.2) | collective-permute-done | bytes 196640 | tf_op jit(solution)/shard_map/ppermute | solution.py:306
  52.5 1.9 %collective-permute-done.14.refs_2_ = bf16[4,4,128,128]{3,2,1,0:T(8,128)(2,1)S(1)} collective-permute-done((bf16[4,4,128,128]{3,2,1,0:T(8,128)(2,1)S(1)}, bf16[4,4,128,128]{3,2,1,0:T(8,128)(2,1)S(1)}, u32[]{:S(2)}, u32[]{:S(2)}) %collective-permute-start.14) | collective-permute-done | bytes 524320 | tf_op jit(solution)/shard_map/ppermute | solution.py:306
  55.5 3.6 %collective-permute-start.17 = (bf16[4,128,128]{2,1,0:T(8,128)(2,1)S(1)}, bf16[4,128,128]{2,1,0:T(8,128)(2,1)S(1)}, u32[]{:S(2)}, u32[]{:S(2)}) collective-permute-start(bf16[4,128,128]{2,1,0:T(8,128)(2,1)S(1)} %get-tuple-element.40), channel_id=1, source_target_pairs={{0,64},{32,96},{64,0},{96,32},{1,65},{33,97},{65,1},{97,33},{2,66}... | collective-permute-start | bytes 393224 | tf_op jit(solution)/shard_map/ppermute | solution.py:306
  59.9 2.0 %collective-permute-done.16.refs_2_ = bf16[4,128,128]{2,1,0:T(8,128)(2,1)S(1)} collective-permute-done((bf16[4,128,128]{2,1,0:T(8,128)(2,1)S(1)}, bf16[4,128,128]{2,1,0:T(8,128)(2,1)S(1)}, u32[]{:S(2)}, u32[]{:S(2)}) %collective-permute-start.16) | collective-permute-done | bytes 131104 | tf_op jit(solution)/shard_map/ppermute | solution.py:306
  61.8 3.7 %collective-permute-done.17.refs_3_ = bf16[4,128,128]{2,1,0:T(8,128)(2,1)S(1)} collective-permute-done((bf16[4,128,128]{2,1,0:T(8,128)(2,1)S(1)}, bf16[4,128,128]{2,1,0:T(8,128)(2,1)S(1)}, u32[]{:S(2)}, u32[]{:S(2)}) %collective-permute-start.17) | collective-permute-done | bytes 131104 | tf_op jit(solution)/shard_map/ppermute | solution.py:306
  66.1 3.4 %collective-permute-start.19 = (bf16[2,128,128]{2,1,0:T(8,128)(2,1)S(1)}, bf16[2,128,128]{2,1,0:T(8,128)(2,1)S(1)}, u32[]{:S(2)}, u32[]{:S(2)}) collective-permute-start(bf16[2,128,128]{2,1,0:T(8,128)(2,1)S(1)} %get-tuple-element.43), channel_id=1, source_target_pairs={{0,8},{8,0},{16,24},{24,16},{1,9},{9,1},{17,25},{25,17},{2,10},{10... | collective-permute-start | bytes 196616 | tf_op jit(solution)/shard_map/ppermute | solution.py:384
  69.5 2.4 %collective-permute-done.19.refs_1_ = bf16[2,128,128]{2,1,0:T(8,128)(2,1)S(1)} collective-permute-done((bf16[2,128,128]{2,1,0:T(8,128)(2,1)S(1)}, bf16[2,128,128]{2,1,0:T(8,128)(2,1)S(1)}, u32[]{:S(2)}, u32[]{:S(2)}) %collective-permute-start.19) | collective-permute-done | bytes 65568 | tf_op jit(solution)/shard_map/ppermute | solution.py:384
  71.8 5.2 %collective-permute-start.20 = (f32[128,128]{1,0:T(8,128)S(1)}, f32[128,128]{1,0:T(8,128)S(1)}, u32[]{:S(2)}, u32[]{:S(2)}) collective-permute-start(f32[128,128]{1,0:T(8,128)S(1)} %get-tuple-element.47), channel_id=1, source_target_pairs={{0,24},{8,16},{16,8},{24,0},{1,25},{9,17},{17,9},{25,1},{2,26},{10... | collective-permute-start | bytes 196616 | tf_op jit(solution)/shard_map/ppermute | solution.py:386
  77.1 1.5 %shard_map.90 = (bf16[128,2048]{1,0:T(8,128)(2,1)}, bf16[128,1024]{1,0:T(8,128)(2,1)}, f32[8,128]{1,0:T(8,128)S(1)}) custom-call(s32[5]{0:T(128)S(1)} %stack.23.refs_0_, bf16[4,2,128,384]{3,2,1,0:T(8,128)(2,1)S(1)} %shard_map.79.refs_9_.refs_1_, bf16[2,128,384]{2,1,0:T(8,128)(2,1)S(1)} %collective-permute-done.refs_0_.refs_2_, ...), custom_call_target="tpu_custom_call" | custom-call | bytes 1048576 | tf_op jit(solution)/shard_map/pallas_call | solution.py:288
  (44 shorter events, 8.0 us)
Async XLA Ops:
  0.6 7.7 %copy-start.2 = (bf16[1,128,4096]{2,1,0:T(8,128)(2,1)S(1)}, bf16[1,128,4096]{2,1,0:T(8,128)(2,1)}, u32[]{:S(2)}) copy-start(bf16[1,128,4096]{2,1,0:T(8,128)(2,1)} %param.9) | copy-start | bytes 3145732
  0.6 1.1 %copy-start.3 = (bf16[1,128,2048]{2,1,0:T(8,128)(2,1)S(1)}, bf16[1,128,2048]{2,1,0:T(8,128)(2,1)}, u32[]{:S(2)}) copy-start(bf16[1,128,2048]{2,1,0:T(8,128)(2,1)} %param.8) | copy-start | bytes 1572868
  2.6 17.6 %all-to-all-start = ((bf16[8,128,256]{2,1,0:T(8,128)(2,1)}), bf16[8,128,256]{2,1,0:T(8,128)(2,1)S(1)}, u32[]{:S(2)}, u32[]{:S(2)}) async-start(bf16[8,128,256]{2,1,0:T(8,128)(2,1)} %shard_map.77.refs_2_), calls=%async_computation | async-start | bytes 1048576 | tf_op jit(solution)/shard_map/all_to_all | solution.py:318
  9.0 15.9 %collective-permute-start.9 = (bf16[128,1024]{1,0:T(8,128)(2,1)S(1)}, bf16[128,1024]{1,0:T(8,128)(2,1)S(1)}, u32[]{:S(2)}, u32[]{:S(2)}) collective-permute-start(bf16[128,1024]{1,0:T(8,128)(2,1)S(1)} %get-tuple-element.31), channel_id=1, source_target_pairs={{0,2},{2,4},{4,6},{6,0},{1,3},{3,5},{5,7},{7,1},{8,10},{10,12},{12... | collective-permute-start | bytes 786440 | tf_op jit(solution)/shard_map/ppermute | solution.py:306
  10.7 17.0 %collective-permute-start.10 = (bf16[128,1024]{1,0:T(8,128)(2,1)S(1)}, bf16[128,1024]{1,0:T(8,128)(2,1)S(1)}, u32[]{:S(2)}, u32[]{:S(2)}) collective-permute-start(bf16[128,1024]{1,0:T(8,128)(2,1)S(1)} %get-tuple-element.32), channel_id=1, source_target_pairs={{0,4},{2,6},{4,0},{6,2},{1,5},{3,7},{5,1},{7,3},{8,12},{10,14},{12... | collective-permute-start | bytes 786440 | tf_op jit(solution)/shard_map/ppermute | solution.py:306
  11.6 17.5 %collective-permute-start.11 = (bf16[128,1024]{1,0:T(8,128)(2,1)S(1)}, bf16[128,1024]{1,0:T(8,128)(2,1)S(1)}, u32[]{:S(2)}, u32[]{:S(2)}) collective-permute-start(bf16[128,1024]{1,0:T(8,128)(2,1)S(1)} %get-tuple-element.33), channel_id=1, source_target_pairs={{0,6},{2,0},{4,2},{6,4},{1,7},{3,1},{5,3},{7,5},{8,14},{10,8},{12,... | collective-permute-start | bytes 786440 | tf_op jit(solution)/shard_map/ppermute | solution.py:306
  14.0 15.1 %collective-permute-start.12 = (bf16[128,1024]{1,0:T(8,128)(2,1)S(1)}, bf16[128,1024]{1,0:T(8,128)(2,1)S(1)}, u32[]{:S(2)}, u32[]{:S(2)}) collective-permute-start(bf16[128,1024]{1,0:T(8,128)(2,1)S(1)} %get-tuple-element.30.refs_5_), channel_id=1, source_target_pairs={{0,128},{128,0},{1,129},{129,1},{2,130},{130,2},{3,131},{131,3},{4... | collective-permute-start | bytes 786440 | tf_op jit(solution)/shard_map/ppermute | solution.py:306
  20.2 1.7 %copy-start = (bf16[2,2560,256]{2,1,0:T(8,128)(2,1)S(1)}, bf16[2,2560,256]{2,1,0:T(8,128)(2,1)}, u32[]{:S(2)}) copy-start(bf16[2,2560,256]{2,1,0:T(8,128)(2,1)} %shard_map.76.refs_1_) | copy-start | bytes 7864324
  21.9 13.6 %copy-start.1 = (bf16[2,2560,256]{2,1,0:T(8,128)(2,1)S(1)}, bf16[2,2560,256]{2,1,0:T(8,128)(2,1)}, u32[]{:S(2)}) copy-start(bf16[2,2560,256]{2,1,0:T(8,128)(2,1)} %shard_map.76.refs_1_) | copy-start | bytes 7864324
  21.9 13.6 %copy-start.4 = (bf16[1,1024,256]{2,1,0:T(8,128)(2,1)S(1)}, bf16[1,1024,256]{2,1,0:T(8,128)(2,1)}, u32[]{:S(2)}) copy-start(bf16[1,1024,256]{2,1,0:T(8,128)(2,1)} %param.5) | copy-start | bytes 1572868
  21.9 13.6 %copy-start.5 = (bf16[1,1024,128]{2,1,0:T(8,128)(2,1)S(1)}, bf16[1,1024,128]{2,1,0:T(8,128)(2,1)}, u32[]{:S(2)}) copy-start(bf16[1,1024,128]{2,1,0:T(8,128)(2,1)} %param.6) | copy-start | bytes 786436
  21.9 13.6 %copy-start.6 = (bf16[1,1024,128]{2,1,0:T(8,128)(2,1)S(1)}, bf16[1,1024,128]{2,1,0:T(8,128)(2,1)}, u32[]{:S(2)}) copy-start(bf16[1,1024,128]{2,1,0:T(8,128)(2,1)} %param.7) | copy-start | bytes 786436
  23.4 6.4 %collective-permute-start.3 = (bf16[128,256]{1,0:T(8,128)(2,1)S(1)}, bf16[128,256]{1,0:T(8,128)(2,1)S(1)}, u32[]{:S(2)}, u32[]{:S(2)}) collective-permute-start(bf16[128,256]{1,0:T(8,128)(2,1)S(1)} %get-tuple-element.27), channel_id=1, source_target_pairs={{0,32},{32,64},{64,96},{96,0},{1,33},{33,65},{65,97},{97,1},{2,34}... | collective-permute-start | bytes 196616 | tf_op jit(solution)/shard_map/ppermute | solution.py:306
  25.0 5.8 %collective-permute-start.4 = (bf16[128,256]{1,0:T(8,128)(2,1)S(1)}, bf16[128,256]{1,0:T(8,128)(2,1)S(1)}, u32[]{:S(2)}, u32[]{:S(2)}) collective-permute-start(bf16[128,256]{1,0:T(8,128)(2,1)S(1)} %get-tuple-element.28), channel_id=1, source_target_pairs={{0,64},{32,96},{64,0},{96,32},{1,65},{33,97},{65,1},{97,33},{2,66}... | collective-permute-start | bytes 196616 | tf_op jit(solution)/shard_map/ppermute | solution.py:306
  27.7 4.3 %collective-permute-start.5 = (bf16[128,256]{1,0:T(8,128)(2,1)S(1)}, bf16[128,256]{1,0:T(8,128)(2,1)S(1)}, u32[]{:S(2)}, u32[]{:S(2)}) collective-permute-start(bf16[128,256]{1,0:T(8,128)(2,1)S(1)} %get-tuple-element.29), channel_id=1, source_target_pairs={{0,96},{32,0},{64,32},{96,64},{1,97},{33,1},{65,33},{97,65},{2,98}... | collective-permute-start | bytes 196616 | tf_op jit(solution)/shard_map/ppermute | solution.py:306
  29.2 18.6 %collective-permute-start.13 = (bf16[3,128,1024]{2,1,0:T(8,128)(2,1)S(1)}, bf16[3,128,1024]{2,1,0:T(8,128)(2,1)S(1)}, u32[]{:S(2)}, u32[]{:S(2)}) collective-permute-start(bf16[3,128,1024]{2,1,0:T(8,128)(2,1)S(1)} %shard_map.83), channel_id=1, source_target_pairs={{0,128},{128,0},{1,129},{129,1},{2,130},{130,2},{3,131},{131,3},{4... | collective-permute-start | bytes 2359304 | tf_op jit(solution)/shard_map/ppermute | solution.py:306
  32.5 10.9 %collective-permute-start.6 = (bf16[512,256]{1,0:T(8,128)(2,1)S(1)}, bf16[512,256]{1,0:T(8,128)(2,1)S(1)}, u32[]{:S(2)}, u32[]{:S(2)}) collective-permute-start(bf16[512,256]{1,0:T(8,128)(2,1)S(1)} %shard_map.80.refs_1_), channel_id=1, source_target_pairs={{0,6},{2,0},{4,2},{6,4},{1,7},{3,1},{5,3},{7,5},{8,14},{10,8},{12,... | collective-permute-start | bytes 786440 | tf_op jit(solution)/shard_map/ppermute | solution.py:306
  33.9 11.4 %collective-permute-start.7 = (bf16[512,256]{1,0:T(8,128)(2,1)S(1)}, bf16[512,256]{1,0:T(8,128)(2,1)S(1)}, u32[]{:S(2)}, u32[]{:S(2)}) collective-permute-start(bf16[512,256]{1,0:T(8,128)(2,1)S(1)} %shard_map.80.refs_1_), channel_id=1, source_target_pairs={{0,4},{2,6},{4,0},{6,2},{1,5},{3,7},{5,1},{7,3},{8,12},{10,14},{12... | collective-permute-start | bytes 786440 | tf_op jit(solution)/shard_map/ppermute | solution.py:306
  33.9 12.4 %collective-permute-start.8 = (bf16[512,256]{1,0:T(8,128)(2,1)S(1)}, bf16[512,256]{1,0:T(8,128)(2,1)S(1)}, u32[]{:S(2)}, u32[]{:S(2)}) collective-permute-start(bf16[512,256]{1,0:T(8,128)(2,1)S(1)} %shard_map.80.refs_1_), channel_id=1, source_target_pairs={{0,2},{2,4},{4,6},{6,0},{1,3},{3,5},{5,7},{7,1},{8,10},{10,12},{12... | collective-permute-start | bytes 786440 | tf_op jit(solution)/shard_map/ppermute | solution.py:306
  39.9 9.2 %collective-permute-start = (bf16[2,128,384]{2,1,0:T(8,128)(2,1)S(1)}, bf16[2,128,384]{2,1,0:T(8,128)(2,1)S(1)}, u32[]{:S(2)}, u32[]{:S(2)}) collective-permute-start(bf16[2,128,384]{2,1,0:T(8,128)(2,1)S(1)} %get-tuple-element.51), channel_id=1, source_target_pairs={{0,32},{32,64},{64,96},{96,0},{1,33},{33,65},{65,97},{97,1},{2,34}... | collective-permute-start | bytes 589832 | tf_op jit(solution)/shard_map/ppermute | solution.py:306
  43.4 7.2 %collective-permute-start.1 = (bf16[2,128,384]{2,1,0:T(8,128)(2,1)S(1)}, bf16[2,128,384]{2,1,0:T(8,128)(2,1)S(1)}, u32[]{:S(2)}, u32[]{:S(2)}) collective-permute-start(bf16[2,128,384]{2,1,0:T(8,128)(2,1)S(1)} %get-tuple-element.50), channel_id=1, source_target_pairs={{0,64},{32,96},{64,0},{96,32},{1,65},{33,97},{65,1},{97,33},{2,66}... | collective-permute-start | bytes 589832 | tf_op jit(solution)/shard_map/ppermute | solution.py:306
  45.3 7.1 %collective-permute-start.2 = (bf16[2,128,384]{2,1,0:T(8,128)(2,1)S(1)}, bf16[2,128,384]{2,1,0:T(8,128)(2,1)S(1)}, u32[]{:S(2)}, u32[]{:S(2)}) collective-permute-start(bf16[2,128,384]{2,1,0:T(8,128)(2,1)S(1)} %get-tuple-element.49), channel_id=1, source_target_pairs={{0,96},{32,0},{64,32},{96,64},{1,97},{33,1},{65,33},{97,65},{2,98}... | collective-permute-start | bytes 589832 | tf_op jit(solution)/shard_map/ppermute | solution.py:306
  52.5 1.9 %collective-permute-start.14 = (bf16[4,4,128,128]{3,2,1,0:T(8,128)(2,1)S(1)}, bf16[4,4,128,128]{3,2,1,0:T(8,128)(2,1)S(1)}, u32[]{:S(2)}, u32[]{:S(2)}) collective-permute-start(bf16[4,4,128,128]{3,2,1,0:T(8,128)(2,1)S(1)} %shard_map.85), channel_id=1, source_target_pairs={{0,1},{1,0},{2,3},{3,2},{4,5},{5,4},{6,7},{7,6},{8,9},{9,8},{10,11... | collective-permute-start | bytes 1572872 | tf_op jit(solution)/shard_map/ppermute | solution.py:306
  55.0 6.8 %collective-permute-start.16 = (bf16[4,128,128]{2,1,0:T(8,128)(2,1)S(1)}, bf16[4,128,128]{2,1,0:T(8,128)(2,1)S(1)}, u32[]{:S(2)}, u32[]{:S(2)}) collective-permute-start(bf16[4,128,128]{2,1,0:T(8,128)(2,1)S(1)} %get-tuple-element.39), channel_id=1, source_target_pairs={{0,32},{32,64},{64,96},{96,0},{1,33},{33,65},{65,97},{97,1},{2,34}... | collective-permute-start | bytes 393224 | tf_op jit(solution)/shard_map/ppermute | solution.py:306
  55.5 10.0 %collective-permute-start.17 = (bf16[4,128,128]{2,1,0:T(8,128)(2,1)S(1)}, bf16[4,128,128]{2,1,0:T(8,128)(2,1)S(1)}, u32[]{:S(2)}, u32[]{:S(2)}) collective-permute-start(bf16[4,128,128]{2,1,0:T(8,128)(2,1)S(1)} %get-tuple-element.40), channel_id=1, source_target_pairs={{0,64},{32,96},{64,0},{96,32},{1,65},{33,97},{65,1},{97,33},{2,66}... | collective-permute-start | bytes 393224 | tf_op jit(solution)/shard_map/ppermute | solution.py:306
  59.2 6.3 %collective-permute-start.18 = (bf16[4,128,128]{2,1,0:T(8,128)(2,1)S(1)}, bf16[4,128,128]{2,1,0:T(8,128)(2,1)S(1)}, u32[]{:S(2)}, u32[]{:S(2)}) collective-permute-start(bf16[4,128,128]{2,1,0:T(8,128)(2,1)S(1)} %get-tuple-element.41), channel_id=1, source_target_pairs={{0,96},{32,0},{64,32},{96,64},{1,97},{33,1},{65,33},{97,65},{2,98}... | collective-permute-start | bytes 393224 | tf_op jit(solution)/shard_map/ppermute | solution.py:306
  59.8 17.3 %collective-permute-start.15 = (bf16[4,128,384]{2,1,0:T(8,128)(2,1)S(1)}, bf16[4,128,384]{2,1,0:T(8,128)(2,1)S(1)}, u32[]{:S(2)}, u32[]{:S(2)}) collective-permute-start(bf16[4,128,384]{2,1,0:T(8,128)(2,1)S(1)} %shard_map.87), channel_id=1, source_target_pairs={{0,128},{128,0},{1,129},{129,1},{2,130},{130,2},{3,131},{131,3},{4... | collective-permute-start | bytes 1179656 | tf_op jit(solution)/shard_map/ppermute | solution.py:306
  66.1 5.7 %collective-permute-start.19 = (bf16[2,128,128]{2,1,0:T(8,128)(2,1)S(1)}, bf16[2,128,128]{2,1,0:T(8,128)(2,1)S(1)}, u32[]{:S(2)}, u32[]{:S(2)}) collective-permute-start(bf16[2,128,128]{2,1,0:T(8,128)(2,1)S(1)} %get-tuple-element.43), channel_id=1, source_target_pairs={{0,8},{8,0},{16,24},{24,16},{1,9},{9,1},{17,25},{25,17},{2,10},{10... | collective-permute-start | bytes 196616 | tf_op jit(solution)/shard_map/ppermute | solution.py:384
  71.8 7.7 %collective-permute-start.20 = (f32[128,128]{1,0:T(8,128)S(1)}, f32[128,128]{1,0:T(8,128)S(1)}, u32[]{:S(2)}, u32[]{:S(2)}) collective-permute-start(f32[128,128]{1,0:T(8,128)S(1)} %get-tuple-element.47), channel_id=1, source_target_pairs={{0,24},{8,16},{16,8},{24,0},{1,25},{9,17},{17,9},{25,1},{2,26},{10... | collective-permute-start | bytes 196616 | tf_op jit(solution)/shard_map/ppermute | solution.py:386

commit v7 on v6

--- a/solution.py
+++ b/solution.py
@@ -27,15 +27,24 @@
     return block * (block + 1) // 2 * BLK
 
 
-def probs_kernel(q_ref, k_ref, p_ref, buf_ref, sems):
+def probs_kernel(q_hbm, k_hbm, p_ref, buf_ref, q_ref, k_ref, sems, in_sems):
     length = k_ref.shape[0]
     inv_root = 1.0 / math.sqrt(HD)
     shape = (BLK, BLK)
     keep = lax.broadcasted_iota(jnp.int32, shape, 0) <= lax.broadcasted_iota(jnp.int32, shape, 1)
+    loads = []
+    for start in range(0, length, BLK):
+        rows = pl.ds(start, BLK)
+        for step, (src, dst) in enumerate(((k_hbm, k_ref), (q_hbm, q_ref))):
+            sem = in_sems.at[start // BLK, step]
+            loads.append(pltpu.make_async_copy(src.at[rows], dst.at[rows], sem))
+            loads[-1].start()
     copies = []
-    for head in range(2):
-        for start in range(0, length, BLK):
-            stop = start + BLK
+    for start in range(0, length, BLK):
+        stop = start + BLK
+        loads.pop(0).wait()
+        loads.pop(0).wait()
+        for head in range(2):
             q_block = q_ref[start:stop, head * HD : (head + 1) * HD]
             scores = dot(k_ref[:stop], q_block, NT) * inv_root
             last = jnp.where(keep, scores[start:], -jnp.inf)
@@ -126,13 +135,18 @@
 def probs_of(q, k):
     length = k.shape[0]
     rows = packed_row(length)
-    vmem = pl.BlockSpec(memory_space=pltpu.VMEM)
     return pl.pallas_call(
         probs_kernel,
-        in_specs=[vmem, vmem],
+        in_specs=[pl.BlockSpec(memory_space=pl.ANY)] * 2,
         out_specs=pl.BlockSpec(memory_space=pl.ANY),
         out_shape=pltpu.HBM((2, rows, BLK), BF16),
-        scratch_shapes=[pltpu.VMEM((2, rows, BLK), BF16), pltpu.SemaphoreType.DMA((8,))],
+        scratch_shapes=[
+            pltpu.VMEM((2, rows, BLK), BF16),
+            pltpu.VMEM((length, 2 * HD), BF16),
+            pltpu.VMEM((length, HD), BF16),
+            pltpu.SemaphoreType.DMA((8,)),
+            pltpu.SemaphoreType.DMA((length // BLK, 2)),
+        ],
         compiler_params=params(),
         cost_estimate=pl.CostEstimate(
             flops=LONG, bytes_accessed=5 << 20, transcendentals=length * length

time: 80.9 us -> 81.7 us (level)
  no operation moved by 1% of the time
where the time goes in v7:
time: 81.7 us; the launch traced here: 81.2 us
  starting transfers between devices  39.4 us (48%)
  Pallas kernels  19.6 us (24%)
  waiting for transfers between devices  18.4 us (23%)
  local copies, waits for them, and re-layouts  3.02 us (4%)
    ppermute x19, starting transfers between devices, shift(): lax.ppermute(array, axis, [(i, (i + by) % size) for i in range(size)])  24.9 us
    ppermute x19, waiting for transfers between devices, shift(): lax.ppermute(array, axis, [(i, (i + by) % size) for i in range(size)])  15 us
    pallas_call x15, Pallas kernels, call(): pl.pallas_call(body, out_shape=shapes, in_specs=specs, out_specs=out_spec...  14.9 us
    all_to_all x1, starting transfers between devices, on_device(): cot = lax.all_to_all(cot_parts, seq, 0, 0).reshape(length, 2 * HD)  5.65 us
    ppermute x1, starting transfers between devices, on_device(): got = lax.ppermute(send, 'z_hi', [(z, 3 - z) for z in range(4)])  5.47 us
    pallas_call x1, Pallas kernels, probs_of(): pl.pallas_call(probs_kernel, in_specs=[pl.BlockSpec(memory_space=pl.ANY)]...  4.7 us
    ppermute x1, starting transfers between devices, on_device(): got = lax.ppermute(send, 'z_hi', [(z, z ^ 1) for z in range(4)])  3.36 us
    unnamed x14, local copies, waits for them, and re-layouts  2.87 us
  transfers between devices with their start and end apart: 22, of which 10 were waited for; matrix products, arithmetic and copies ran while one was open for 0% of the time, Pallas kernels for 21%

profile of v7, /device:TPU:8, one launch (start us, length us, event | category | flops | bytes accessed | tf_op | source)
XLA Modules:
  0.0 81.2 jit_solution(8697213201249001302)
XLA Ops:
  0.7 1.1 %copy-done.3 = bf16[1,128,2048]{2,1,0:T(8,128)(2,1)S(1)} copy-done((bf16[1,128,2048]{2,1,0:T(8,128)(2,1)S(1)}, bf16[1,128,2048]{2,1,0:T(8,128)(2,1)}, u32[]{:S(2)}) %copy-start.3) | copy-done | bytes 524312
  2.6 5.7 %all-to-all-start = ((bf16[8,128,256]{2,1,0:T(8,128)(2,1)}), bf16[8,128,256]{2,1,0:T(8,128)(2,1)S(1)}, u32[]{:S(2)}, u32[]{:S(2)}) async-start(bf16[8,128,256]{2,1,0:T(8,128)(2,1)} %shard_map.77.refs_2_), calls=%async_computation | async-start | bytes 1048576 | tf_op jit(solution)/shard_map/all_to_all | solution.py:332
  9.0 1.7 %collective-permute-start.9 = (bf16[128,1024]{1,0:T(8,128)(2,1)S(1)}, bf16[128,1024]{1,0:T(8,128)(2,1)S(1)}, u32[]{:S(2)}, u32[]{:S(2)}) collective-permute-start(bf16[128,1024]{1,0:T(8,128)(2,1)S(1)} %get-tuple-element.31), channel_id=1, source_target_pairs={{0,2},{2,4},{4,6},{6,0},{1,3},{3,5},{5,7},{7,1},{8,10},{10,12},{12... | collective-permute-start | bytes 786440 | tf_op jit(solution)/shard_map/ppermute | solution.py:320
  10.7 0.9 %collective-permute-start.10 = (bf16[128,1024]{1,0:T(8,128)(2,1)S(1)}, bf16[128,1024]{1,0:T(8,128)(2,1)S(1)}, u32[]{:S(2)}, u32[]{:S(2)}) collective-permute-start(bf16[128,1024]{1,0:T(8,128)(2,1)S(1)} %get-tuple-element.32), channel_id=1, source_target_pairs={{0,4},{2,6},{4,0},{6,2},{1,5},{3,7},{5,1},{7,3},{8,12},{10,14},{12... | collective-permute-start | bytes 786440 | tf_op jit(solution)/shard_map/ppermute | solution.py:320
  11.6 2.4 %collective-permute-start.11 = (bf16[128,1024]{1,0:T(8,128)(2,1)S(1)}, bf16[128,1024]{1,0:T(8,128)(2,1)S(1)}, u32[]{:S(2)}, u32[]{:S(2)}) collective-permute-start(bf16[128,1024]{1,0:T(8,128)(2,1)S(1)} %get-tuple-element.33), channel_id=1, source_target_pairs={{0,6},{2,0},{4,2},{6,4},{1,7},{3,1},{5,3},{7,5},{8,14},{10,8},{12,... | collective-permute-start | bytes 786440 | tf_op jit(solution)/shard_map/ppermute | solution.py:320
  14.0 2.0 %collective-permute-start.12 = (bf16[128,1024]{1,0:T(8,128)(2,1)S(1)}, bf16[128,1024]{1,0:T(8,128)(2,1)S(1)}, u32[]{:S(2)}, u32[]{:S(2)}) collective-permute-start(bf16[128,1024]{1,0:T(8,128)(2,1)S(1)} %get-tuple-element.30.refs_5_), channel_id=1, source_target_pairs={{0,128},{128,0},{1,129},{129,1},{2,130},{130,2},{3,131},{131,3},{4... | collective-permute-start | bytes 786440 | tf_op jit(solution)/shard_map/ppermute | solution.py:320
  16.1 4.7 %shard_map.76.refs_1_ = bf16[2,2560,256]{2,1,0:T(8,128)(2,1)} custom-call(bf16[1024,256]{1,0:T(8,128)(2,1)} %bitcast.23, bf16[1024,128]{1,0:T(8,128)(2,1)} %bitcast.25), custom_call_target="tpu_custom_call" | custom-call | flops 34359738368 | bytes 5242880 | tf_op jit(solution)/shard_map/pallas_call | solution.py:138
  20.8 1.7 %copy-done = bf16[2,2560,256]{2,1,0:T(8,128)(2,1)S(1)} copy-done((bf16[2,2560,256]{2,1,0:T(8,128)(2,1)S(1)}, bf16[2,2560,256]{2,1,0:T(8,128)(2,1)}, u32[]{:S(2)}) %copy-start) | copy-done | bytes 2621464
  22.5 1.5 %shard_map.78 = (bf16[128,256]{1,0:T(8,128)(2,1)S(1)}, bf16[128,256]{1,0:T(8,128)(2,1)S(1)}, bf16[128,256]{1,0:T(8,128)(2,1)S(1)}, bf16[128,256]{1,0:T(8,128)(2,1)S(1)}) custom-call(s32[5]{0:T(128)S(1)} %stack.23.refs_0_, bf16[2,2560,256]{2,1,0:T(8,128)(2,1)S(1)} %copy-done, bf16[1024,256]{1,0:T(8,128)(2,1)S(1)} %bitcast.19), custom_call_target="tpu_custom_call" | custom-call | flops 536870912 | bytes 5242880 | tf_op jit(solution)/shard_map/pallas_call | solution.py:302
  24.0 1.5 %collective-permute-start.3 = (bf16[128,256]{1,0:T(8,128)(2,1)S(1)}, bf16[128,256]{1,0:T(8,128)(2,1)S(1)}, u32[]{:S(2)}, u32[]{:S(2)}) collective-permute-start(bf16[128,256]{1,0:T(8,128)(2,1)S(1)} %get-tuple-element.27), channel_id=1, source_target_pairs={{0,32},{32,64},{64,96},{96,0},{1,33},{33,65},{65,97},{97,1},{2,34}... | collective-permute-start | bytes 196616 | tf_op jit(solution)/shard_map/ppermute | solution.py:320
  25.6 2.7 %collective-permute-start.4 = (bf16[128,256]{1,0:T(8,128)(2,1)S(1)}, bf16[128,256]{1,0:T(8,128)(2,1)S(1)}, u32[]{:S(2)}, u32[]{:S(2)}) collective-permute-start(bf16[128,256]{1,0:T(8,128)(2,1)S(1)} %get-tuple-element.28), channel_id=1, source_target_pairs={{0,64},{32,96},{64,0},{96,32},{1,65},{33,97},{65,1},{97,33},{2,66}... | collective-permute-start | bytes 196616 | tf_op jit(solution)/shard_map/ppermute | solution.py:320
  28.3 1.5 %collective-permute-start.5 = (bf16[128,256]{1,0:T(8,128)(2,1)S(1)}, bf16[128,256]{1,0:T(8,128)(2,1)S(1)}, u32[]{:S(2)}, u32[]{:S(2)}) collective-permute-start(bf16[128,256]{1,0:T(8,128)(2,1)S(1)} %get-tuple-element.29), channel_id=1, source_target_pairs={{0,96},{32,0},{64,32},{96,64},{1,97},{33,1},{65,33},{97,65},{2,98}... | collective-permute-start | bytes 196616 | tf_op jit(solution)/shard_map/ppermute | solution.py:320
  31.4 1.2 %collective-permute-done.5.refs_4_ = bf16[128,256]{1,0:T(8,128)(2,1)S(1)} collective-permute-done((bf16[128,256]{1,0:T(8,128)(2,1)S(1)}, bf16[128,256]{1,0:T(8,128)(2,1)S(1)}, u32[]{:S(2)}, u32[]{:S(2)}) %collective-permute-start.5) | collective-permute-done | bytes 65568 | tf_op jit(solution)/shard_map/ppermute | solution.py:320
  33.1 1.4 %collective-permute-start.6 = (bf16[512,256]{1,0:T(8,128)(2,1)S(1)}, bf16[512,256]{1,0:T(8,128)(2,1)S(1)}, u32[]{:S(2)}, u32[]{:S(2)}) collective-permute-start(bf16[512,256]{1,0:T(8,128)(2,1)S(1)} %shard_map.80.refs_1_), channel_id=1, source_target_pairs={{0,6},{2,0},{4,2},{6,4},{1,7},{3,1},{5,3},{7,5},{8,14},{10,8},{12,... | collective-permute-start | bytes 786440 | tf_op jit(solution)/shard_map/ppermute | solution.py:320
  34.5 1.6 %collective-permute-start.8 = (bf16[512,256]{1,0:T(8,128)(2,1)S(1)}, bf16[512,256]{1,0:T(8,128)(2,1)S(1)}, u32[]{:S(2)}, u32[]{:S(2)}) collective-permute-start(bf16[512,256]{1,0:T(8,128)(2,1)S(1)} %shard_map.80.refs_1_), channel_id=1, source_target_pairs={{0,2},{2,4},{4,6},{6,0},{1,3},{3,5},{5,7},{7,1},{8,10},{10,12},{12... | collective-permute-start | bytes 786440 | tf_op jit(solution)/shard_map/ppermute | solution.py:320
  36.1 4.3 %shard_map.79.refs_9_.refs_1_ = bf16[4,2,128,384]{3,2,1,0:T(8,128)(2,1)S(1)} custom-call(s32[5]{0:T(128)S(1)} %stack.23.refs_0_, bf16[2,2560,256]{2,1,0:T(8,128)(2,1)S(1)} %copy-done.1, bf16[1024,256]{1,0:T(8,128)(2,1)S(1)} %bitcast.24, bf16[1024,128]{1,0:T(8,128)(2,1)S(1)} %bitcast.26, bf16[1024,128]{1,0:T(8,128)(2,1)S(1)} %bitcast.27, ...), custom_call_target="tpu_custom_call" | custom-call | flops 34359738368 | bytes 6291456 | tf_op jit(solution)/shard_map/pallas_call | solution.py:302
  41.2 2.8 %collective-permute-done.6.refs_2_ = bf16[512,256]{1,0:T(8,128)(2,1)S(1)} collective-permute-done((bf16[512,256]{1,0:T(8,128)(2,1)S(1)}, bf16[512,256]{1,0:T(8,128)(2,1)S(1)}, u32[]{:S(2)}, u32[]{:S(2)}) %collective-permute-start.6) | collective-permute-done | bytes 262176 | tf_op jit(solution)/shard_map/ppermute | solution.py:320
  44.0 1.9 %collective-permute-start.1 = (bf16[2,128,384]{2,1,0:T(8,128)(2,1)S(1)}, bf16[2,128,384]{2,1,0:T(8,128)(2,1)S(1)}, u32[]{:S(2)}, u32[]{:S(2)}) collective-permute-start(bf16[2,128,384]{2,1,0:T(8,128)(2,1)S(1)} %get-tuple-element.50), channel_id=1, source_target_pairs={{0,64},{32,96},{64,0},{96,32},{1,65},{33,97},{65,1},{97,33},{2,66}... | collective-permute-start | bytes 589832 | tf_op jit(solution)/shard_map/ppermute | solution.py:320
  45.9 1.1 %collective-permute-start.2 = (bf16[2,128,384]{2,1,0:T(8,128)(2,1)S(1)}, bf16[2,128,384]{2,1,0:T(8,128)(2,1)S(1)}, u32[]{:S(2)}, u32[]{:S(2)}) collective-permute-start(bf16[2,128,384]{2,1,0:T(8,128)(2,1)S(1)} %get-tuple-element.49), channel_id=1, source_target_pairs={{0,96},{32,0},{64,32},{96,64},{1,97},{33,1},{65,33},{97,65},{2,98}... | collective-permute-start | bytes 589832 | tf_op jit(solution)/shard_map/ppermute | solution.py:320
  47.1 1.5 %shard_map.82 = (f32[512,1024]{1,0:T(8,128)S(1)}, bf16[512,512]{1,0:T(8,128)(2,1)S(1)}) custom-call(s32[5]{0:T(128)S(1)} %stack.23.refs_0_, bf16[512,256]{1,0:T(8,128)(2,1)S(1)} %shard_map.80.refs_1_, bf16[512,256]{1,0:T(8,128)(2,1)S(1)} %collective-permute-done.6.refs_2_, bf16[512,256]{1,0:T(8,128)(2,1)S(1)} %collective-permute-done.7.refs_3_, ...), custom_call_target="tpu_custom_call" | custom-call | tf_op jit(solution)/shard_map/pallas_call | solution.py:302
  48.6 1.3 %shard_map.84 = (f32[4,4,128,128]{3,2,1,0:T(8,128)S(1)}, bf16[4,4,128,128]{3,2,1,0:T(8,128)(2,1)S(1)}) custom-call(s32[5]{0:T(128)S(1)} %stack.23.refs_0_, f32[512,1024]{1,0:T(8,128)S(1)} %get-tuple-element.34.refs_1_, bf16[512,512]{1,0:T(8,128)(2,1)S(1)} %get-tuple-element.35.refs_2_, bf16[128,1024]{1,0:T(8,128)(2,1)S(1)} %collective-permute-done.12.refs_4_.refs_3_, ...), custom_call_target="tpu_custom_call" | custom-call | flops 34359738368 | bytes 5242880 | tf_op jit(solution)/shard_map/pallas_call | solution.py:302
  49.9 1.3 %collective-permute-done.1.refs_1_.refs_3_ = bf16[2,128,384]{2,1,0:T(8,128)(2,1)S(1)} collective-permute-done((bf16[2,128,384]{2,1,0:T(8,128)(2,1)S(1)}, bf16[2,128,384]{2,1,0:T(8,128)(2,1)S(1)}, u32[]{:S(2)}, u32[]{:S(2)}) %collective-permute-start.1) | collective-permute-done | bytes 196640 | tf_op jit(solution)/shard_map/ppermute | solution.py:320
  51.2 1.8 %collective-permute-done.2.refs_2_.refs_4_ = bf16[2,128,384]{2,1,0:T(8,128)(2,1)S(1)} collective-permute-done((bf16[2,128,384]{2,1,0:T(8,128)(2,1)S(1)}, bf16[2,128,384]{2,1,0:T(8,128)(2,1)S(1)}, u32[]{:S(2)}, u32[]{:S(2)}) %collective-permute-start.2) | collective-permute-done | bytes 196640 | tf_op jit(solution)/shard_map/ppermute | solution.py:320
  53.0 1.9 %collective-permute-done.14.refs_2_ = bf16[4,4,128,128]{3,2,1,0:T(8,128)(2,1)S(1)} collective-permute-done((bf16[4,4,128,128]{3,2,1,0:T(8,128)(2,1)S(1)}, bf16[4,4,128,128]{3,2,1,0:T(8,128)(2,1)S(1)}, u32[]{:S(2)}, u32[]{:S(2)}) %collective-permute-start.14) | collective-permute-done | bytes 524320 | tf_op jit(solution)/shard_map/ppermute | solution.py:320
  56.3 3.5 %collective-permute-start.17 = (bf16[4,128,128]{2,1,0:T(8,128)(2,1)S(1)}, bf16[4,128,128]{2,1,0:T(8,128)(2,1)S(1)}, u32[]{:S(2)}, u32[]{:S(2)}) collective-permute-start(bf16[4,128,128]{2,1,0:T(8,128)(2,1)S(1)} %get-tuple-element.40), channel_id=1, source_target_pairs={{0,64},{32,96},{64,0},{96,32},{1,65},{33,97},{65,1},{97,33},{2,66}... | collective-permute-start | bytes 393224 | tf_op jit(solution)/shard_map/ppermute | solution.py:320
  61.0 1.4 %collective-permute-done.16.refs_2_ = bf16[4,128,128]{2,1,0:T(8,128)(2,1)S(1)} collective-permute-done((bf16[4,128,128]{2,1,0:T(8,128)(2,1)S(1)}, bf16[4,128,128]{2,1,0:T(8,128)(2,1)S(1)}, u32[]{:S(2)}, u32[]{:S(2)}) %collective-permute-start.16) | collective-permute-done | bytes 131104 | tf_op jit(solution)/shard_map/ppermute | solution.py:320
  62.4 3.7 %collective-permute-done.17.refs_3_ = bf16[4,128,128]{2,1,0:T(8,128)(2,1)S(1)} collective-permute-done((bf16[4,128,128]{2,1,0:T(8,128)(2,1)S(1)}, bf16[4,128,128]{2,1,0:T(8,128)(2,1)S(1)}, u32[]{:S(2)}, u32[]{:S(2)}) %collective-permute-start.17) | collective-permute-done | bytes 131104 | tf_op jit(solution)/shard_map/ppermute | solution.py:320
  66.7 3.4 %collective-permute-start.19 = (bf16[2,128,128]{2,1,0:T(8,128)(2,1)S(1)}, bf16[2,128,128]{2,1,0:T(8,128)(2,1)S(1)}, u32[]{:S(2)}, u32[]{:S(2)}) collective-permute-start(bf16[2,128,128]{2,1,0:T(8,128)(2,1)S(1)} %get-tuple-element.43), channel_id=1, source_target_pairs={{0,8},{8,0},{16,24},{24,16},{1,9},{9,1},{17,25},{25,17},{2,10},{10... | collective-permute-start | bytes 196616 | tf_op jit(solution)/shard_map/ppermute | solution.py:398
  70.1 2.4 %collective-permute-done.19.refs_1_ = bf16[2,128,128]{2,1,0:T(8,128)(2,1)S(1)} collective-permute-done((bf16[2,128,128]{2,1,0:T(8,128)(2,1)S(1)}, bf16[2,128,128]{2,1,0:T(8,128)(2,1)S(1)}, u32[]{:S(2)}, u32[]{:S(2)}) %collective-permute-start.19) | collective-permute-done | bytes 65568 | tf_op jit(solution)/shard_map/ppermute | solution.py:398
  72.5 5.5 %collective-permute-start.20 = (f32[128,128]{1,0:T(8,128)S(1)}, f32[128,128]{1,0:T(8,128)S(1)}, u32[]{:S(2)}, u32[]{:S(2)}) collective-permute-start(f32[128,128]{1,0:T(8,128)S(1)} %get-tuple-element.47), channel_id=1, source_target_pairs={{0,24},{8,16},{16,8},{24,0},{1,25},{9,17},{17,9},{25,1},{2,26},{10... | collective-permute-start | bytes 196616 | tf_op jit(solution)/shard_map/ppermute | solution.py:400
  77.9 1.5 %shard_map.90 = (bf16[128,2048]{1,0:T(8,128)(2,1)}, bf16[128,1024]{1,0:T(8,128)(2,1)}, f32[8,128]{1,0:T(8,128)S(1)}) custom-call(s32[5]{0:T(128)S(1)} %stack.23.refs_0_, bf16[4,2,128,384]{3,2,1,0:T(8,128)(2,1)S(1)} %shard_map.79.refs_9_.refs_1_, bf16[2,128,384]{2,1,0:T(8,128)(2,1)S(1)} %collective-permute-done.refs_0_.refs_2_, ...), custom_call_target="tpu_custom_call" | custom-call | bytes 1048576 | tf_op jit(solution)/shard_map/pallas_call | solution.py:302
  79.5 1.0 %collective-permute-done.20.refs_1_ = f32[128,128]{1,0:T(8,128)S(1)} collective-permute-done((f32[128,128]{1,0:T(8,128)S(1)}, f32[128,128]{1,0:T(8,128)S(1)}, u32[]{:S(2)}, u32[]{:S(2)}) %collective-permute-start.20) | collective-permute-done | bytes 65568 | tf_op jit(solution)/shard_map/ppermute | solution.py:400
  (44 shorter events, 8.5 us)
Async XLA Ops:
  0.6 7.7 %copy-start.2 = (bf16[1,128,4096]{2,1,0:T(8,128)(2,1)S(1)}, bf16[1,128,4096]{2,1,0:T(8,128)(2,1)}, u32[]{:S(2)}) copy-start(bf16[1,128,4096]{2,1,0:T(8,128)(2,1)} %param.9) | copy-start | bytes 3145732
  0.6 1.1 %copy-start.3 = (bf16[1,128,2048]{2,1,0:T(8,128)(2,1)S(1)}, bf16[1,128,2048]{2,1,0:T(8,128)(2,1)}, u32[]{:S(2)}) copy-start(bf16[1,128,2048]{2,1,0:T(8,128)(2,1)} %param.8) | copy-start | bytes 1572868
  2.6 18.2 %all-to-all-start = ((bf16[8,128,256]{2,1,0:T(8,128)(2,1)}), bf16[8,128,256]{2,1,0:T(8,128)(2,1)S(1)}, u32[]{:S(2)}, u32[]{:S(2)}) async-start(bf16[8,128,256]{2,1,0:T(8,128)(2,1)} %shard_map.77.refs_2_), calls=%async_computation | async-start | bytes 1048576 | tf_op jit(solution)/shard_map/all_to_all | solution.py:332
  9.0 16.6 %collective-permute-start.9 = (bf16[128,1024]{1,0:T(8,128)(2,1)S(1)}, bf16[128,1024]{1,0:T(8,128)(2,1)S(1)}, u32[]{:S(2)}, u32[]{:S(2)}) collective-permute-start(bf16[128,1024]{1,0:T(8,128)(2,1)S(1)} %get-tuple-element.31), channel_id=1, source_target_pairs={{0,2},{2,4},{4,6},{6,0},{1,3},{3,5},{5,7},{7,1},{8,10},{10,12},{12... | collective-permute-start | bytes 786440 | tf_op jit(solution)/shard_map/ppermute | solution.py:320
  10.7 17.6 %collective-permute-start.10 = (bf16[128,1024]{1,0:T(8,128)(2,1)S(1)}, bf16[128,1024]{1,0:T(8,128)(2,1)S(1)}, u32[]{:S(2)}, u32[]{:S(2)}) collective-permute-start(bf16[128,1024]{1,0:T(8,128)(2,1)S(1)} %get-tuple-element.32), channel_id=1, source_target_pairs={{0,4},{2,6},{4,0},{6,2},{1,5},{3,7},{5,1},{7,3},{8,12},{10,14},{12... | collective-permute-start | bytes 786440 | tf_op jit(solution)/shard_map/ppermute | solution.py:320
  11.6 18.1 %collective-permute-start.11 = (bf16[128,1024]{1,0:T(8,128)(2,1)S(1)}, bf16[128,1024]{1,0:T(8,128)(2,1)S(1)}, u32[]{:S(2)}, u32[]{:S(2)}) collective-permute-start(bf16[128,1024]{1,0:T(8,128)(2,1)S(1)} %get-tuple-element.33), channel_id=1, source_target_pairs={{0,6},{2,0},{4,2},{6,4},{1,7},{3,1},{5,3},{7,5},{8,14},{10,8},{12,... | collective-permute-start | bytes 786440 | tf_op jit(solution)/shard_map/ppermute | solution.py:320
  14.0 15.7 %collective-permute-start.12 = (bf16[128,1024]{1,0:T(8,128)(2,1)S(1)}, bf16[128,1024]{1,0:T(8,128)(2,1)S(1)}, u32[]{:S(2)}, u32[]{:S(2)}) collective-permute-start(bf16[128,1024]{1,0:T(8,128)(2,1)S(1)} %get-tuple-element.30.refs_5_), channel_id=1, source_target_pairs={{0,128},{128,0},{1,129},{129,1},{2,130},{130,2},{3,131},{131,3},{4... | collective-permute-start | bytes 786440 | tf_op jit(solution)/shard_map/ppermute | solution.py:320
  20.8 1.7 %copy-start = (bf16[2,2560,256]{2,1,0:T(8,128)(2,1)S(1)}, bf16[2,2560,256]{2,1,0:T(8,128)(2,1)}, u32[]{:S(2)}) copy-start(bf16[2,2560,256]{2,1,0:T(8,128)(2,1)} %shard_map.76.refs_1_) | copy-start | bytes 7864324
  22.5 13.6 %copy-start.1 = (bf16[2,2560,256]{2,1,0:T(8,128)(2,1)S(1)}, bf16[2,2560,256]{2,1,0:T(8,128)(2,1)}, u32[]{:S(2)}) copy-start(bf16[2,2560,256]{2,1,0:T(8,128)(2,1)} %shard_map.76.refs_1_) | copy-start | bytes 7864324
  22.5 13.6 %copy-start.4 = (bf16[1,1024,256]{2,1,0:T(8,128)(2,1)S(1)}, bf16[1,1024,256]{2,1,0:T(8,128)(2,1)}, u32[]{:S(2)}) copy-start(bf16[1,1024,256]{2,1,0:T(8,128)(2,1)} %param.5) | copy-start | bytes 1572868
  22.5 13.6 %copy-start.5 = (bf16[1,1024,128]{2,1,0:T(8,128)(2,1)S(1)}, bf16[1,1024,128]{2,1,0:T(8,128)(2,1)}, u32[]{:S(2)}) copy-start(bf16[1,1024,128]{2,1,0:T(8,128)(2,1)} %param.6) | copy-start | bytes 786436
  22.5 13.6 %copy-start.6 = (bf16[1,1024,128]{2,1,0:T(8,128)(2,1)S(1)}, bf16[1,1024,128]{2,1,0:T(8,128)(2,1)}, u32[]{:S(2)}) copy-start(bf16[1,1024,128]{2,1,0:T(8,128)(2,1)} %param.7) | copy-start | bytes 786436
  24.0 6.4 %collective-permute-start.3 = (bf16[128,256]{1,0:T(8,128)(2,1)S(1)}, bf16[128,256]{1,0:T(8,128)(2,1)S(1)}, u32[]{:S(2)}, u32[]{:S(2)}) collective-permute-start(bf16[128,256]{1,0:T(8,128)(2,1)S(1)} %get-tuple-element.27), channel_id=1, source_target_pairs={{0,32},{32,64},{64,96},{96,0},{1,33},{33,65},{65,97},{97,1},{2,34}... | collective-permute-start | bytes 196616 | tf_op jit(solution)/shard_map/ppermute | solution.py:320
  25.6 5.8 %collective-permute-start.4 = (bf16[128,256]{1,0:T(8,128)(2,1)S(1)}, bf16[128,256]{1,0:T(8,128)(2,1)S(1)}, u32[]{:S(2)}, u32[]{:S(2)}) collective-permute-start(bf16[128,256]{1,0:T(8,128)(2,1)S(1)} %get-tuple-element.28), channel_id=1, source_target_pairs={{0,64},{32,96},{64,0},{96,32},{1,65},{33,97},{65,1},{97,33},{2,66}... | collective-permute-start | bytes 196616 | tf_op jit(solution)/shard_map/ppermute | solution.py:320
  28.3 4.3 %collective-permute-start.5 = (bf16[128,256]{1,0:T(8,128)(2,1)S(1)}, bf16[128,256]{1,0:T(8,128)(2,1)S(1)}, u32[]{:S(2)}, u32[]{:S(2)}) collective-permute-start(bf16[128,256]{1,0:T(8,128)(2,1)S(1)} %get-tuple-element.29), channel_id=1, source_target_pairs={{0,96},{32,0},{64,32},{96,64},{1,97},{33,1},{65,33},{97,65},{2,98}... | collective-permute-start | bytes 196616 | tf_op jit(solution)/shard_map/ppermute | solution.py:320
  29.8 18.8 %collective-permute-start.13 = (bf16[3,128,1024]{2,1,0:T(8,128)(2,1)S(1)}, bf16[3,128,1024]{2,1,0:T(8,128)(2,1)S(1)}, u32[]{:S(2)}, u32[]{:S(2)}) collective-permute-start(bf16[3,128,1024]{2,1,0:T(8,128)(2,1)S(1)} %shard_map.83), channel_id=1, source_target_pairs={{0,128},{128,0},{1,129},{129,1},{2,130},{130,2},{3,131},{131,3},{4... | collective-permute-start | bytes 2359304 | tf_op jit(solution)/shard_map/ppermute | solution.py:320
  33.1 10.9 %collective-permute-start.6 = (bf16[512,256]{1,0:T(8,128)(2,1)S(1)}, bf16[512,256]{1,0:T(8,128)(2,1)S(1)}, u32[]{:S(2)}, u32[]{:S(2)}) collective-permute-start(bf16[512,256]{1,0:T(8,128)(2,1)S(1)} %shard_map.80.refs_1_), channel_id=1, source_target_pairs={{0,6},{2,0},{4,2},{6,4},{1,7},{3,1},{5,3},{7,5},{8,14},{10,8},{12,... | collective-permute-start | bytes 786440 | tf_op jit(solution)/shard_map/ppermute | solution.py:320
  34.5 11.4 %collective-permute-start.7 = (bf16[512,256]{1,0:T(8,128)(2,1)S(1)}, bf16[512,256]{1,0:T(8,128)(2,1)S(1)}, u32[]{:S(2)}, u32[]{:S(2)}) collective-permute-start(bf16[512,256]{1,0:T(8,128)(2,1)S(1)} %shard_map.80.refs_1_), channel_id=1, source_target_pairs={{0,4},{2,6},{4,0},{6,2},{1,5},{3,7},{5,1},{7,3},{8,12},{10,14},{12... | collective-permute-start | bytes 786440 | tf_op jit(solution)/shard_map/ppermute | solution.py:320
  34.5 12.5 %collective-permute-start.8 = (bf16[512,256]{1,0:T(8,128)(2,1)S(1)}, bf16[512,256]{1,0:T(8,128)(2,1)S(1)}, u32[]{:S(2)}, u32[]{:S(2)}) collective-permute-start(bf16[512,256]{1,0:T(8,128)(2,1)S(1)} %shard_map.80.refs_1_), channel_id=1, source_target_pairs={{0,2},{2,4},{4,6},{6,0},{1,3},{3,5},{5,7},{7,1},{8,10},{10,12},{12... | collective-permute-start | bytes 786440 | tf_op jit(solution)/shard_map/ppermute | solution.py:320
  40.5 9.4 %collective-permute-start = (bf16[2,128,384]{2,1,0:T(8,128)(2,1)S(1)}, bf16[2,128,384]{2,1,0:T(8,128)(2,1)S(1)}, u32[]{:S(2)}, u32[]{:S(2)}) collective-permute-start(bf16[2,128,384]{2,1,0:T(8,128)(2,1)S(1)} %get-tuple-element.51), channel_id=1, source_target_pairs={{0,32},{32,64},{64,96},{96,0},{1,33},{33,65},{65,97},{97,1},{2,34}... | collective-permute-start | bytes 589832 | tf_op jit(solution)/shard_map/ppermute | solution.py:320
  44.0 7.2 %collective-permute-start.1 = (bf16[2,128,384]{2,1,0:T(8,128)(2,1)S(1)}, bf16[2,128,384]{2,1,0:T(8,128)(2,1)S(1)}, u32[]{:S(2)}, u32[]{:S(2)}) collective-permute-start(bf16[2,128,384]{2,1,0:T(8,128)(2,1)S(1)} %get-tuple-element.50), channel_id=1, source_target_pairs={{0,64},{32,96},{64,0},{96,32},{1,65},{33,97},{65,1},{97,33},{2,66}... | collective-permute-start | bytes 589832 | tf_op jit(solution)/shard_map/ppermute | solution.py:320
  45.9 7.1 %collective-permute-start.2 = (bf16[2,128,384]{2,1,0:T(8,128)(2,1)S(1)}, bf16[2,128,384]{2,1,0:T(8,128)(2,1)S(1)}, u32[]{:S(2)}, u32[]{:S(2)}) collective-permute-start(bf16[2,128,384]{2,1,0:T(8,128)(2,1)S(1)} %get-tuple-element.49), channel_id=1, source_target_pairs={{0,96},{32,0},{64,32},{96,64},{1,97},{33,1},{65,33},{97,65},{2,98}... | collective-permute-start | bytes 589832 | tf_op jit(solution)/shard_map/ppermute | solution.py:320
  53.0 1.9 %collective-permute-start.14 = (bf16[4,4,128,128]{3,2,1,0:T(8,128)(2,1)S(1)}, bf16[4,4,128,128]{3,2,1,0:T(8,128)(2,1)S(1)}, u32[]{:S(2)}, u32[]{:S(2)}) collective-permute-start(bf16[4,4,128,128]{3,2,1,0:T(8,128)(2,1)S(1)} %shard_map.85), channel_id=1, source_target_pairs={{0,1},{1,0},{2,3},{3,2},{4,5},{5,4},{6,7},{7,6},{8,9},{9,8},{10,11... | collective-permute-start | bytes 1572872 | tf_op jit(solution)/shard_map/ppermute | solution.py:320
  55.6 6.8 %collective-permute-start.16 = (bf16[4,128,128]{2,1,0:T(8,128)(2,1)S(1)}, bf16[4,128,128]{2,1,0:T(8,128)(2,1)S(1)}, u32[]{:S(2)}, u32[]{:S(2)}) collective-permute-start(bf16[4,128,128]{2,1,0:T(8,128)(2,1)S(1)} %get-tuple-element.39), channel_id=1, source_target_pairs={{0,32},{32,64},{64,96},{96,0},{1,33},{33,65},{65,97},{97,1},{2,34}... | collective-permute-start | bytes 393224 | tf_op jit(solution)/shard_map/ppermute | solution.py:320
  56.3 9.8 %collective-permute-start.17 = (bf16[4,128,128]{2,1,0:T(8,128)(2,1)S(1)}, bf16[4,128,128]{2,1,0:T(8,128)(2,1)S(1)}, u32[]{:S(2)}, u32[]{:S(2)}) collective-permute-start(bf16[4,128,128]{2,1,0:T(8,128)(2,1)S(1)} %get-tuple-element.40), channel_id=1, source_target_pairs={{0,64},{32,96},{64,0},{96,32},{1,65},{33,97},{65,1},{97,33},{2,66}... | collective-permute-start | bytes 393224 | tf_op jit(solution)/shard_map/ppermute | solution.py:320
  59.8 6.3 %collective-permute-start.18 = (bf16[4,128,128]{2,1,0:T(8,128)(2,1)S(1)}, bf16[4,128,128]{2,1,0:T(8,128)(2,1)S(1)}, u32[]{:S(2)}, u32[]{:S(2)}) collective-permute-start(bf16[4,128,128]{2,1,0:T(8,128)(2,1)S(1)} %get-tuple-element.41), channel_id=1, source_target_pairs={{0,96},{32,0},{64,32},{96,64},{1,97},{33,1},{65,33},{97,65},{2,98}... | collective-permute-start | bytes 393224 | tf_op jit(solution)/shard_map/ppermute | solution.py:320
  60.4 17.6 %collective-permute-start.15 = (bf16[4,128,384]{2,1,0:T(8,128)(2,1)S(1)}, bf16[4,128,384]{2,1,0:T(8,128)(2,1)S(1)}, u32[]{:S(2)}, u32[]{:S(2)}) collective-permute-start(bf16[4,128,384]{2,1,0:T(8,128)(2,1)S(1)} %shard_map.87), channel_id=1, source_target_pairs={{0,128},{128,0},{1,129},{129,1},{2,130},{130,2},{3,131},{131,3},{4... | collective-permute-start | bytes 1179656 | tf_op jit(solution)/shard_map/ppermute | solution.py:320
  66.7 5.7 %collective-permute-start.19 = (bf16[2,128,128]{2,1,0:T(8,128)(2,1)S(1)}, bf16[2,128,128]{2,1,0:T(8,128)(2,1)S(1)}, u32[]{:S(2)}, u32[]{:S(2)}) collective-permute-start(bf16[2,128,128]{2,1,0:T(8,128)(2,1)S(1)} %get-tuple-element.43), channel_id=1, source_target_pairs={{0,8},{8,0},{16,24},{24,16},{1,9},{9,1},{17,25},{25,17},{2,10},{10... | collective-permute-start | bytes 196616 | tf_op jit(solution)/shard_map/ppermute | solution.py:398
  72.5 8.0 %collective-permute-start.20 = (f32[128,128]{1,0:T(8,128)S(1)}, f32[128,128]{1,0:T(8,128)S(1)}, u32[]{:S(2)}, u32[]{:S(2)}) collective-permute-start(f32[128,128]{1,0:T(8,128)S(1)} %get-tuple-element.47), channel_id=1, source_target_pairs={{0,24},{8,16},{16,8},{24,0},{1,25},{9,17},{17,9},{25,1},{2,26},{10... | collective-permute-start | bytes 196616 | tf_op jit(solution)/shard_map/ppermute | solution.py:400
